TPU v7x, 32 devices: a whole 2x2x4 slice. The times are simulated.
32 devices in a mesh: row: 8 (over z, y), col: 4 (over x, core).
Axes of the slice: x: 2, y: 2, z: 4, core: 2. Of those that a mesh axis runs over, the one named last changes fastest.
Arguments:
- state: float32 [5, 8, 64, 512], P(None, None, 'row', 'col'), may hold values from -1.6 to 7, as said below
- gamma: float32 [8, 64, 512], P(None, 'row', 'col'), may hold values from 1.2 to 1.67
Outputs:
- advanced: float32 [5, 8, 64, 512], P(None, None, 'row', 'col')
Inputs may be any that keep to these rules, and one draw needn't show every extreme that they name: `state`: density lies in 0.5 to 2, every velocity (momentum / density) in -0.8 to 0.8, and energy minus kinetic energy is 1.25 to 5, so that pressure is positive for every gamma in its range.
All inputs are finite; a program needn't handle non-finite values.
Results may differ from a plain program's by a relative error of at most 0.00002.
Values sent between devices are 32-bit elements; how exact they have to be, the bound alone decides.
No kernel may reach another device: no remote copies, remote signals or barrier semaphores. Data moves between devices by JAX's collectives and lax.ppermute only.
A program may use at most 64 MiB of HBM per device.

v0:
```python
import jax
import jax.numpy as jnp
from jax import lax
from jax.sharding import PartitionSpec as P

step_ratio = 0.08


def minmod(first, second):
    return jnp.maximum(jnp.minimum(first, second), 0.0) + jnp.minimum(
        jnp.maximum(first, second), 0.0
    )


def window(array, start, stop, sweep_axis):
    return lax.slice_in_dim(array, start, stop, axis=sweep_axis)


def fluxes(density, normal_vel, trans_one, trans_two, pressure, gamma_side):
    energy = pressure / (gamma_side - 1.0) + 0.5 * density * (
        normal_vel * normal_vel + trans_one * trans_one + trans_two * trans_two
    )
    conserved = [density, density * normal_vel, density * trans_one, density * trans_two, energy]
    flux = [
        density * normal_vel,
        density * normal_vel * normal_vel + pressure,
        density * normal_vel * trans_one,
        density * normal_vel * trans_two,
        normal_vel * (energy + pressure),
    ]
    speed = jnp.abs(normal_vel) + jnp.sqrt(gamma_side * pressure / density)
    return (conserved, flux, speed)


def sweep_update(padded, gamma_pad, sweep_axis, normal):
    length = gamma_pad.shape[sweep_axis]
    density = padded[0]
    velocity = [padded[1] / density, padded[2] / density, padded[3] / density]
    kinetic = 0.5 * (padded[1] * velocity[0] + padded[2] * velocity[1] + padded[3] * velocity[2])
    pressure = (gamma_pad - 1.0) * (padded[4] - kinetic)
    others = [component for component in range(3) if component != normal]
    primitives = [density, velocity[normal], velocity[others[0]], velocity[others[1]], pressure]
    left_states = []
    right_states = []
    for quantity in primitives:
        lower_zone = window(quantity, 1, length - 2, sweep_axis)
        upper_zone = window(quantity, 2, length - 1, sweep_axis)
        face_value = (
            7.0 * (lower_zone + upper_zone)
            - (
                window(quantity, 0, length - 3, sweep_axis)
                + window(quantity, 3, length, sweep_axis)
            )
        ) / 12.0
        face_value = jnp.minimum(
            jnp.maximum(face_value, jnp.minimum(lower_zone, upper_zone)),
            jnp.maximum(lower_zone, upper_zone),
        )
        centre = window(quantity, 2, length - 2, sweep_axis)
        rise_right = window(face_value, 1, length - 3, sweep_axis) - centre
        rise_left = centre - window(face_value, 0, length - 4, sweep_axis)
        upper_edge = centre + minmod(rise_right, 2.0 * rise_left)
        lower_edge = centre - minmod(rise_left, 2.0 * rise_right)
        left_states.append(window(upper_edge, 0, length - 5, sweep_axis))
        right_states.append(window(lower_edge, 1, length - 4, sweep_axis))
    cons_left, flux_left, speed_left = fluxes(
        *left_states, window(gamma_pad, 2, length - 3, sweep_axis)
    )
    cons_right, flux_right, speed_right = fluxes(
        *right_states, window(gamma_pad, 3, length - 2, sweep_axis)
    )
    speed = jnp.maximum(speed_left, speed_right)
    interface = [
        0.5 * (flux_left[item] + flux_right[item])
        - 0.5 * speed * (cons_right[item] - cons_left[item])
        for item in range(5)
    ]
    field_flux = [interface[0], None, None, None, interface[4]]
    field_flux[1 + normal] = interface[1]
    field_flux[1 + others[0]] = interface[2]
    field_flux[1 + others[1]] = interface[3]
    updated = []
    for field in range(5):
        change = window(field_flux[field], 1, length - 5, sweep_axis) - window(
            field_flux[field], 0, length - 6, sweep_axis
        )
        updated.append(window(padded[field], 3, length - 3, sweep_axis) - step_ratio * change)
    return jnp.stack(updated)


def edge_sweep(conserved, gamma_field, sweep_axis, normal):
    widths = [(0, 0)] * gamma_field.ndim
    widths[sweep_axis] = (3, 3)
    gamma_pad = jnp.pad(gamma_field, widths, mode="edge")
    padded = jnp.pad(conserved, [(0, 0)] + widths, mode="edge")
    return sweep_update(padded, gamma_pad, sweep_axis, normal)


def along_second(block):
    swept = edge_sweep(block[:5], block[5], 1, 1)
    return jnp.concatenate([swept, block[5:6]], axis=0)


def along_third(block):
    swept = edge_sweep(block[:5], block[5], 2, 2)
    return lax.all_to_all(swept, "col", split_axis=3, concat_axis=2, tiled=True)


def body(state, gamma):
    after_first = edge_sweep(state, gamma, 0, 0)
    joined = jnp.concatenate([after_first, gamma[None]], axis=0)
    joined = along_second(lax.all_to_all(joined, "row", split_axis=1, concat_axis=2, tiled=True))
    swept = along_third(lax.all_to_all(joined, "col", split_axis=2, concat_axis=3, tiled=True))
    advanced = lax.all_to_all(swept, "row", split_axis=2, concat_axis=1, tiled=True)
    return advanced


def solution(mesh):
    in_specs = (P(None, None, "row", "col"), P(None, "row", "col"))
    out_specs = P(None, None, "row", "col")
    return jax.shard_map(body, mesh=mesh, in_specs=in_specs, out_specs=out_specs, check_vma=False)
```

profile of v0, /device:TPU:0, one launch (start us, length us, event | category | flops | bytes accessed | tf_op | source)
XLA Modules:
  0.0 60.2 jit_solution(2322459257375057742)
XLA Ops:
  0.0 0.0 copy-start.1
  0.0 0.8 %slice_bitcast_fusion.20 = (f32[5,8,128]{2,1,0:T(8,128)S(1)}, f32[5,8,128]{2,1,0:T(8,128)S(1)}) fusion(f32[5,8,8,128]{3,2,1,0:T(8,128)} %param.2), kind=kLoop, calls=%fused_computation.305 | loop fusion | bytes 81920 | tf_op jit(solution)/shard_map/jit(_pad)/slice | solution.py:95
  0.8 0.9 %pad_maximum_fusion = f32[5,14,8,128]{3,2,1,0:T(8,128)S(1)} fusion(f32[5,3,8,128]{3,2,1,0:T(8,128)S(1)} %reshape.544, f32[5,8,8,128]{3,2,1,0:T(8,128)} %param.2, f32[5,3,8,128]{3,2,1,0:T(8,128)S(1)} %reshape.543), kind=kLoop, calls=%fused_computation | loop fusion | flops 143360 | bytes 573440 | tf_op jit(solution)/shard_map/jit(_pad)/concatenate | solution.py:95
  1.7 0.9 %fusion.25 = f32[1,11,8,128]{3,2,1,0:T(8,128)S(1)} fusion(f32[5,3,8,128]{3,2,1,0:T(8,128)S(1)} %reshape.544, f32[5,8,8,128]{3,2,1,0:T(8,128)} %param.2, f32[5,3,8,128]{3,2,1,0:T(8,128)S(1)} %reshape.543, f32[5,14,8,128]{3,2,1,0:T(8,128)S(1)} %pad_maximum_fusion), kind=kLoop, calls=%fused_computation.41 | loop fusion | flops 123904 | bytes 421888 | tf_op jit(solution)/shard_map/min | solution.py:55
  2.6 0.0 copy-done.1
  2.9 0.0 copy-start
  2.9 0.2 multiply_subtract_fusion.10
  3.0 0.1 multiply_subtract_fusion.11
  3.1 0.1 multiply_subtract_fusion.12
  3.2 0.1 multiply_subtract_fusion.13
  3.3 0.5 copy-done
  3.9 15.0 %all_to_all.54 = f32[6,8,8,128]{3,2,0,1:T(8,128)S(1)} all-to-all(f32[6,8,8,128]{3,2,0,1:T(8,128)S(1)} %constant_dynamic-update-slice_fusion), channel_id=1, replica_groups=mesh['row'=8,'col'=4] {'row'}, dimensions={1} | all-to-all | bytes 393216 | tf_op jit(solution)/shard_map/all_to_all | solution.py:112
  19.4 0.2 multiply_subtract_fusion.5
  19.6 0.1 multiply_subtract_fusion.6
  19.7 0.1 multiply_subtract_fusion.8
  19.8 0.1 multiply_subtract_fusion.7
  20.0 0.2 copy.129
  20.2 7.9 %all_to_all.55 = f32[6,1,64,128]{3,1,0,2:T(1,128)S(1)} all-to-all(f32[6,1,64,128]{3,1,0,2:T(1,128)S(1)} %copy.129), channel_id=1, replica_groups=mesh['row'=8,'col'=4] {'col'}, dimensions={2} | all-to-all | bytes 393216 | tf_op jit(solution)/shard_map/all_to_all | solution.py:113
  28.2 0.3 slice_reduce_fusion.3
  28.5 0.1 copy.131
  28.5 0.4 slice_reduce_fusion.1
  29.0 0.1 reshape.552
  29.0 0.1 reshape.553
  29.1 0.1 pad_maximum_fusion.1
  29.3 0.1 fusion.45
  29.4 0.1 reshape.554
  29.5 0.1 reshape.555
  29.5 0.1 fusion.48
  29.6 0.1 fusion.37
  29.7 0.1 fusion.33
  29.8 0.1 fusion.29
  30.0 0.1 fusion.41
  30.1 0.1 slice_subtract_fusion.12
  30.2 0.1 slice_subtract_fusion.2
  30.3 0.1 slice_subtract_fusion.5
  30.3 0.1 slice_subtract_fusion.8
  30.4 0.1 slice_subtract_fusion.14
  30.5 0.3 multiply_subtract_fusion
  30.8 0.1 multiply_subtract_fusion.1
  31.0 0.1 constant_dynamic-update-slice_fusion.16
  31.1 0.1 constant_dynamic-update-slice_fusion.15
  31.1 0.1 constant_dynamic-update-slice_fusion.14
  31.2 0.1 constant_dynamic-update-slice_fusion.13
  31.3 0.1 constant_dynamic-update-slice_fusion.12
  31.4 0.8 %copy.137 = f32[5,1,16,512]{2,1,0,3:T(1,128)S(1)} copy(f32[5,1,16,512]{3,2,1,0:T(8,128)S(1)} %constant_dynamic-update-slice_fusion.12) | data formatting | bytes 327680 | tf_op jit(solution)/shard_map/stack | solution.py:88
  32.3 0.5 broadcast.617
  32.8 4.0 %reduce.8 = f32[512,5,16]{2,1,0:T(8,128)S(1)} reduce(f32[512,5,1,16]{3,2,1,0:T(1,128)S(1)} %bitcast.244, f32[]{:T(128)} %broadcast.617), dimensions={2}, to_apply=%bitcast.221.reduce_sub_computation | reduce | bytes 327684
  36.8 0.6 %reshape.564 = f32[4,1,10240]{2,1,0:T(1,128)S(1)} reshape(f32[512,5,16]{2,1,0:T(8,128)S(1)} %reduce.8) | data formatting | bytes 327680
  37.4 7.3 %all_to_all.56 = f32[4,1,10240]{2,1,0:T(1,128)S(1)} all-to-all(f32[4,1,10240]{2,1,0:T(1,128)S(1)} %reshape.564), channel_id=1, replica_groups=mesh['row'=8,'col'=4] {'col'}, dimensions={0} | all-to-all | bytes 327680 | tf_op jit(solution)/shard_map/all_to_all | solution.py:106
  44.7 1.1 %reduce.9 = f32[4,10240]{1,0:T(4,128)S(1)} reduce(f32[4,1,10240]{2,1,0:T(1,128)S(1)} %all_to_all.56, f32[]{:T(128)} %broadcast.617), dimensions={1}, to_apply=%all_to_all.44.reduce_sub_computation | reduce | bytes 327684 | tf_op jit(solution)/shard_map/all_to_all | solution.py:106
  45.8 2.2 %reshape.565 = f32[512,5,1,16]{3,2,1,0:T(1,128)S(1)} reshape(f32[4,10240]{1,0:T(4,128)S(1)} %reduce.9) | data formatting | bytes 327680
  48.0 0.7 %copy.138 = f32[5,1,16,512]{3,1,2,0:T(1,128)S(1)} copy(f32[5,1,16,512]{2,1,0,3:T(1,128)S(1)} %bitcast.245) | data formatting | bytes 327680 | tf_op jit(solution)/shard_map/all_to_all | solution.py:106
  48.8 0.2 copy.140
  49.0 10.5 %all_to_all.57 = f32[5,1,64,128]{3,1,0,2:T(1,128)S(1)} all-to-all(f32[5,1,64,128]{3,1,0,2:T(1,128)S(1)} %copy.140), channel_id=1, replica_groups=mesh['row'=8,'col'=4] {'row'}, dimensions={2} | all-to-all | bytes 327680 | tf_op jit(solution)/shard_map/all_to_all | solution.py:114
  59.5 0.7 %copy.149 = f32[5,1,64,128]{3,2,0,1:T(8,128)} copy(f32[5,1,64,128]{3,1,0,2:T(1,128)S(1)} %all_to_all.57) | data formatting | bytes 327680 | tf_op jit(solution)/shard_map/all_to_all | solution.py:114
  (58 shorter events, 0.7 us)
Async XLA Ops:
  0.0 2.6 %copy-start.1 = (f32[8,8,128]{2,1,0:T(8,128)S(1)}, f32[8,8,128]{2,1,0:T(8,128)}, u32[]{:S(2)}) copy-start(f32[8,8,128]{2,1,0:T(8,128)} %param.3) | copy-start | bytes 98308
  2.9 0.9 %copy-start = (f32[5,8,8,128]{3,2,1,0:T(8,128)S(1)}, f32[5,8,8,128]{3,2,1,0:T(8,128)}, u32[]{:S(2)}) copy-start(f32[5,8,8,128]{3,2,1,0:T(8,128)} %param.2) | copy-start | bytes 491524
where the time goes:
time: 60.6 us; the launch traced here: 60.2 us
  blocking collectives  40.8 us (67%)
  other arithmetic  10.3 us (17%)
  local copies, waits for them, and re-layouts  8.5 us (14%)
  between operations  0.62 us (1%)
    all_to_all x1, blocking collectives, body(): lax.all_to_all(joined, 'row', split_axis=1, concat_axis=2, tiled=True)  15 us
    all_to_all x1, blocking collectives, body(): lax.all_to_all(swept, 'row', split_axis=2, concat_axis=1, tiled=True)  10.5 us
    all_to_all x1, blocking collectives, body(): lax.all_to_all(joined, 'col', split_axis=2, concat_axis=3, tiled=True)  7.9 us
    all_to_all x1, blocking collectives, along_third(): return lax.all_to_all(swept, 'col', split_axis=3, concat_axis=2, tiled=True)  7.34 us
    unnamed x15, other arithmetic  4.41 us
    unnamed x9, local copies, waits for them, and re-layouts  3.88 us
    min x13, other arithmetic, sweep_update(): jnp.minimum(jnp.maximum(face_value, jnp.minimum(lower_zone, upper_zone)),...  1.56 us
    sub x10, other arithmetic, sweep_update(): 0.5 * (flux_left[item] + flux_right[item])  1.29 us

commit v1 on v0

v1 whole, which is shorter than its diff:
```python
import functools

import jax
import jax.numpy as jnp
from jax import lax
from jax.experimental import pallas as pl
from jax.experimental.pallas import tpu as pltpu
from jax.sharding import PartitionSpec as P

STEP = 0.08
HALO = 3
SUB, LANES = 8, 128
GROUP = LANES // SUB


def recip(x):
    r = pl.reciprocal(x, approx=True)
    return r * (2.0 - x * r)


def clamp_zero(u, v):
    return jnp.maximum(jnp.minimum(u, jnp.maximum(v, 0.0)), jnp.minimum(v, 0.0))


def primitives(cons, gam1, normal):
    rho, m0, m1, m2, energy = cons
    inv = recip(rho)
    vel = [m0 * inv, m1 * inv, m2 * inv]
    kinetic = 0.5 * (m0 * vel[0] + m1 * vel[1] + m2 * vel[2])
    pressure = gam1 * (energy - kinetic)
    others = [c for c in range(3) if c != normal]
    return [rho, vel[normal], vel[others[0]], vel[others[1]], pressure]


def face_rise(before, here, after):
    if here is None:
        return None
    rise = 0.5 * here
    if before is not None and after is not None:
        rise = rise + (before - after) * (1.0 / 12.0)
    elif before is not None:
        rise = rise + before * (1.0 / 12.0)
    elif after is not None:
        rise = rise - after * (1.0 / 12.0)
    return clamp_zero(rise, here)


def edges(q, right, left):
    if right is None or left is None:
        return q, q
    return q + clamp_zero(right, 2.0 * left), q - clamp_zero(left, 2.0 * right)


def state_flux(prim, gamma, inv_gam1):
    rho, un, u1, u2, p = prim
    mn, m1, m2 = rho * un, rho * u1, rho * u2
    nn = mn * un
    energy = p * inv_gam1 + 0.5 * (nn + m1 * u1 + m2 * u2)
    flux = [mn, nn + p, mn * u1, mn * u2, un * (energy + p)]
    gp = gamma * p
    speed = jnp.abs(un) + gp * lax.rsqrt(jnp.maximum(gp * rho, 1e-30))
    return [rho, mn, m1, m2, energy], flux, speed


def double_flux(left, right):
    if left is right:
        return [f + f for f in left[1]]
    speed = jnp.maximum(left[2], right[2])
    return [
        (left[1][k] + right[1][k]) - speed * (right[0][k] - left[0][k]) for k in range(5)
    ]


def place(normal):
    others = [c for c in range(3) if c != normal]
    return [0, 1 + normal, 1 + others[0], 1 + others[1], 4]


def updated(cons, flux_right, flux_left, normal):
    out = list(cons)
    for k, field in enumerate(place(normal)):
        out[field] = cons[field] - (0.5 * STEP) * (flux_right[k] - flux_left[k])
    return out


def sweep_rows(load, load_gamma, store, n, normal, outflow):
    cons, gam, prim, diff, rise, edge = {}, {}, {}, {}, {}, {}

    def zone(i):
        return min(max(i, 0), n - 1) if outflow else i

    def get(i):
        i = zone(i)
        if i not in cons:
            cons[i] = load(i)
            g = load_gamma(i)
            gam1 = g - 1.0
            gam[i] = (g, recip(gam1))
            prim[i] = primitives(cons[i], gam1, normal)
        return prim[i]

    def get_diff(i):
        if i not in diff:
            a, b = get(i), get(i + 1)
            diff[i] = [None] * 5 if a is b else [y - x for x, y in zip(a, b)]
        return diff[i]

    def get_rise(i):
        if i not in rise:
            before, here, after = get_diff(i - 1), get_diff(i), get_diff(i + 1)
            right = [face_rise(*t) for t in zip(before, here, after)]
            left = [None if r is None else h - r for h, r in zip(here, right)]
            rise[i] = (right, left)
        return rise[i]

    def get_edge(i):
        if i not in edge:
            q, right, left = get(i), get_rise(i)[0], get_rise(i - 1)[1]
            pairs = [edges(*t) for t in zip(q, right, left)]
            upper = [p[0] for p in pairs]
            lower = [p[1] for p in pairs]
            if all(u is w for u, w in zip(upper, lower)):
                one = state_flux(upper, *gam[zone(i)])
                edge[i] = (one, one, zone(i))
            else:
                edge[i] = [upper, lower, zone(i)]
        return edge[i]

    def side(i, which):
        e = get_edge(i)
        if isinstance(e, tuple):
            return e[which]
        return state_flux(e[which], *gam[e[2]])

    def face(i):
        if outflow and i < 0:
            whole = get_edge(0)
            return double_flux(whole[0], whole[0])
        if outflow and i == n - 1:
            whole = get_edge(n - 1)
            return double_flux(whole[1], whole[1])
        return double_flux(side(i, 0), side(i + 1, 1))

    previous = face(-1)
    for i in range(n):
        current = face(i)
        store(i, updated(cons[i], current, previous, normal))
        previous = current


def first_kernel(row_axis, state_ref, gamma_ref, swept_ref, one_ref, two_ref):
    nx, ny = gamma_ref.shape[0], gamma_ref.shape[1]

    def store(x, cons):
        for f in range(5):
            swept_ref[f, pl.ds(x, ny, stride=nx), :] = cons[f]

    sweep_rows(
        lambda x: [state_ref[f, x] for f in range(5)],
        lambda x: gamma_ref[x],
        store,
        nx,
        0,
        True,
    )
    for x in range(nx):
        swept_ref[5, pl.ds(x, ny, stride=nx), :] = gamma_ref[x]
    odd = lax.rem(lax.axis_index(row_axis), 2)
    low, high = 0, (ny - HALO) * nx
    start_one = pl.multiple_of(jnp.where(odd == 1, low, high), SUB)
    start_two = pl.multiple_of(jnp.where(odd == 1, high, low), SUB)
    for f in range(6):
        one_ref[f] = swept_ref[f, pl.ds(start_one, HALO * nx), :]
        two_ref[f] = swept_ref[f, pl.ds(start_two, HALO * nx), :]


def second_kernel(row_axis, rows, swept_ref, one_ref, two_ref, next_ref, window_ref):
    nx = swept_ref.shape[1] // SUB
    ny = SUB
    row = lax.axis_index(row_axis)
    odd = lax.rem(row, 2) == 1
    first, last = row == 0, row == rows - 1
    lane = lax.broadcasted_iota(jnp.int32, (SUB, LANES), 1)
    group = lane // GROUP
    for tile in range(nx // SUB):
        base = tile * SUB

        def load_field(f, y):
            if 0 <= y < ny:
                return swept_ref[f, pl.ds(y * nx + base, SUB), :]
            at = pl.ds((y + HALO if y < 0 else y - ny) * nx + base, SUB)
            one, two = one_ref[f, at, :], two_ref[f, at, :]
            if y < 0:
                got = jnp.where(odd, one, two)
                return jnp.where(first, swept_ref[f, pl.ds(base, SUB), :], got)
            got = jnp.where(odd, two, one)
            return jnp.where(last, swept_ref[f, pl.ds((ny - 1) * nx + base, SUB), :], got)

        windows = [None] * 6

        def into_window(f, y, value):
            turn = (GROUP * y + 6) % LANES
            rolled = pltpu.roll(value, turn, 1) if turn else value
            windows[f] = rolled if windows[f] is None else jnp.where(group == y, rolled, windows[f])

        def store(y, cons):
            for f in range(5):
                next_ref[f, pl.ds(y * nx + base, SUB), :] = cons[f]
                into_window(f, y, cons[f])

        sweep_rows(
            lambda y: [load_field(f, y) for f in range(5)],
            lambda y: load_field(5, y),
            store,
            ny,
            1,
            False,
        )
        for y in range(ny):
            into_window(5, y, swept_ref[5, pl.ds(y * nx + base, SUB), :])
        for f in range(6):
            window_ref[f, pl.ds(base, SUB), :] = windows[f]


def sweep_lanes(cons, gamma, normal):
    def ahead(x):
        return pltpu.roll(x, LANES - 1, 1)

    def behind(x):
        return pltpu.roll(x, 1, 1)

    gam1 = gamma - 1.0
    inv_gam1 = recip(gam1)
    prim = primitives(cons, gam1, normal)
    upper, lower_next = [], []
    for q in prim:
        here = ahead(q) - q
        right = face_rise(behind(here), here, ahead(here))
        left = behind(here - right)
        up, low = edges(q, right, left)
        upper.append(up)
        lower_next.append(ahead(low))
    flux = double_flux(
        state_flux(upper, gamma, inv_gam1),
        state_flux(lower_next, ahead(gamma), ahead(inv_gam1)),
    )
    return updated(cons, flux, [behind(x) for x in flux], normal)


def third_kernel(col_axis, cols, swept_ref, gamma_ref, window_ref, one_ref, two_ref, out_ref):
    nx = window_ref.shape[1]
    ny = SUB
    col = lax.axis_index(col_axis)
    odd = lax.rem(col, 2) == 1
    first, last = col == 0, col == cols - 1
    lane = lax.broadcasted_iota(jnp.int32, (SUB, LANES), 1)
    slot = lane % GROUP
    for tile in range(nx // SUB):
        base = tile * SUB
        rows = pl.ds(base, SUB)
        left_window, right_window = [], []
        for f in range(6):
            own, one, two = window_ref[f, rows, :], one_ref[f, rows, :], two_ref[f, rows, :]
            before = jnp.where(odd, one, two)
            after = jnp.where(odd, two, one)
            low = jnp.where(
                slot == 3,
                pltpu.roll(own, LANES - 3, 1),
                jnp.where(slot == 4, pltpu.roll(own, LANES - 2, 1), pltpu.roll(own, LANES - 1, 1)),
            )
            high = jnp.where(
                slot == 6,
                pltpu.roll(own, 1, 1),
                jnp.where(slot == 7, pltpu.roll(own, 2, 1), pltpu.roll(own, 3, 1)),
            )
            before = jnp.where(first, low, before)
            after = jnp.where(last, high, after)
            left_window.append(jnp.where((slot >= 3) & (slot <= 5), before, own))
            right_window.append(jnp.where((slot >= 6) & (slot <= 8), after, own))
        left_new = sweep_lanes(left_window[:5], left_window[5], 2)
        right_new = sweep_lanes(right_window[:5], right_window[5], 2)
        edge_new = [jnp.where(slot >= 6, a, b) for a, b in zip(left_new, right_new)]
        at_edge = (lane < HALO) | (lane >= LANES - HALO)
        for y in range(ny):
            at = pl.ds(y * nx + base, SUB)
            cons = [swept_ref[f, at, :] for f in range(5)]
            inner = sweep_lanes(cons, gamma_ref[5, at, :], 2)
            turn = (LANES - 6 - GROUP * y) % LANES
            for f in range(5):
                edge = pltpu.roll(edge_new[f], turn, 1)
                out_ref[f, pl.ds(base * ny + y, SUB, stride=ny), :] = jnp.where(
                    at_edge, edge, inner[f]
                )


def swap_pairs(mesh, axis, inner):
    rows, cols = mesh.shape["row"], mesh.shape["col"]
    pairs = []
    for r in range(rows):
        for c in range(cols):
            k, n = (r, rows) if axis == "row" else (c, cols)
            if not inner:
                k ^= 1
            elif 0 < k < n - 1:
                k = ((k - 1) ^ 1) + 1
            else:
                k = None
            if axis == "row":
                to = (r, c ^ 1) if k is None else (k, c)
            else:
                to = (r ^ 1, c) if k is None else (r, k)
            pairs.append((r * cols + c, to[0] * cols + to[1]))
    return pairs


def body(mesh, state, gamma):
    rows, cols = mesh.shape["row"], mesh.shape["col"]
    _, nx, ny, nz = state.shape
    assert ny == SUB and nz == LANES and nx % SUB == 0 and rows % 2 == 0 and cols % 2 == 0
    shape = lambda *dims: jax.ShapeDtypeStruct(dims, jnp.float32)
    swap = lambda x, axis, inner: lax.ppermute(x, ("row", "col"), swap_pairs(mesh, axis, inner))

    swept, one, two = pl.pallas_call(
        functools.partial(first_kernel, "row"),
        out_shape=(
            shape(6, ny * nx, nz),
            shape(6, HALO * nx, nz),
            shape(6, HALO * nx, nz),
        ),
        name="sweep_first",
    )(state, gamma)
    one, two = swap(one, "row", False), swap(two, "row", True)
    after, window = pl.pallas_call(
        functools.partial(second_kernel, "row", rows),
        out_shape=(shape(5, ny * nx, nz), shape(6, nx, nz)),
        name="sweep_second",
    )(swept, one, two)
    one, two = swap(window, "col", False), swap(window, "col", True)
    out = pl.pallas_call(
        functools.partial(third_kernel, "col", cols),
        out_shape=shape(5, nx * ny, nz),
        name="sweep_third",
    )(after, swept, window, one, two)
    return out.reshape(5, nx, ny, nz)


def solution(mesh):
    in_specs = (P(None, None, "row", "col"), P(None, "row", "col"))
    out_specs = P(None, None, "row", "col")
    return jax.shard_map(
        functools.partial(body, mesh),
        mesh=mesh,
        in_specs=in_specs,
        out_specs=out_specs,
        check_vma=False,
    )
```

time: 60.6 us -> 19.2 us (0.32)
  blocking collectives: 40.8 us -> 0 us
  other arithmetic: 10.3 us -> 0 us
  local copies, waits for them, and re-layouts: 8.5 us -> 1.27 us
  Pallas kernels: 0 us -> 6.77 us
  waiting for transfers between devices: 0 us -> 5.69 us
  starting transfers between devices: 0 us -> 5.32 us
  between operations: 0.62 us -> 0.01 us
    all_to_all x4 -> x0, blocking collectives: 40.8 us -> none  [the longest x1 15 us: body(): lax.all_to_all(joined, 'row', split_axis=1, concat_axis=2, tiled=True)]
    pallas_call x0 -> x3, Pallas kernels: none -> 6.77 us  [the longest x1 2.89 us: body(): pl.pallas_call(functools.partial(third_kernel, 'col', cols), out_shape=sh...]
    ppermute x0 -> x4, waiting for transfers between devices: none -> 5.69 us  [body(): lax.ppermute(x, ('row', 'col'), swap_pairs(mesh, axis, inner))]
    ppermute x0 -> x4, starting transfers between devices: none -> 5.32 us  [body(): lax.ppermute(x, ('row', 'col'), swap_pairs(mesh, axis, inner))]
    unnamed x15 -> x0, other arithmetic: 4.41 us -> none
    unnamed x9 -> x8, local copies, waits for them, and re-layouts: 3.88 us -> 1.27 us
    sub x25 -> x0, other arithmetic: 1.85 us -> none  [the longest x10 1.29 us: sweep_update(): 0.5 * (flux_left[item] + flux_right[item])]
    slice x12 -> x0, local copies, waits for them, and re-layouts: 1.61 us -> none  [the longest x3 1.16 us: edge_sweep(): padded = jnp.pad(conserved, [(0, 0)] + widths, mode='edge')]
  transfers between devices with their start and end apart: 0 -> 4, of which waited for: 0 -> 2; matrix products, arithmetic and copies ran while one was open for 0% -> 0% of each run, Pallas kernels for 0% -> 0%
where the time goes in v1:
time: 19.2 us; the launch traced here: 19.1 us
  Pallas kernels  6.77 us (35%)
  waiting for transfers between devices  5.69 us (30%)
  starting transfers between devices  5.32 us (28%)
  local copies, waits for them, and re-layouts  1.27 us (7%)
    ppermute x4, waiting for transfers between devices, body(): lax.ppermute(x, ('row', 'col'), swap_pairs(mesh, axis, inner))  5.69 us
    ppermute x4, starting transfers between devices, body(): lax.ppermute(x, ('row', 'col'), swap_pairs(mesh, axis, inner))  5.32 us
    pallas_call x1, Pallas kernels, body(): pl.pallas_call(functools.partial(third_kernel, 'col', cols), out_shape=sh...  2.89 us
    pallas_call x1, Pallas kernels, body(): pl.pallas_call(functools.partial(second_kernel, 'row', rows), out_shape=(...  2 us
    pallas_call x1, Pallas kernels, body(): pl.pallas_call(functools.partial(first_kernel, 'row'), out_shape=(shape(6...  1.87 us
    unnamed x8, local copies, waits for them, and re-layouts  1.27 us
  transfers between devices with their start and end apart: 4, of which 2 were waited for; matrix products, arithmetic and copies ran while one was open for 0% of the time, Pallas kernels for 0%

profile of v1, /device:TPU:0, one launch (start us, length us, event | category | flops | bytes accessed | tf_op | source)
XLA Modules:
  0.0 19.1 jit_solution(12440505541525698782)
XLA Ops:
  0.0 1.9 %sweep_first.1 = (f32[6,64,128]{2,1,0:T(8,128)}, f32[6,24,128]{2,1,0:T(8,128)}, f32[6,24,128]{2,1,0:T(8,128)}) custom-call(f32[5,8,8,128]{3,2,1,0:T(8,128)} %state_ref.1, f32[8,8,128]{2,1,0:T(8,128)} %gamma_ref.1), custom_call_target="tpu_custom_call" | custom-call | tf_op jit(solution)/shard_map/sweep_first/pallas_call | solution.py:323
  1.9 3.0 %collective-permute-start = (f32[6,24,128]{2,1,0:T(8,128)}, f32[6,24,128]{2,1,0:T(8,128)S(1)}, u32[]{:S(2)}, u32[]{:S(2)}) collective-permute-start(f32[6,24,128]{2,1,0:T(8,128)} %get-tuple-element.11), channel_id=1, source_target_pairs={{0,4},{1,5},{2,6},{3,7},{4,0},{5,1},{6,2},{7,3},{8,12},{9,13},{10,... | collective-permute-start | bytes 221192 | tf_op jit(solution)/shard_map/ppermute | solution.py:321
  4.8 0.0 collective-permute-start.1
  4.8 3.7 %collective-permute-done.one_ref = f32[6,24,128]{2,1,0:T(8,128)S(1)} collective-permute-done((f32[6,24,128]{2,1,0:T(8,128)}, f32[6,24,128]{2,1,0:T(8,128)S(1)}, u32[]{:S(2)}, u32[]{:S(2)}) %collective-permute-start) | collective-permute-done | bytes 73760 | tf_op jit(solution)/shard_map/ppermute | solution.py:321
  8.5 0.0 copy-start
  8.5 0.0 collective-permute-done.1.two_ref
  8.5 0.0 copy-start.1
  8.5 0.6 %copy-done = f32[6,24,128]{2,1,0:T(8,128)} copy-done((f32[6,24,128]{2,1,0:T(8,128)}, f32[6,24,128]{2,1,0:T(8,128)S(1)}, u32[]{:S(2)}) %copy-start) | copy-done | bytes 73752
  9.2 0.0 copy-done.1
  9.2 2.0 %sweep_second.1 = (f32[5,64,128]{2,1,0:T(8,128)}, f32[6,8,128]{2,1,0:T(8,128)}) custom-call(f32[6,64,128]{2,1,0:T(8,128)} %get-tuple-element.10.swept_ref.gamma_ref, f32[6,24,128]{2,1,0:T(8,128)} %copy-done, f32[6,24,128]{2,1,0:T(8,128)} %copy-done.1), custom_call_target="tpu_custom_call" | custom-call | tf_op jit(solution)/shard_map/sweep_second/pallas_call | solution.py:333
  11.2 2.3 %collective-permute-start.3 = (f32[6,8,128]{2,1,0:T(8,128)}, f32[6,8,128]{2,1,0:T(8,128)S(1)}, u32[]{:S(2)}, u32[]{:S(2)}) collective-permute-start(f32[6,8,128]{2,1,0:T(8,128)} %get-tuple-element.14.window_ref), channel_id=1, source_target_pairs={{0,4},{1,2},{2,1},{3,7},{4,0},{5,6},{6,5},{7,3},{8,12},{9,10},{10,... | collective-permute-start | bytes 73736 | tf_op jit(solution)/shard_map/ppermute | solution.py:321
  13.5 0.0 collective-permute-start.2
  13.5 2.0 %collective-permute-done.3.two_ref = f32[6,8,128]{2,1,0:T(8,128)S(1)} collective-permute-done((f32[6,8,128]{2,1,0:T(8,128)}, f32[6,8,128]{2,1,0:T(8,128)S(1)}, u32[]{:S(2)}, u32[]{:S(2)}) %collective-permute-start.3) | collective-permute-done | bytes 24608 | tf_op jit(solution)/shard_map/ppermute | solution.py:321
  15.5 0.0 copy-start.2
  15.5 0.0 collective-permute-done.2.one_ref
  15.6 0.0 copy-start.3
  15.6 0.6 %copy-done.2 = f32[6,8,128]{2,1,0:T(8,128)} copy-done((f32[6,8,128]{2,1,0:T(8,128)}, f32[6,8,128]{2,1,0:T(8,128)S(1)}, u32[]{:S(2)}) %copy-start.2) | copy-done | bytes 24600
  16.2 0.0 copy-done.3
  16.2 2.9 %sweep_third.1 = f32[5,64,128]{2,1,0:T(8,128)} custom-call(f32[5,64,128]{2,1,0:T(8,128)} %get-tuple-element.13.swept_ref, f32[6,64,128]{2,1,0:T(8,128)} %get-tuple-element.10.swept_ref.gamma_ref, f32[6,8,128]{2,1,0:T(8,128)} %get-tuple-element.14.window_ref, f32[6,8,128]{2,1,0:T(8,128)} %copy-done.3, f32[6,8,128]{2,1,0:T(8,128)} %copy-done.2), custom_call_target="tpu_custom_call" | custom-call | tf_op jit(solution)/shard_map/sweep_third/pallas_call | solution.py:339
Async XLA Ops:
  1.9 6.6 %collective-permute-start = (f32[6,24,128]{2,1,0:T(8,128)}, f32[6,24,128]{2,1,0:T(8,128)S(1)}, u32[]{:S(2)}, u32[]{:S(2)}) collective-permute-start(f32[6,24,128]{2,1,0:T(8,128)} %get-tuple-element.11), channel_id=1, source_target_pairs={{0,4},{1,5},{2,6},{3,7},{4,0},{5,1},{6,2},{7,3},{8,12},{9,13},{10,... | collective-permute-start | bytes 221192 | tf_op jit(solution)/shard_map/ppermute | solution.py:321
  4.8 3.7 %collective-permute-start.1 = (f32[6,24,128]{2,1,0:T(8,128)}, f32[6,24,128]{2,1,0:T(8,128)S(1)}, u32[]{:S(2)}, u32[]{:S(2)}) collective-permute-start(f32[6,24,128]{2,1,0:T(8,128)} %get-tuple-element.12), channel_id=1, source_target_pairs={{0,1},{1,0},{2,3},{3,2},{4,8},{5,9},{6,10},{7,11},{8,4},{9,5},{10,... | collective-permute-start | bytes 221192 | tf_op jit(solution)/shard_map/ppermute | solution.py:321
  8.5 0.6 %copy-start = (f32[6,24,128]{2,1,0:T(8,128)}, f32[6,24,128]{2,1,0:T(8,128)S(1)}, u32[]{:S(2)}) copy-start(f32[6,24,128]{2,1,0:T(8,128)S(1)} %collective-permute-done.one_ref) | copy-start | bytes 221188
  8.5 0.7 %copy-start.1 = (f32[6,24,128]{2,1,0:T(8,128)}, f32[6,24,128]{2,1,0:T(8,128)S(1)}, u32[]{:S(2)}) copy-start(f32[6,24,128]{2,1,0:T(8,128)S(1)} %collective-permute-done.1.two_ref) | copy-start | bytes 221188
  11.2 4.4 %collective-permute-start.3 = (f32[6,8,128]{2,1,0:T(8,128)}, f32[6,8,128]{2,1,0:T(8,128)S(1)}, u32[]{:S(2)}, u32[]{:S(2)}) collective-permute-start(f32[6,8,128]{2,1,0:T(8,128)} %get-tuple-element.14.window_ref), channel_id=1, source_target_pairs={{0,4},{1,2},{2,1},{3,7},{4,0},{5,6},{6,5},{7,3},{8,12},{9,10},{10,... | collective-permute-start | bytes 73736 | tf_op jit(solution)/shard_map/ppermute | solution.py:321
  13.5 2.0 %collective-permute-start.2 = (f32[6,8,128]{2,1,0:T(8,128)}, f32[6,8,128]{2,1,0:T(8,128)S(1)}, u32[]{:S(2)}, u32[]{:S(2)}) collective-permute-start(f32[6,8,128]{2,1,0:T(8,128)} %get-tuple-element.14.window_ref), channel_id=1, source_target_pairs={{0,1},{1,0},{2,3},{3,2},{4,5},{5,4},{6,7},{7,6},{8,9},{9,8},{10,11... | collective-permute-start | bytes 73736 | tf_op jit(solution)/shard_map/ppermute | solution.py:321
  15.5 0.6 %copy-start.2 = (f32[6,8,128]{2,1,0:T(8,128)}, f32[6,8,128]{2,1,0:T(8,128)S(1)}, u32[]{:S(2)}) copy-start(f32[6,8,128]{2,1,0:T(8,128)S(1)} %collective-permute-done.3.two_ref) | copy-start | bytes 73732
  15.6 0.6 %copy-start.3 = (f32[6,8,128]{2,1,0:T(8,128)}, f32[6,8,128]{2,1,0:T(8,128)S(1)}, u32[]{:S(2)}) copy-start(f32[6,8,128]{2,1,0:T(8,128)S(1)} %collective-permute-done.2.one_ref) | copy-start | bytes 73732

commit v2 on v1

--- a/solution.py
+++ b/solution.py
@@ -317,30 +317,36 @@
     rows, cols = mesh.shape["row"], mesh.shape["col"]
     _, nx, ny, nz = state.shape
     assert ny == SUB and nz == LANES and nx % SUB == 0 and rows % 2 == 0 and cols % 2 == 0
-    shape = lambda *dims: jax.ShapeDtypeStruct(dims, jnp.float32)
+    here = lambda *dims: pltpu.VMEM(dims, jnp.float32)
+    keep = lambda x: pltpu.with_memory_space_constraint(x, pltpu.VMEM)
+    near = pl.BlockSpec(memory_space=pltpu.VMEM)
     swap = lambda x, axis, inner: lax.ppermute(x, ("row", "col"), swap_pairs(mesh, axis, inner))
 
     swept, one, two = pl.pallas_call(
         functools.partial(first_kernel, "row"),
         out_shape=(
-            shape(6, ny * nx, nz),
-            shape(6, HALO * nx, nz),
-            shape(6, HALO * nx, nz),
+            here(6, ny * nx, nz),
+            here(6, HALO * nx, nz),
+            here(6, HALO * nx, nz),
         ),
+        out_specs=(near,) * 3,
         name="sweep_first",
     )(state, gamma)
     one, two = swap(one, "row", False), swap(two, "row", True)
     after, window = pl.pallas_call(
         functools.partial(second_kernel, "row", rows),
-        out_shape=(shape(5, ny * nx, nz), shape(6, nx, nz)),
+        out_shape=(here(5, ny * nx, nz), here(6, nx, nz)),
+        in_specs=[near] * 3,
+        out_specs=(near,) * 2,
         name="sweep_second",
-    )(swept, one, two)
+    )(keep(swept), keep(one), keep(two))
     one, two = swap(window, "col", False), swap(window, "col", True)
     out = pl.pallas_call(
         functools.partial(third_kernel, "col", cols),
-        out_shape=shape(5, nx * ny, nz),
+        out_shape=jax.ShapeDtypeStruct((5, nx * ny, nz), jnp.float32),
+        in_specs=[near] * 5,
         name="sweep_third",
-    )(after, swept, window, one, two)
+    )(keep(after), keep(swept), keep(window), keep(one), keep(two))
     return out.reshape(5, nx, ny, nz)
 
 

time: 19.2 us -> 14.3 us (0.74)
  Pallas kernels: 6.77 us -> 3.41 us
  local copies, waits for them, and re-layouts: 1.27 us -> 0 us
  waiting for transfers between devices: 5.69 us -> 5.17 us
  starting transfers between devices: 5.32 us -> 5.53 us
    pallas_call x2, Pallas kernels: 4.76 us -> 3.02 us  [the longest x1 1.87 us: body(): pl.pallas_call(functools.partial(third_kernel, 'col', cols), out_shape=ja...]
    pallas_call x1, Pallas kernels: 2 us -> 0.39 us  [body(): pl.pallas_call(functools.partial(second_kernel, 'row', rows), out_shape=(...]
    unnamed x8 -> x0, local copies, waits for them, and re-layouts: 1.27 us -> none
    ppermute x4, waiting for transfers between devices: 5.69 us -> 5.17 us  [body(): lax.ppermute(x, ('row', 'col'), swap_pairs(mesh, axis, inner))]
    ppermute x4, starting transfers between devices: 5.32 us -> 5.53 us  [body(): lax.ppermute(x, ('row', 'col'), swap_pairs(mesh, axis, inner))]
where the time goes in v2:
time: 14.3 us; the launch traced here: 14.1 us
  starting transfers between devices  5.53 us (39%)
  waiting for transfers between devices  5.17 us (36%)
  Pallas kernels  3.41 us (24%)
    ppermute x4, starting transfers between devices, body(): lax.ppermute(x, ('row', 'col'), swap_pairs(mesh, axis, inner))  5.53 us
    ppermute x4, waiting for transfers between devices, body(): lax.ppermute(x, ('row', 'col'), swap_pairs(mesh, axis, inner))  5.17 us
    pallas_call x1, Pallas kernels, body(): pl.pallas_call(functools.partial(third_kernel, 'col', cols), out_shape=ja...  1.87 us
    pallas_call x1, Pallas kernels, body(): pl.pallas_call(functools.partial(first_kernel, 'row'), out_shape=(here(6,...  1.15 us
    pallas_call x1, Pallas kernels, body(): pl.pallas_call(functools.partial(second_kernel, 'row', rows), out_shape=(...  0.39 us
  transfers between devices with their start and end apart: 4, of which 2 were waited for; matrix products, arithmetic and copies ran while one was open for 0% of the time, Pallas kernels for 0%

profile of v2, /device:TPU:0, one launch (start us, length us, event | category | flops | bytes accessed | tf_op | source)
XLA Modules:
  0.0 14.1 jit_solution(17477926433181315937)
XLA Ops:
  0.0 1.1 %sweep_first.1 = (f32[6,64,128]{2,1,0:T(8,128)S(1)}, f32[6,24,128]{2,1,0:T(8,128)S(1)}, f32[6,24,128]{2,1,0:T(8,128)S(1)}) custom-call(f32[5,8,8,128]{3,2,1,0:T(8,128)} %state_ref.1, f32[8,8,128]{2,1,0:T(8,128)} %gamma_ref.1), custom_call_target="tpu_custom_call" | custom-call | tf_op jit(solution)/shard_map/sweep_first/pallas_call | solution.py:325
  1.2 3.0 %collective-permute-start = (f32[6,24,128]{2,1,0:T(8,128)S(1)}, f32[6,24,128]{2,1,0:T(8,128)S(1)}, u32[]{:S(2)}, u32[]{:S(2)}) collective-permute-start(f32[6,24,128]{2,1,0:T(8,128)S(1)} %get-tuple-element.11), channel_id=1, source_target_pairs={{0,4},{1,5},{2,6},{3,7},{4,0},{5,1},{6,2},{7,3},{8,12},{9,13},{10,... | collective-permute-start | bytes 221192 | tf_op jit(solution)/shard_map/ppermute | solution.py:323
  4.2 0.0 collective-permute-start.1
  4.2 3.4 %collective-permute-done.one_ref = f32[6,24,128]{2,1,0:T(8,128)S(1)} collective-permute-done((f32[6,24,128]{2,1,0:T(8,128)S(1)}, f32[6,24,128]{2,1,0:T(8,128)S(1)}, u32[]{:S(2)}, u32[]{:S(2)}) %collective-permute-start) | collective-permute-done | bytes 73760 | tf_op jit(solution)/shard_map/ppermute | solution.py:323
  7.6 0.0 collective-permute-done.1.two_ref
  7.6 0.4 %sweep_second.1 = (f32[5,64,128]{2,1,0:T(8,128)S(1)}, f32[6,8,128]{2,1,0:T(8,128)S(1)}) custom-call(f32[6,64,128]{2,1,0:T(8,128)S(1)} %get-tuple-element.10.swept_ref.gamma_ref, f32[6,24,128]{2,1,0:T(8,128)S(1)} %collective-permute-done.one_ref, f32[6,24,128]{2,1,0:T(8,128)S(1)} %collective-permute-done.1.two_ref), custom_call_target="tpu_custom_call" | custom-call | tf_op jit(solution)/shard_map/sweep_second/pallas_call | solution.py:336
  8.0 2.5 %collective-permute-start.3 = (f32[6,8,128]{2,1,0:T(8,128)S(1)}, f32[6,8,128]{2,1,0:T(8,128)S(1)}, u32[]{:S(2)}, u32[]{:S(2)}) collective-permute-start(f32[6,8,128]{2,1,0:T(8,128)S(1)} %get-tuple-element.14.window_ref), channel_id=1, source_target_pairs={{0,4},{1,2},{2,1},{3,7},{4,0},{5,6},{6,5},{7,3},{8,12},{9,10},{10,... | collective-permute-start | bytes 73736 | tf_op jit(solution)/shard_map/ppermute | solution.py:323
  10.4 0.0 collective-permute-start.2
  10.4 1.8 %collective-permute-done.3.two_ref = f32[6,8,128]{2,1,0:T(8,128)S(1)} collective-permute-done((f32[6,8,128]{2,1,0:T(8,128)S(1)}, f32[6,8,128]{2,1,0:T(8,128)S(1)}, u32[]{:S(2)}, u32[]{:S(2)}) %collective-permute-start.3) | collective-permute-done | bytes 24608 | tf_op jit(solution)/shard_map/ppermute | solution.py:323
  12.3 0.0 collective-permute-done.2.one_ref
  12.3 1.9 %sweep_third.1 = f32[5,64,128]{2,1,0:T(8,128)} custom-call(f32[5,64,128]{2,1,0:T(8,128)S(1)} %get-tuple-element.13.swept_ref, f32[6,64,128]{2,1,0:T(8,128)S(1)} %get-tuple-element.10.swept_ref.gamma_ref, f32[6,8,128]{2,1,0:T(8,128)S(1)} %get-tuple-element.14.window_ref, f32[6,8,128]{2,1,0:T(8,128)S(1)} %collective-permute-done.2.one_ref, ...), custom_call_target="tpu_custom_call" | custom-call | tf_op jit(solution)/shard_map/sweep_third/pallas_call | solution.py:344
Async XLA Ops:
  1.2 6.4 %collective-permute-start = (f32[6,24,128]{2,1,0:T(8,128)S(1)}, f32[6,24,128]{2,1,0:T(8,128)S(1)}, u32[]{:S(2)}, u32[]{:S(2)}) collective-permute-start(f32[6,24,128]{2,1,0:T(8,128)S(1)} %get-tuple-element.11), channel_id=1, source_target_pairs={{0,4},{1,5},{2,6},{3,7},{4,0},{5,1},{6,2},{7,3},{8,12},{9,13},{10,... | collective-permute-start | bytes 221192 | tf_op jit(solution)/shard_map/ppermute | solution.py:323
  4.2 3.4 %collective-permute-start.1 = (f32[6,24,128]{2,1,0:T(8,128)S(1)}, f32[6,24,128]{2,1,0:T(8,128)S(1)}, u32[]{:S(2)}, u32[]{:S(2)}) collective-permute-start(f32[6,24,128]{2,1,0:T(8,128)S(1)} %get-tuple-element.12), channel_id=1, source_target_pairs={{0,1},{1,0},{2,3},{3,2},{4,8},{5,9},{6,10},{7,11},{8,4},{9,5},{10,... | collective-permute-start | bytes 221192 | tf_op jit(solution)/shard_map/ppermute | solution.py:323
  8.0 4.3 %collective-permute-start.3 = (f32[6,8,128]{2,1,0:T(8,128)S(1)}, f32[6,8,128]{2,1,0:T(8,128)S(1)}, u32[]{:S(2)}, u32[]{:S(2)}) collective-permute-start(f32[6,8,128]{2,1,0:T(8,128)S(1)} %get-tuple-element.14.window_ref), channel_id=1, source_target_pairs={{0,4},{1,2},{2,1},{3,7},{4,0},{5,6},{6,5},{7,3},{8,12},{9,10},{10,... | collective-permute-start | bytes 73736 | tf_op jit(solution)/shard_map/ppermute | solution.py:323
  10.4 1.8 %collective-permute-start.2 = (f32[6,8,128]{2,1,0:T(8,128)S(1)}, f32[6,8,128]{2,1,0:T(8,128)S(1)}, u32[]{:S(2)}, u32[]{:S(2)}) collective-permute-start(f32[6,8,128]{2,1,0:T(8,128)S(1)} %get-tuple-element.14.window_ref), channel_id=1, source_target_pairs={{0,1},{1,0},{2,3},{3,2},{4,5},{5,4},{6,7},{7,6},{8,9},{9,8},{10,11... | collective-permute-start | bytes 73736 | tf_op jit(solution)/shard_map/ppermute | solution.py:323

commit v3 on v2

--- a/solution.py
+++ b/solution.py
@@ -247,7 +247,20 @@
     return updated(cons, flux, [behind(x) for x in flux], normal)
 
 
-def third_kernel(col_axis, cols, swept_ref, gamma_ref, window_ref, one_ref, two_ref, out_ref):
+def third_kernel(swept_ref, gamma_ref, out_ref):
+    ny = SUB
+    nx = swept_ref.shape[1] // ny
+    for tile in range(nx // SUB):
+        base = tile * SUB
+        for y in range(ny):
+            at = pl.ds(y * nx + base, SUB)
+            cons = [swept_ref[f, at, :] for f in range(5)]
+            inner = sweep_lanes(cons, gamma_ref[5, at, :], 2)
+            for f in range(5):
+                out_ref[f, pl.ds(base * ny + y, SUB, stride=ny), :] = inner[f]
+
+
+def edge_kernel(col_axis, cols, inner_ref, window_ref, one_ref, two_ref, out_ref, held, sems):
     nx = window_ref.shape[1]
     ny = SUB
     col = lax.axis_index(col_axis)
@@ -255,9 +268,10 @@
     first, last = col == 0, col == cols - 1
     lane = lax.broadcasted_iota(jnp.int32, (SUB, LANES), 1)
     slot = lane % GROUP
+    at_edge = (lane < HALO) | (lane >= LANES - HALO)
+    edge_new = []
     for tile in range(nx // SUB):
-        base = tile * SUB
-        rows = pl.ds(base, SUB)
+        rows = pl.ds(tile * SUB, SUB)
         left_window, right_window = [], []
         for f in range(6):
             own, one, two = window_ref[f, rows, :], one_ref[f, rows, :], two_ref[f, rows, :]
@@ -279,18 +293,20 @@
             right_window.append(jnp.where((slot >= 6) & (slot <= 8), after, own))
         left_new = sweep_lanes(left_window[:5], left_window[5], 2)
         right_new = sweep_lanes(right_window[:5], right_window[5], 2)
-        edge_new = [jnp.where(slot >= 6, a, b) for a, b in zip(left_new, right_new)]
-        at_edge = (lane < HALO) | (lane >= LANES - HALO)
-        for y in range(ny):
-            at = pl.ds(y * nx + base, SUB)
-            cons = [swept_ref[f, at, :] for f in range(5)]
-            inner = sweep_lanes(cons, gamma_ref[5, at, :], 2)
-            turn = (LANES - 6 - GROUP * y) % LANES
-            for f in range(5):
-                edge = pltpu.roll(edge_new[f], turn, 1)
-                out_ref[f, pl.ds(base * ny + y, SUB, stride=ny), :] = jnp.where(
-                    at_edge, edge, inner[f]
-                )
+        edge_new.append([jnp.where(slot >= 6, a, b) for a, b in zip(left_new, right_new)])
+    copies = []
+    for f in range(5):
+        for tile in range(nx // SUB):
+            for y in range(ny):
+                turn = (LANES - 6 - GROUP * y) % LANES
+                edge = pltpu.roll(edge_new[tile][f], turn, 1)
+                at = pl.ds(tile * SUB * ny + y, SUB, stride=ny)
+                held[f, at, :] = jnp.where(at_edge, edge, inner_ref[f, at, :])
+        copy = pltpu.make_async_copy(held.at[f], out_ref.at[f], sems.at[f])
+        copy.start()
+        copies.append(copy)
+    for copy in copies:
+        copy.wait()
 
 
 def swap_pairs(mesh, axis, inner):
@@ -308,7 +324,7 @@
             if axis == "row":
                 to = (r, c ^ 1) if k is None else (k, c)
             else:
-                to = (r ^ 1, c) if k is None else (r, k)
+                to = (r, cols - 1 - c) if k is None else (r, k)
             pairs.append((r * cols + c, to[0] * cols + to[1]))
     return pairs
 
@@ -341,12 +357,24 @@
         name="sweep_second",
     )(keep(swept), keep(one), keep(two))
     one, two = swap(window, "col", False), swap(window, "col", True)
+    inner = pl.pallas_call(
+        third_kernel,
+        out_shape=here(5, nx * ny, nz),
+        in_specs=[near] * 2,
+        out_specs=near,
+        name="sweep_third",
+    )(keep(after), keep(swept))
     out = pl.pallas_call(
-        functools.partial(third_kernel, "col", cols),
+        functools.partial(edge_kernel, "col", cols),
         out_shape=jax.ShapeDtypeStruct((5, nx * ny, nz), jnp.float32),
-        in_specs=[near] * 5,
-        name="sweep_third",
-    )(keep(after), keep(swept), keep(window), keep(one), keep(two))
+        in_specs=[near] * 4,
+        out_specs=pl.BlockSpec(memory_space=pltpu.HBM),
+        scratch_shapes=[
+            pltpu.VMEM((5, nx * ny, nz), jnp.float32),
+            pltpu.SemaphoreType.DMA((5,)),
+        ],
+        name="third_edges",
+    )(keep(inner), keep(window), keep(one), keep(two))
     return out.reshape(5, nx, ny, nz)
 
 

time: 14.3 us -> 13.6 us (0.951)
  the two profiles are of different devices: /device:TPU:0 before, /device:TPU:9 now
where the time goes in v3:
time: 13.6 us; the launch traced here: 13.4 us
  waiting for transfers between devices  5.55 us (41%)
  starting transfers between devices  4.56 us (34%)
  Pallas kernels  3.32 us (24%)
    ppermute x4, waiting for transfers between devices, body(): lax.ppermute(x, ('row', 'col'), swap_pairs(mesh, axis, inner))  5.55 us
    ppermute x4, starting transfers between devices, body(): lax.ppermute(x, ('row', 'col'), swap_pairs(mesh, axis, inner))  4.56 us
    pallas_call x1, Pallas kernels, body(): pl.pallas_call(functools.partial(edge_kernel, 'col', cols), out_shape=jax...  1.26 us
    pallas_call x1, Pallas kernels, body(): pl.pallas_call(functools.partial(first_kernel, 'row'), out_shape=(here(6,...  1.15 us
    pallas_call x1, Pallas kernels, body(): pl.pallas_call(third_kernel, out_shape=here(5, nx * ny, nz), in_specs=[ne...  0.52 us
    pallas_call x1, Pallas kernels, body(): pl.pallas_call(functools.partial(second_kernel, 'row', rows), out_shape=(...  0.39 us
  transfers between devices with their start and end apart: 4, of which 3 were waited for; matrix products, arithmetic and copies ran while one was open for 0% of the time, Pallas kernels for 4%

profile of v3, /device:TPU:9, one launch (start us, length us, event | category | flops | bytes accessed | tf_op | source)
XLA Modules:
  0.0 13.4 jit_solution(12763205092861160142)
XLA Ops:
  0.0 1.1 %sweep_first.1 = (f32[6,64,128]{2,1,0:T(8,128)S(1)}, f32[6,24,128]{2,1,0:T(8,128)S(1)}, f32[6,24,128]{2,1,0:T(8,128)S(1)}) custom-call(f32[5,8,8,128]{3,2,1,0:T(8,128)} %state_ref.1, f32[8,8,128]{2,1,0:T(8,128)} %gamma_ref.1), custom_call_target="tpu_custom_call" | custom-call | tf_op jit(solution)/shard_map/sweep_first/pallas_call | solution.py:341
  1.2 1.3 %collective-permute-start = (f32[6,24,128]{2,1,0:T(8,128)S(1)}, f32[6,24,128]{2,1,0:T(8,128)S(1)}, u32[]{:S(2)}, u32[]{:S(2)}) collective-permute-start(f32[6,24,128]{2,1,0:T(8,128)S(1)} %get-tuple-element.11), channel_id=1, source_target_pairs={{0,4},{1,5},{2,6},{3,7},{4,0},{5,1},{6,2},{7,3},{8,12},{9,13},{10,... | collective-permute-start | bytes 221192 | tf_op jit(solution)/shard_map/ppermute | solution.py:339
  2.5 0.0 collective-permute-start.1
  2.5 2.0 %collective-permute-done.one_ref = f32[6,24,128]{2,1,0:T(8,128)S(1)} collective-permute-done((f32[6,24,128]{2,1,0:T(8,128)S(1)}, f32[6,24,128]{2,1,0:T(8,128)S(1)}, u32[]{:S(2)}, u32[]{:S(2)}) %collective-permute-start) | collective-permute-done | bytes 73760 | tf_op jit(solution)/shard_map/ppermute | solution.py:339
  4.4 2.1 %collective-permute-done.1.two_ref = f32[6,24,128]{2,1,0:T(8,128)S(1)} collective-permute-done((f32[6,24,128]{2,1,0:T(8,128)S(1)}, f32[6,24,128]{2,1,0:T(8,128)S(1)}, u32[]{:S(2)}, u32[]{:S(2)}) %collective-permute-start.1) | collective-permute-done | bytes 73760 | tf_op jit(solution)/shard_map/ppermute | solution.py:339
  6.6 0.4 %sweep_second.1 = (f32[5,64,128]{2,1,0:T(8,128)S(1)}, f32[6,8,128]{2,1,0:T(8,128)S(1)}) custom-call(f32[6,64,128]{2,1,0:T(8,128)S(1)} %get-tuple-element.10.swept_ref.gamma_ref, f32[6,24,128]{2,1,0:T(8,128)S(1)} %collective-permute-done.one_ref, f32[6,24,128]{2,1,0:T(8,128)S(1)} %collective-permute-done.1.two_ref), custom_call_target="tpu_custom_call" | custom-call | tf_op jit(solution)/shard_map/sweep_second/pallas_call | solution.py:352
  7.0 3.2 %collective-permute-start.3 = (f32[6,8,128]{2,1,0:T(8,128)S(1)}, f32[6,8,128]{2,1,0:T(8,128)S(1)}, u32[]{:S(2)}, u32[]{:S(2)}) collective-permute-start(f32[6,8,128]{2,1,0:T(8,128)S(1)} %get-tuple-element.14.window_ref), channel_id=1, source_target_pairs={{0,3},{1,2},{2,1},{3,0},{4,7},{5,6},{6,5},{7,4},{8,11},{9,10},{10,... | collective-permute-start | bytes 73736 | tf_op jit(solution)/shard_map/ppermute | solution.py:339
  10.2 0.0 collective-permute-start.2
  10.2 0.5 %sweep_third.1.inner_ref = f32[5,64,128]{2,1,0:T(8,128)S(1)} custom-call(f32[5,64,128]{2,1,0:T(8,128)S(1)} %get-tuple-element.13.swept_ref, f32[6,64,128]{2,1,0:T(8,128)S(1)} %get-tuple-element.10.swept_ref.gamma_ref), custom_call_target="tpu_custom_call" | custom-call | tf_op jit(solution)/shard_map/sweep_third/pallas_call | solution.py:360
  10.7 1.4 %collective-permute-done.3.two_ref = f32[6,8,128]{2,1,0:T(8,128)S(1)} collective-permute-done((f32[6,8,128]{2,1,0:T(8,128)S(1)}, f32[6,8,128]{2,1,0:T(8,128)S(1)}, u32[]{:S(2)}, u32[]{:S(2)}) %collective-permute-start.3) | collective-permute-done | bytes 24608 | tf_op jit(solution)/shard_map/ppermute | solution.py:339
  12.2 0.0 collective-permute-done.2.one_ref
  12.2 1.3 %third_edges.1 = f32[5,64,128]{2,1,0:T(8,128)} custom-call(f32[5,64,128]{2,1,0:T(8,128)S(1)} %sweep_third.1.inner_ref, f32[6,8,128]{2,1,0:T(8,128)S(1)} %get-tuple-element.14.window_ref, f32[6,8,128]{2,1,0:T(8,128)S(1)} %collective-permute-done.2.one_ref, f32[6,8,128]{2,1,0:T(8,128)S(1)} %collective-permute-done.3.two_ref), custom_call_target="tpu_custom_call" | custom-call | tf_op jit(solution)/shard_map/third_edges/pallas_call | solution.py:367
Async XLA Ops:
  1.2 3.3 %collective-permute-start = (f32[6,24,128]{2,1,0:T(8,128)S(1)}, f32[6,24,128]{2,1,0:T(8,128)S(1)}, u32[]{:S(2)}, u32[]{:S(2)}) collective-permute-start(f32[6,24,128]{2,1,0:T(8,128)S(1)} %get-tuple-element.11), channel_id=1, source_target_pairs={{0,4},{1,5},{2,6},{3,7},{4,0},{5,1},{6,2},{7,3},{8,12},{9,13},{10,... | collective-permute-start | bytes 221192 | tf_op jit(solution)/shard_map/ppermute | solution.py:339
  2.5 4.1 %collective-permute-start.1 = (f32[6,24,128]{2,1,0:T(8,128)S(1)}, f32[6,24,128]{2,1,0:T(8,128)S(1)}, u32[]{:S(2)}, u32[]{:S(2)}) collective-permute-start(f32[6,24,128]{2,1,0:T(8,128)S(1)} %get-tuple-element.12), channel_id=1, source_target_pairs={{0,1},{1,0},{2,3},{3,2},{4,8},{5,9},{6,10},{7,11},{8,4},{9,5},{10,... | collective-permute-start | bytes 221192 | tf_op jit(solution)/shard_map/ppermute | solution.py:339
  7.0 5.2 %collective-permute-start.3 = (f32[6,8,128]{2,1,0:T(8,128)S(1)}, f32[6,8,128]{2,1,0:T(8,128)S(1)}, u32[]{:S(2)}, u32[]{:S(2)}) collective-permute-start(f32[6,8,128]{2,1,0:T(8,128)S(1)} %get-tuple-element.14.window_ref), channel_id=1, source_target_pairs={{0,3},{1,2},{2,1},{3,0},{4,7},{5,6},{6,5},{7,4},{8,11},{9,10},{10,... | collective-permute-start | bytes 73736 | tf_op jit(solution)/shard_map/ppermute | solution.py:339
  10.2 2.0 %collective-permute-start.2 = (f32[6,8,128]{2,1,0:T(8,128)S(1)}, f32[6,8,128]{2,1,0:T(8,128)S(1)}, u32[]{:S(2)}, u32[]{:S(2)}) collective-permute-start(f32[6,8,128]{2,1,0:T(8,128)S(1)} %get-tuple-element.14.window_ref), channel_id=1, source_target_pairs={{0,1},{1,0},{2,3},{3,2},{4,5},{5,4},{6,7},{7,6},{8,9},{9,8},{10,11... | collective-permute-start | bytes 73736 | tf_op jit(solution)/shard_map/ppermute | solution.py:339

commit v4 on v3

--- a/solution.py
+++ b/solution.py
@@ -83,7 +83,8 @@
     return out
 
 
-def sweep_rows(load, load_gamma, store, n, normal, outflow):
+def sweep_rows(load, load_gamma, store, n, normal, halo=None):
+    outflow = halo is None
     cons, gam, prim, diff, rise, edge = {}, {}, {}, {}, {}, {}
 
     def zone(i):
@@ -92,11 +93,16 @@
     def get(i):
         i = zone(i)
         if i not in cons:
-            cons[i] = load(i)
-            g = load_gamma(i)
-            gam1 = g - 1.0
-            gam[i] = (g, recip(gam1))
-            prim[i] = primitives(cons[i], gam1, normal)
+            inside = 0 <= i < n
+            if inside or i in (-1, n):
+                g = load_gamma(i)
+                gam1 = g - 1.0
+                gam[i] = (g, recip(gam1))
+            if inside:
+                cons[i] = load(i)
+                prim[i] = primitives(cons[i], gam1, normal)
+            else:
+                prim[i] = halo(i, get(0 if i < 0 else n - 1))
         return prim[i]
 
     def get_diff(i):
@@ -161,20 +167,28 @@
         store,
         nx,
         0,
-        True,
     )
     for x in range(nx):
         swept_ref[5, pl.ds(x, ny, stride=nx), :] = gamma_ref[x]
-    odd = lax.rem(lax.axis_index(row_axis), 2)
-    low, high = 0, (ny - HALO) * nx
-    start_one = pl.multiple_of(jnp.where(odd == 1, low, high), SUB)
-    start_two = pl.multiple_of(jnp.where(odd == 1, high, low), SUB)
-    for f in range(6):
-        one_ref[f] = swept_ref[f, pl.ds(start_one, HALO * nx), :]
-        two_ref[f] = swept_ref[f, pl.ds(start_two, HALO * nx), :]
-
-
-def second_kernel(row_axis, rows, swept_ref, one_ref, two_ref, next_ref, window_ref):
+    odd = lax.rem(lax.axis_index(row_axis), 2) == 1
+    for base in range(0, nx, SUB):
+        sides = []
+        for zones, last in ((range(HALO), 0), (range(ny - HALO, ny), ny - 1)):
+            rows = []
+            for y in zones:
+                at = pl.ds(y * nx + base, SUB)
+                gamma = swept_ref[5, at, :]
+                rows.append(primitives([swept_ref[f, at, :] for f in range(5)], gamma - 1.0, 1))
+            rows = [row[k] for k in range(5) for row in rows]
+            rows.append(swept_ref[5, pl.ds(last * nx + base, SUB), :])
+            sides.append(rows)
+        at = pl.ds(base, SUB)
+        for k, (low, high) in enumerate(zip(*sides)):
+            one_ref[k, at, :] = jnp.where(odd, low, high)
+            two_ref[k, at, :] = jnp.where(odd, high, low)
+
+
+def second_kernel(row_axis, rows, swept_ref, two_ref, one_ref, next_ref, window_ref):
     nx = swept_ref.shape[1] // SUB
     ny = SUB
     row = lax.axis_index(row_axis)
@@ -185,16 +199,26 @@
     for tile in range(nx // SUB):
         base = tile * SUB
 
-        def load_field(f, y):
+        at_base = pl.ds(base, SUB)
+
+        def own(f, y):
+            return swept_ref[f, pl.ds(y * nx + base, SUB), :]
+
+        def received(k, low_side):
+            one, two = one_ref[k, at_base, :], two_ref[k, at_base, :]
+            return jnp.where(odd, one, two) if low_side else jnp.where(odd, two, one)
+
+        def halo(y, nearest):
+            j, end = (y + HALO, first) if y < 0 else (y - ny, last)
+            return [
+                jnp.where(end, nearest[k], received(HALO * k + j, y < 0)) for k in range(5)
+            ]
+
+        def load_gamma(y):
             if 0 <= y < ny:
-                return swept_ref[f, pl.ds(y * nx + base, SUB), :]
-            at = pl.ds((y + HALO if y < 0 else y - ny) * nx + base, SUB)
-            one, two = one_ref[f, at, :], two_ref[f, at, :]
-            if y < 0:
-                got = jnp.where(odd, one, two)
-                return jnp.where(first, swept_ref[f, pl.ds(base, SUB), :], got)
-            got = jnp.where(odd, two, one)
-            return jnp.where(last, swept_ref[f, pl.ds((ny - 1) * nx + base, SUB), :], got)
+                return own(5, y)
+            end, edge = (first, 0) if y < 0 else (last, ny - 1)
+            return jnp.where(end, own(5, edge), received(5 * HALO, y < 0))
 
         windows = [None] * 6
 
@@ -209,15 +233,15 @@
                 into_window(f, y, cons[f])
 
         sweep_rows(
-            lambda y: [load_field(f, y) for f in range(5)],
-            lambda y: load_field(5, y),
+            lambda y: [own(f, y) for f in range(5)],
+            load_gamma,
             store,
             ny,
             1,
-            False,
+            halo,
         )
         for y in range(ny):
-            into_window(5, y, swept_ref[5, pl.ds(y * nx + base, SUB), :])
+            into_window(5, y, own(5, y))
         for f in range(6):
             window_ref[f, pl.ds(base, SUB), :] = windows[f]
 
@@ -245,6 +269,26 @@
         state_flux(lower_next, ahead(gamma), ahead(inv_gam1)),
     )
     return updated(cons, flux, [behind(x) for x in flux], normal)
+
+
+def sweep_window(cons, gamma, normal):
+    def turned(x, by):
+        return pltpu.roll(x, (LANES - by) % LANES, 1)
+
+    gam1 = gamma - 1.0
+    inv_gam1 = recip(gam1)
+    upper, lower = [], []
+    for q in primitives(cons, gam1, normal):
+        line = [q if k == 0 else turned(q, k) for k in range(-2, 4)]
+        diff = [b - a for a, b in zip(line, line[1:])]
+        rise = [face_rise(*diff[k : k + 3]) for k in range(3)]
+        upper.append(q + clamp_zero(rise[1], 2.0 * (diff[1] - rise[0])))
+        lower.append(line[3] - clamp_zero(diff[2] - rise[1], 2.0 * rise[2]))
+    flux = double_flux(
+        state_flux(upper, gamma, inv_gam1),
+        state_flux(lower, turned(gamma, 1), turned(inv_gam1, 1)),
+    )
+    return updated(cons, flux, [turned(x, -1) for x in flux], normal)
 
 
 def third_kernel(swept_ref, gamma_ref, out_ref):
@@ -291,8 +335,8 @@
             after = jnp.where(last, high, after)
             left_window.append(jnp.where((slot >= 3) & (slot <= 5), before, own))
             right_window.append(jnp.where((slot >= 6) & (slot <= 8), after, own))
-        left_new = sweep_lanes(left_window[:5], left_window[5], 2)
-        right_new = sweep_lanes(right_window[:5], right_window[5], 2)
+        left_new = sweep_window(left_window[:5], left_window[5], 2)
+        right_new = sweep_window(right_window[:5], right_window[5], 2)
         edge_new.append([jnp.where(slot >= 6, a, b) for a, b in zip(left_new, right_new)])
     copies = []
     for f in range(5):
@@ -342,20 +386,21 @@
         functools.partial(first_kernel, "row"),
         out_shape=(
             here(6, ny * nx, nz),
-            here(6, HALO * nx, nz),
-            here(6, HALO * nx, nz),
+            here(5 * HALO + 1, nx, nz),
+            here(5 * HALO + 1, nx, nz),
         ),
         out_specs=(near,) * 3,
         name="sweep_first",
     )(state, gamma)
-    one, two = swap(one, "row", False), swap(two, "row", True)
+    two = swap(two, "row", True)
+    one = swap(one, "row", False)
     after, window = pl.pallas_call(
         functools.partial(second_kernel, "row", rows),
         out_shape=(here(5, ny * nx, nz), here(6, nx, nz)),
         in_specs=[near] * 3,
         out_specs=(near,) * 2,
         name="sweep_second",
-    )(keep(swept), keep(one), keep(two))
+    )(keep(swept), keep(two), keep(one))
     one, two = swap(window, "col", False), swap(window, "col", True)
     inner = pl.pallas_call(
         third_kernel,

time: 13.6 us -> 13.1 us (0.963)
  the two profiles are of different devices: /device:TPU:9 before, /device:TPU:0 now
where the time goes in v4:
time: 13.1 us; the launch traced here: 12.9 us
  starting transfers between devices  6.22 us (47%)
  waiting for transfers between devices  3.58 us (27%)
  Pallas kernels  3.11 us (24%)
    ppermute x4, starting transfers between devices, body(): lax.ppermute(x, ('row', 'col'), swap_pairs(mesh, axis, inner))  6.22 us
    ppermute x4, waiting for transfers between devices, body(): lax.ppermute(x, ('row', 'col'), swap_pairs(mesh, axis, inner))  3.58 us
    pallas_call x1, Pallas kernels, body(): pl.pallas_call(functools.partial(first_kernel, 'row'), out_shape=(here(6,...  1.16 us
    pallas_call x1, Pallas kernels, body(): pl.pallas_call(functools.partial(edge_kernel, 'col', cols), out_shape=jax...  1.08 us
    pallas_call x1, Pallas kernels, body(): pl.pallas_call(third_kernel, out_shape=here(5, nx * ny, nz), in_specs=[ne...  0.51 us
    pallas_call x1, Pallas kernels, body(): pl.pallas_call(functools.partial(second_kernel, 'row', rows), out_shape=(...  0.35 us
  transfers between devices with their start and end apart: 4, of which 2 were waited for; matrix products, arithmetic and copies ran while one was open for 0% of the time, Pallas kernels for 4%

profile of v4, /device:TPU:0, one launch (start us, length us, event | category | flops | bytes accessed | tf_op | source)
XLA Modules:
  0.0 12.9 jit_solution(8453602035241183341)
XLA Ops:
  0.0 1.2 %sweep_first.1 = (f32[6,64,128]{2,1,0:T(8,128)S(1)}, f32[16,8,128]{2,1,0:T(8,128)S(1)}, f32[16,8,128]{2,1,0:T(8,128)S(1)}) custom-call(f32[5,8,8,128]{3,2,1,0:T(8,128)} %state_ref.1, f32[8,8,128]{2,1,0:T(8,128)} %gamma_ref.1), custom_call_target="tpu_custom_call" | custom-call | tf_op jit(solution)/shard_map/sweep_first/pallas_call | solution.py:385
  1.2 0.5 %collective-permute-start = (f32[16,8,128]{2,1,0:T(8,128)S(1)}, f32[16,8,128]{2,1,0:T(8,128)S(1)}, u32[]{:S(2)}, u32[]{:S(2)}) collective-permute-start(f32[16,8,128]{2,1,0:T(8,128)S(1)} %get-tuple-element.11), channel_id=1, source_target_pairs={{0,1},{1,0},{2,3},{3,2},{4,8},{5,9},{6,10},{7,11},{8,4},{9,5},{10,... | collective-permute-start | bytes 196616 | tf_op jit(solution)/shard_map/ppermute | solution.py:383
  1.7 4.0 %collective-permute-start.1 = (f32[16,8,128]{2,1,0:T(8,128)S(1)}, f32[16,8,128]{2,1,0:T(8,128)S(1)}, u32[]{:S(2)}, u32[]{:S(2)}) collective-permute-start(f32[16,8,128]{2,1,0:T(8,128)S(1)} %get-tuple-element.12), channel_id=1, source_target_pairs={{0,4},{1,5},{2,6},{3,7},{4,0},{5,1},{6,2},{7,3},{8,12},{9,13},{10,... | collective-permute-start | bytes 196616 | tf_op jit(solution)/shard_map/ppermute | solution.py:383
  5.7 0.0 collective-permute-done.two_ref
  5.7 2.2 %collective-permute-done.1.one_ref = f32[16,8,128]{2,1,0:T(8,128)S(1)} collective-permute-done((f32[16,8,128]{2,1,0:T(8,128)S(1)}, f32[16,8,128]{2,1,0:T(8,128)S(1)}, u32[]{:S(2)}, u32[]{:S(2)}) %collective-permute-start.1) | collective-permute-done | bytes 65568 | tf_op jit(solution)/shard_map/ppermute | solution.py:383
  8.0 0.4 %sweep_second.1 = (f32[5,64,128]{2,1,0:T(8,128)S(1)}, f32[6,8,128]{2,1,0:T(8,128)S(1)}) custom-call(f32[6,64,128]{2,1,0:T(8,128)S(1)} %get-tuple-element.10.swept_ref.gamma_ref, f32[16,8,128]{2,1,0:T(8,128)S(1)} %collective-permute-done.two_ref, f32[16,8,128]{2,1,0:T(8,128)S(1)} %collective-permute-done.1.one_ref), custom_call_target="tpu_custom_call" | custom-call | tf_op jit(solution)/shard_map/sweep_second/pallas_call | solution.py:397
  8.3 0.5 %collective-permute-start.3 = (f32[6,8,128]{2,1,0:T(8,128)S(1)}, f32[6,8,128]{2,1,0:T(8,128)S(1)}, u32[]{:S(2)}, u32[]{:S(2)}) collective-permute-start(f32[6,8,128]{2,1,0:T(8,128)S(1)} %get-tuple-element.14.window_ref), channel_id=1, source_target_pairs={{0,3},{1,2},{2,1},{3,0},{4,7},{5,6},{6,5},{7,4},{8,11},{9,10},{10,... | collective-permute-start | bytes 73736 | tf_op jit(solution)/shard_map/ppermute | solution.py:383
  8.8 1.2 %collective-permute-start.2 = (f32[6,8,128]{2,1,0:T(8,128)S(1)}, f32[6,8,128]{2,1,0:T(8,128)S(1)}, u32[]{:S(2)}, u32[]{:S(2)}) collective-permute-start(f32[6,8,128]{2,1,0:T(8,128)S(1)} %get-tuple-element.14.window_ref), channel_id=1, source_target_pairs={{0,1},{1,0},{2,3},{3,2},{4,5},{5,4},{6,7},{7,6},{8,9},{9,8},{10,11... | collective-permute-start | bytes 73736 | tf_op jit(solution)/shard_map/ppermute | solution.py:383
  10.0 0.5 %sweep_third.1.inner_ref = f32[5,64,128]{2,1,0:T(8,128)S(1)} custom-call(f32[5,64,128]{2,1,0:T(8,128)S(1)} %get-tuple-element.13.swept_ref, f32[6,64,128]{2,1,0:T(8,128)S(1)} %get-tuple-element.10.swept_ref.gamma_ref), custom_call_target="tpu_custom_call" | custom-call | tf_op jit(solution)/shard_map/sweep_third/pallas_call | solution.py:405
  10.5 1.3 %collective-permute-done.3.two_ref = f32[6,8,128]{2,1,0:T(8,128)S(1)} collective-permute-done((f32[6,8,128]{2,1,0:T(8,128)S(1)}, f32[6,8,128]{2,1,0:T(8,128)S(1)}, u32[]{:S(2)}, u32[]{:S(2)}) %collective-permute-start.3) | collective-permute-done | bytes 24608 | tf_op jit(solution)/shard_map/ppermute | solution.py:383
  11.9 0.0 collective-permute-done.2.one_ref
  11.9 1.1 %third_edges.1 = f32[5,64,128]{2,1,0:T(8,128)} custom-call(f32[5,64,128]{2,1,0:T(8,128)S(1)} %sweep_third.1.inner_ref, f32[6,8,128]{2,1,0:T(8,128)S(1)} %get-tuple-element.14.window_ref, f32[6,8,128]{2,1,0:T(8,128)S(1)} %collective-permute-done.2.one_ref, f32[6,8,128]{2,1,0:T(8,128)S(1)} %collective-permute-done.3.two_ref), custom_call_target="tpu_custom_call" | custom-call | tf_op jit(solution)/shard_map/third_edges/pallas_call | solution.py:412
Async XLA Ops:
  1.2 4.6 %collective-permute-start = (f32[16,8,128]{2,1,0:T(8,128)S(1)}, f32[16,8,128]{2,1,0:T(8,128)S(1)}, u32[]{:S(2)}, u32[]{:S(2)}) collective-permute-start(f32[16,8,128]{2,1,0:T(8,128)S(1)} %get-tuple-element.11), channel_id=1, source_target_pairs={{0,1},{1,0},{2,3},{3,2},{4,8},{5,9},{6,10},{7,11},{8,4},{9,5},{10,... | collective-permute-start | bytes 196616 | tf_op jit(solution)/shard_map/ppermute | solution.py:383
  1.7 6.3 %collective-permute-start.1 = (f32[16,8,128]{2,1,0:T(8,128)S(1)}, f32[16,8,128]{2,1,0:T(8,128)S(1)}, u32[]{:S(2)}, u32[]{:S(2)}) collective-permute-start(f32[16,8,128]{2,1,0:T(8,128)S(1)} %get-tuple-element.12), channel_id=1, source_target_pairs={{0,4},{1,5},{2,6},{3,7},{4,0},{5,1},{6,2},{7,3},{8,12},{9,13},{10,... | collective-permute-start | bytes 196616 | tf_op jit(solution)/shard_map/ppermute | solution.py:383
  8.3 3.5 %collective-permute-start.3 = (f32[6,8,128]{2,1,0:T(8,128)S(1)}, f32[6,8,128]{2,1,0:T(8,128)S(1)}, u32[]{:S(2)}, u32[]{:S(2)}) collective-permute-start(f32[6,8,128]{2,1,0:T(8,128)S(1)} %get-tuple-element.14.window_ref), channel_id=1, source_target_pairs={{0,3},{1,2},{2,1},{3,0},{4,7},{5,6},{6,5},{7,4},{8,11},{9,10},{10,... | collective-permute-start | bytes 73736 | tf_op jit(solution)/shard_map/ppermute | solution.py:383
  8.8 3.1 %collective-permute-start.2 = (f32[6,8,128]{2,1,0:T(8,128)S(1)}, f32[6,8,128]{2,1,0:T(8,128)S(1)}, u32[]{:S(2)}, u32[]{:S(2)}) collective-permute-start(f32[6,8,128]{2,1,0:T(8,128)S(1)} %get-tuple-element.14.window_ref), channel_id=1, source_target_pairs={{0,1},{1,0},{2,3},{3,2},{4,5},{5,4},{6,7},{7,6},{8,9},{9,8},{10,11... | collective-permute-start | bytes 73736 | tf_op jit(solution)/shard_map/ppermute | solution.py:383

commit v5 on v3

v5 whole, which is shorter than its diff:
```python
import functools

import jax
import jax.numpy as jnp
from jax import lax
from jax.experimental import pallas as pl
from jax.experimental.pallas import tpu as pltpu
from jax.sharding import PartitionSpec as P

STEP = 0.08
HALO = 3
SUB, LANES = 8, 128
GROUP = LANES // SUB


def recip(x):
    r = pl.reciprocal(x, approx=True)
    return r * (2.0 - x * r)


def clamp_zero(u, v):
    return jnp.maximum(jnp.minimum(u, jnp.maximum(v, 0.0)), jnp.minimum(v, 0.0))


def primitives(cons, gam1, normal):
    rho, m0, m1, m2, energy = cons
    inv = recip(rho)
    vel = [m0 * inv, m1 * inv, m2 * inv]
    kinetic = 0.5 * (m0 * vel[0] + m1 * vel[1] + m2 * vel[2])
    pressure = gam1 * (energy - kinetic)
    others = [c for c in range(3) if c != normal]
    return [rho, vel[normal], vel[others[0]], vel[others[1]], pressure]


def face_rise(before, here, after):
    if here is None:
        return None
    rise = 0.5 * here
    if before is not None and after is not None:
        rise = rise + (before - after) * (1.0 / 12.0)
    elif before is not None:
        rise = rise + before * (1.0 / 12.0)
    elif after is not None:
        rise = rise - after * (1.0 / 12.0)
    return clamp_zero(rise, here)


def edges(q, right, left):
    if right is None or left is None:
        return q, q
    return q + clamp_zero(right, 2.0 * left), q - clamp_zero(left, 2.0 * right)


def state_flux(prim, gamma, inv_gam1):
    rho, un, u1, u2, p = prim
    mn, m1, m2 = rho * un, rho * u1, rho * u2
    nn = mn * un
    energy = p * inv_gam1 + 0.5 * (nn + m1 * u1 + m2 * u2)
    flux = [mn, nn + p, mn * u1, mn * u2, un * (energy + p)]
    gp = gamma * p
    speed = jnp.abs(un) + gp * lax.rsqrt(jnp.maximum(gp * rho, 1e-30))
    return [rho, mn, m1, m2, energy], flux, speed


def double_flux(left, right):
    if left is right:
        return [f + f for f in left[1]]
    speed = jnp.maximum(left[2], right[2])
    return [
        (left[1][k] + right[1][k]) - speed * (right[0][k] - left[0][k]) for k in range(5)
    ]


def place(normal):
    others = [c for c in range(3) if c != normal]
    return [0, 1 + normal, 1 + others[0], 1 + others[1], 4]


def updated(cons, flux_right, flux_left, normal):
    out = list(cons)
    for k, field in enumerate(place(normal)):
        out[field] = cons[field] - (0.5 * STEP) * (flux_right[k] - flux_left[k])
    return out


class Sweep:
    def __init__(self, n, normal, load, load_gamma, halo=None):
        self.n, self.normal = n, normal
        self.load, self.load_gamma, self.halo = load, load_gamma, halo
        self.cons, self.gam, self.prim, self.diff, self.rise, self.state = {}, {}, {}, {}, {}, {}

    def zone(self, i):
        return i if self.halo else min(max(i, 0), self.n - 1)

    def get_gam(self, i):
        i = self.zone(i)
        if i not in self.gam:
            gamma = self.load_gamma(i)
            gam1 = gamma - 1.0
            self.gam[i] = (gamma, recip(gam1), gam1)
        return self.gam[i]

    def get_cons(self, i):
        if i not in self.cons:
            self.cons[i] = self.load(i)
        return self.cons[i]

    def get(self, i):
        i = self.zone(i)
        if i not in self.prim:
            if 0 <= i < self.n:
                self.prim[i] = primitives(self.get_cons(i), self.get_gam(i)[2], self.normal)
            else:
                self.prim[i] = self.halo(i)
        return self.prim[i]

    def get_diff(self, i):
        if i not in self.diff:
            a, b = self.get(i), self.get(i + 1)
            self.diff[i] = [None] * 5 if a is b else [y - x for x, y in zip(a, b)]
        return self.diff[i]

    def get_rise(self, i):
        if i not in self.rise:
            here = self.get_diff(i)
            right = [face_rise(*t) for t in zip(self.get_diff(i - 1), here, self.get_diff(i + 1))]
            self.rise[i] = (right, [None if r is None else h - r for h, r in zip(here, right)])
        return self.rise[i]

    def get_state(self, i, upper):
        i = self.zone(i)
        if (i, upper) not in self.state:
            q, right, left = self.get(i), self.get_rise(i)[0], self.get_rise(i - 1)[1]
            pairs = [edges(*t) for t in zip(q, right, left)]
            side = [p[0] if upper else p[1] for p in pairs]
            self.state[i, upper] = state_flux(side, *self.get_gam(i)[:2])
            if all(p[0] is p[1] for p in pairs):
                self.state[i, not upper] = self.state[i, upper]
        return self.state[i, upper]

    def face(self, i):
        if not self.halo and i < 0:
            return double_flux(self.get_state(0, True), self.get_state(0, True))
        if not self.halo and i == self.n - 1:
            return double_flux(self.get_state(i, True), self.get_state(i, True))
        return double_flux(self.get_state(i, True), self.get_state(i + 1, False))

    def run(self, zones, store, flux=None):
        flux = self.face(zones[0] - 1) if flux is None else flux
        for i in zones:
            before, flux = flux, self.face(i)
            store(i, updated(self.get_cons(i), flux, before, self.normal))
        return flux


def own_row(y):
    odd = lax.rem(lax.axis_index("row"), 2) == 1
    return jnp.where(odd, SUB - 1 - y, y)


def own_sign():
    return jnp.where(lax.rem(lax.axis_index("row"), 2) == 1, -1.0, 1.0)


def rows_at(y, base, nx):
    return pl.ds(pl.multiple_of(own_row(y) * nx + base, SUB), SUB)


def first_kernel(state_ref, gamma_ref, swept_ref, one_ref, two_ref):
    nx, ny = gamma_ref.shape[0], gamma_ref.shape[1]

    def store(x, cons):
        for f in range(5):
            swept_ref[f, pl.ds(x, ny, stride=nx), :] = cons[f]

    sweep = Sweep(nx, 0, lambda x: [state_ref[f, x] for f in range(5)], lambda x: gamma_ref[x])
    sweep.run(range(nx), store)
    for x in range(nx):
        swept_ref[5, pl.ds(x, ny, stride=nx), :] = gamma_ref[x]
    for base in range(0, nx, SUB):
        at = pl.ds(base, SUB)
        for out_ref, nearest in ((one_ref, range(ny - 1, ny - 1 - HALO, -1)), (two_ref, range(HALO))):
            for j, y in enumerate(nearest):
                row = rows_at(y, base, nx)
                gamma = swept_ref[5, row, :]
                prim = primitives([swept_ref[f, row, :] for f in range(5)], gamma - 1.0, 1)
                for k in range(5):
                    out_ref[HALO * k + j, at, :] = prim[k]
                if j == 0:
                    out_ref[5 * HALO, at, :] = gamma


def row_loads(swept_ref, base, nx, sign):
    def load(y):
        row = rows_at(y, base, nx)
        cons = [swept_ref[f, row, :] for f in range(5)]
        cons[2] = cons[2] * sign
        return cons

    return load, lambda y: swept_ref[5, rows_at(y, base, nx), :]


def into_window(window, y, value):
    turn = (GROUP * y + 6) % LANES
    rolled = pltpu.roll(value, turn, 1) if turn else value
    if window is None:
        return rolled
    group = lax.broadcasted_iota(jnp.int32, (SUB, LANES), 1) // GROUP
    return jnp.where(group == y, rolled, window)


SPLIT = 5


def kept_arrays(sweep, flux):
    cons, fluxes, speed = sweep.get_state(SPLIT, True)
    kept = [sweep.get(SPLIT + 1), sweep.get(SPLIT + 2), sweep.get_diff(SPLIT)]
    return sum(kept + [sweep.get_rise(SPLIT)[1], cons, fluxes, [speed], flux], [])


KEPT = 36


def second_near(rows, swept_ref, two_ref, next_ref, window_ref, kept_ref):
    nx = swept_ref.shape[1] // SUB
    row = lax.axis_index("row")
    end = (row == 0) | (row == rows - 1)
    sign = own_sign()
    for base in range(0, nx, SUB):
        at = pl.ds(base, SUB)
        load, load_own_gamma = row_loads(swept_ref, base, nx, sign)
        windows = [None] * 6

        def load_gamma(y):
            if y >= 0:
                return load_own_gamma(y)
            return jnp.where(end, load_own_gamma(0), two_ref[5 * HALO, at, :])

        def halo(y):
            got = [two_ref[HALO * k - 1 - y, at, :] for k in range(5)]
            got[1] = got[1] * sign
            return [jnp.where(end, p, q) for p, q in zip(sweep.get(0), got)]

        def store(y, cons):
            cons[2] = cons[2] * sign
            for f in range(5):
                next_ref[f, pl.ds(y * nx + base, SUB), :] = cons[f]
                windows[f] = into_window(windows[f], y, cons[f])

        sweep = Sweep(SUB, 1, load, load_gamma, halo)
        flux = sweep.run(range(SPLIT), store)
        for y in range(SUB):
            windows[5] = into_window(windows[5], y, load_own_gamma(y))
        for f in range(6):
            window_ref[f, at, :] = windows[f]
        kept = kept_arrays(sweep, flux)
        assert len(kept) == KEPT
        for k in range(KEPT):
            kept_ref[k, at, :] = kept[k]


def second_far(swept_ref, one_ref, part_ref, kept_ref, next_ref, window_ref):
    nx = swept_ref.shape[1] // SUB
    sign = own_sign()
    for base in range(0, nx, SUB):
        at = pl.ds(base, SUB)
        load, load_own_gamma = row_loads(swept_ref, base, nx, sign)
        windows = [part_ref[f, at, :] for f in range(6)]

        def load_gamma(y):
            return load_own_gamma(y) if y < SUB else one_ref[5 * HALO, at, :]

        def halo(y):
            got = [one_ref[HALO * k + y - SUB, at, :] for k in range(5)]
            got[1] = got[1] * sign
            return got

        def store(y, cons):
            cons[2] = cons[2] * sign
            for f in range(5):
                next_ref[f, pl.ds((y - SPLIT) * nx + base, SUB), :] = cons[f]
                windows[f] = into_window(windows[f], y, cons[f])

        kept = [kept_ref[k, at, :] for k in range(KEPT)]
        sweep = Sweep(SUB, 1, load, load_gamma, halo)
        sweep.prim[SPLIT + 1], sweep.prim[SPLIT + 2] = kept[0:5], kept[5:10]
        sweep.diff[SPLIT] = kept[10:15]
        sweep.rise[SPLIT] = (None, kept[15:20])
        sweep.state[SPLIT, True] = (kept[20:25], kept[25:30], kept[30])
        sweep.run(range(SPLIT, SUB), store, kept[31:36])
        for f in range(6):
            window_ref[f, at, :] = windows[f]


def sweep_lanes(cons, gamma, normal):
    def ahead(x):
        return pltpu.roll(x, LANES - 1, 1)

    def behind(x):
        return pltpu.roll(x, 1, 1)

    gam1 = gamma - 1.0
    inv_gam1 = recip(gam1)
    prim = primitives(cons, gam1, normal)
    upper, lower_next = [], []
    for q in prim:
        here = ahead(q) - q
        right = face_rise(behind(here), here, ahead(here))
        left = behind(here - right)
        up, low = edges(q, right, left)
        upper.append(up)
        lower_next.append(ahead(low))
    flux = double_flux(
        state_flux(upper, gamma, inv_gam1),
        state_flux(lower_next, ahead(gamma), ahead(inv_gam1)),
    )
    return updated(cons, flux, [behind(x) for x in flux], normal)


def sweep_window(cons, gamma, normal):
    def turned(x, by):
        return pltpu.roll(x, (LANES - by) % LANES, 1) if by else x

    gam1 = gamma - 1.0
    gam = {k: (turned(gamma, k), turned(recip(gam1), k)) for k in range(-1, 2)}
    states = {key: [] for key in ((-1, 0), (0, 1), (0, 0), (1, 1))}
    for q in primitives(cons, gam1, normal):
        line = {k: turned(q, k) for k in range(-3, 4)}
        diff = {k: line[k + 1] - line[k] for k in range(-3, 3)}
        rise = {k: face_rise(diff[k - 1], diff[k], diff[k + 1]) for k in range(-2, 2)}
        for k, which in states:
            right, left = rise[k], diff[k - 1] - rise[k - 1]
            if which == k + 1:
                states[k, which].append(line[k] + clamp_zero(right, 2.0 * left))
            else:
                states[k, which].append(line[k] - clamp_zero(left, 2.0 * right))
    side = {key: state_flux(prim, *gam[key[0]]) for key, prim in states.items()}
    before = double_flux(side[-1, 0], side[0, 0])
    after = double_flux(side[0, 1], side[1, 1])
    return updated(cons, after, before, normal)


def third_kernel(
    col_axis, cols, near_ref, far_ref, gamma_ref, window_ref, out_ref, left_ref, right_ref
):
    ny = SUB
    nx = window_ref.shape[1]
    col = lax.axis_index(col_axis)
    slot = lax.broadcasted_iota(jnp.int32, (SUB, LANES), 1) % GROUP
    at_first = (slot >= jnp.where(col == 0, 3, GROUP)) & (slot <= 5)
    at_last = (slot >= jnp.where(col == cols - 1, 6, GROUP)) & (slot <= 8)
    for tile in range(nx // SUB):
        base = tile * SUB
        rows = pl.ds(base, SUB)
        for f in range(6):
            own = window_ref[f, rows, :]
            turned = [pltpu.roll(own, by % LANES, 1) for by in (-3, -2, -1, 1, 2, 3)]
            low = jnp.where(slot == 3, turned[0], jnp.where(slot == 4, turned[1], turned[2]))
            high = jnp.where(slot == 6, turned[3], jnp.where(slot == 7, turned[4], turned[5]))
            left_ref[f, rows, :] = jnp.where(at_first, low, own)
            right_ref[f, rows, :] = jnp.where(at_last, high, own)
        for y in range(ny):
            rows_ref, start = (near_ref, y) if y < SPLIT else (far_ref, y - SPLIT)
            cons = [rows_ref[f, pl.ds(start * nx + base, SUB), :] for f in range(5)]
            inner = sweep_lanes(cons, gamma_ref[5, rows_at(y, base, nx), :], 2)
            for f in range(5):
                out_ref[f, pl.ds(base * ny + own_row(y), SUB, stride=ny), :] = inner[f]


def edge_kernel(
    col_axis, cols, inner_ref, left_ref, right_ref, one_ref, two_ref, out_ref, held, sems
):
    nx = left_ref.shape[1]
    ny = SUB
    col = lax.axis_index(col_axis)
    odd = lax.rem(col, 2) == 1
    lane = lax.broadcasted_iota(jnp.int32, (SUB, LANES), 1)
    slot = lane % GROUP
    at_edge = (lane < HALO) | (lane >= LANES - HALO)
    at_left = (slot >= jnp.where(col == 0, GROUP, 3)) & (slot <= 5)
    at_right = (slot >= jnp.where(col == cols - 1, GROUP, 6)) & (slot <= 8)
    edge_new = []
    for tile in range(nx // SUB):
        rows = pl.ds(tile * SUB, SUB)
        left_window, right_window = [], []
        for f in range(6):
            one, two = one_ref[f, rows, :], two_ref[f, rows, :]
            before = jnp.where(odd, one, two)
            after = jnp.where(odd, two, one)
            left_window.append(jnp.where(at_left, before, left_ref[f, rows, :]))
            right_window.append(jnp.where(at_right, after, right_ref[f, rows, :]))
        left_new = sweep_window(left_window[:5], left_window[5], 2)
        right_new = sweep_window(right_window[:5], right_window[5], 2)
        edge_new.append([jnp.where(slot >= 6, a, b) for a, b in zip(left_new, right_new)])
    copies = []
    for f in range(5):
        for tile in range(nx // SUB):
            for y in range(ny):
                turn = (LANES - 6 - GROUP * y) % LANES
                edge = pltpu.roll(edge_new[tile][f], turn, 1)
                at = pl.ds(tile * SUB * ny + own_row(y), SUB, stride=ny)
                held[f, at, :] = jnp.where(at_edge, edge, inner_ref[f, at, :])
        copy = pltpu.make_async_copy(held.at[f], out_ref.at[f], sems.at[f])
        copy.start()
        copies.append(copy)
    for copy in copies:
        copy.wait()


def swap_pairs(mesh, axis, inner):
    rows, cols = mesh.shape["row"], mesh.shape["col"]
    pairs = []
    for r in range(rows):
        for c in range(cols):
            k, n = (r, rows) if axis == "row" else (c, cols)
            if not inner:
                k ^= 1
            elif 0 < k < n - 1:
                k = ((k - 1) ^ 1) + 1
            else:
                k = None
            if axis == "row":
                to = (r, c ^ 1) if k is None else (k, c)
            else:
                to = (r, cols - 1 - c) if k is None else (r, k)
            pairs.append((r * cols + c, to[0] * cols + to[1]))
    return pairs


def body(mesh, state, gamma):
    rows, cols = mesh.shape["row"], mesh.shape["col"]
    _, nx, ny, nz = state.shape
    assert ny == SUB and nz == LANES and nx % SUB == 0 and rows % 2 == 0 and cols % 2 == 0
    here = lambda *dims: pltpu.VMEM(dims, jnp.float32)
    keep = lambda x: pltpu.with_memory_space_constraint(x, pltpu.VMEM)
    near = pl.BlockSpec(memory_space=pltpu.VMEM)
    swap = lambda x, axis, inner: lax.ppermute(x, ("row", "col"), swap_pairs(mesh, axis, inner))

    swept, one, two = pl.pallas_call(
        first_kernel,
        out_shape=(
            here(6, ny * nx, nz),
            here(5 * HALO + 1, nx, nz),
            here(5 * HALO + 1, nx, nz),
        ),
        out_specs=(near,) * 3,
        name="sweep_first",
    )(state, gamma)
    two = swap(two, "row", True)
    one = swap(one, "row", False)
    near_rows, window, kept = pl.pallas_call(
        functools.partial(second_near, rows),
        out_shape=(here(5, SPLIT * nx, nz), here(6, nx, nz), here(KEPT, nx, nz)),
        in_specs=[near] * 2,
        out_specs=(near,) * 3,
        name="second_near",
    )(keep(swept), keep(two))
    far_rows, window = pl.pallas_call(
        second_far,
        out_shape=(here(5, (ny - SPLIT) * nx, nz), here(6, nx, nz)),
        in_specs=[near] * 4,
        out_specs=(near,) * 2,
        name="second_far",
    )(keep(swept), keep(one), keep(window), keep(kept))
    one, two = swap(window, "col", False), swap(window, "col", True)
    inner, left, right = pl.pallas_call(
        functools.partial(third_kernel, "col", cols),
        out_shape=(here(5, nx * ny, nz), here(6, nx, nz), here(6, nx, nz)),
        in_specs=[near] * 4,
        out_specs=(near,) * 3,
        name="sweep_third",
    )(keep(near_rows), keep(far_rows), keep(swept), keep(window))
    out = pl.pallas_call(
        functools.partial(edge_kernel, "col", cols),
        out_shape=jax.ShapeDtypeStruct((5, nx * ny, nz), jnp.float32),
        in_specs=[near] * 5,
        out_specs=pl.BlockSpec(memory_space=pltpu.HBM),
        scratch_shapes=[
            pltpu.VMEM((5, nx * ny, nz), jnp.float32),
            pltpu.SemaphoreType.DMA((5,)),
        ],
        name="third_edges",
    )(keep(inner), keep(left), keep(right), keep(one), keep(two))
    return out.reshape(5, nx, ny, nz)


def solution(mesh):
    in_specs = (P(None, None, "row", "col"), P(None, "row", "col"))
    out_specs = P(None, None, "row", "col")
    return jax.shard_map(
        functools.partial(body, mesh),
        mesh=mesh,
        in_specs=in_specs,
        out_specs=out_specs,
        check_vma=False,
    )
```

time: 13.6 us -> 12.8 us (0.941)
  the two profiles are of different devices: /device:TPU:9 before, /device:TPU:0 now
where the time goes in v5:
time: 12.8 us; the launch traced here: 12.6 us
  starting transfers between devices  6.2 us (48%)
  waiting for transfers between devices  3.21 us (25%)
  Pallas kernels  3.19 us (25%)
    ppermute x4, starting transfers between devices, body(): lax.ppermute(x, ('row', 'col'), swap_pairs(mesh, axis, inner))  6.2 us
    ppermute x4, waiting for transfers between devices, body(): lax.ppermute(x, ('row', 'col'), swap_pairs(mesh, axis, inner))  3.21 us
    pallas_call x1, Pallas kernels, body(): pl.pallas_call(first_kernel, out_shape=(here(6, ny * nx, nz), here(5 * HA...  1.17 us
    pallas_call x1, Pallas kernels, body(): pl.pallas_call(functools.partial(edge_kernel, 'col', cols), out_shape=jax...  0.98 us
    pallas_call x1, Pallas kernels, body(): pl.pallas_call(functools.partial(third_kernel, 'col', cols), out_shape=(h...  0.6 us
    pallas_call x1, Pallas kernels, body(): pl.pallas_call(functools.partial(second_near, rows), out_shape=(here(5, S...  0.28 us
  transfers between devices with their start and end apart: 4, of which 2 were waited for; matrix products, arithmetic and copies ran while one was open for 0% of the time, Pallas kernels for 7%

profile of v5, /device:TPU:0, one launch (start us, length us, event | category | flops | bytes accessed | tf_op | source)
XLA Modules:
  0.0 12.6 jit_solution(18345942571102736599)
XLA Ops:
  0.0 1.2 %sweep_first.1 = (f32[6,64,128]{2,1,0:T(8,128)S(1)}, f32[16,8,128]{2,1,0:T(8,128)S(1)}, f32[16,8,128]{2,1,0:T(8,128)S(1)}) custom-call(f32[5,8,8,128]{3,2,1,0:T(8,128)} %state_ref.1, f32[8,8,128]{2,1,0:T(8,128)} %gamma_ref.1), custom_call_target="tpu_custom_call" | custom-call | tf_op jit(solution)/shard_map/sweep_first/pallas_call | solution.py:439
  1.2 0.5 %collective-permute-start = (f32[16,8,128]{2,1,0:T(8,128)S(1)}, f32[16,8,128]{2,1,0:T(8,128)S(1)}, u32[]{:S(2)}, u32[]{:S(2)}) collective-permute-start(f32[16,8,128]{2,1,0:T(8,128)S(1)} %get-tuple-element.17), channel_id=1, source_target_pairs={{0,1},{1,0},{2,3},{3,2},{4,8},{5,9},{6,10},{7,11},{8,4},{9,5},{10,... | collective-permute-start | bytes 196616 | tf_op jit(solution)/shard_map/ppermute | solution.py:437
  1.7 4.0 %collective-permute-start.1 = (f32[16,8,128]{2,1,0:T(8,128)S(1)}, f32[16,8,128]{2,1,0:T(8,128)S(1)}, u32[]{:S(2)}, u32[]{:S(2)}) collective-permute-start(f32[16,8,128]{2,1,0:T(8,128)S(1)} %get-tuple-element.19), channel_id=1, source_target_pairs={{0,4},{1,5},{2,6},{3,7},{4,0},{5,1},{6,2},{7,3},{8,12},{9,13},{10,... | collective-permute-start | bytes 196616 | tf_op jit(solution)/shard_map/ppermute | solution.py:437
  5.7 0.0 collective-permute-done.two_ref
  5.7 0.3 %second_near.1 = (f32[5,40,128]{2,1,0:T(8,128)S(1)}, f32[6,8,128]{2,1,0:T(8,128)S(1)}, f32[36,8,128]{2,1,0:T(8,128)S(1)}) custom-call(f32[6,64,128]{2,1,0:T(8,128)S(1)} %get-tuple-element.16.swept_ref.gamma_ref, f32[16,8,128]{2,1,0:T(8,128)S(1)} %collective-permute-done.two_ref), custom_call_target="tpu_custom_call" | custom-call | tf_op jit(solution)/shard_map/second_near/pallas_call | solution.py:451
  6.0 2.0 %collective-permute-done.1.one_ref = f32[16,8,128]{2,1,0:T(8,128)S(1)} collective-permute-done((f32[16,8,128]{2,1,0:T(8,128)S(1)}, f32[16,8,128]{2,1,0:T(8,128)S(1)}, u32[]{:S(2)}, u32[]{:S(2)}) %collective-permute-start.1) | collective-permute-done | bytes 65568 | tf_op jit(solution)/shard_map/ppermute | solution.py:437
  8.0 0.2 %second_far.1 = (f32[5,24,128]{2,1,0:T(8,128)S(1)}, f32[6,8,128]{2,1,0:T(8,128)S(1)}) custom-call(f32[6,64,128]{2,1,0:T(8,128)S(1)} %get-tuple-element.16.swept_ref.gamma_ref, f32[16,8,128]{2,1,0:T(8,128)S(1)} %collective-permute-done.1.one_ref, f32[6,8,128]{2,1,0:T(8,128)S(1)} %get-tuple-element.20.part_ref, f32[36,8,128]{2,1,0:T(8,128)S(1)} %get-tuple-element.21.kept_ref), custom_call_target="tpu_custom_call" | custom-call | tf_op jit(solution)/shard_map/second_far/pallas_call | solution.py:458
  8.1 0.4 %collective-permute-start.3 = (f32[6,8,128]{2,1,0:T(8,128)S(1)}, f32[6,8,128]{2,1,0:T(8,128)S(1)}, u32[]{:S(2)}, u32[]{:S(2)}) collective-permute-start(f32[6,8,128]{2,1,0:T(8,128)S(1)} %get-tuple-element.23.window_ref), channel_id=1, source_target_pairs={{0,3},{1,2},{2,1},{3,0},{4,7},{5,6},{6,5},{7,4},{8,11},{9,10},{10,... | collective-permute-start | bytes 73736 | tf_op jit(solution)/shard_map/ppermute | solution.py:437
  8.6 1.2 %collective-permute-start.2 = (f32[6,8,128]{2,1,0:T(8,128)S(1)}, f32[6,8,128]{2,1,0:T(8,128)S(1)}, u32[]{:S(2)}, u32[]{:S(2)}) collective-permute-start(f32[6,8,128]{2,1,0:T(8,128)S(1)} %get-tuple-element.23.window_ref), channel_id=1, source_target_pairs={{0,1},{1,0},{2,3},{3,2},{4,5},{5,4},{6,7},{7,6},{8,9},{9,8},{10,11... | collective-permute-start | bytes 73736 | tf_op jit(solution)/shard_map/ppermute | solution.py:437
  9.8 0.6 %sweep_third.1 = (f32[5,64,128]{2,1,0:T(8,128)S(1)}, f32[6,8,128]{2,1,0:T(8,128)S(1)}, f32[6,8,128]{2,1,0:T(8,128)S(1)}) custom-call(f32[5,40,128]{2,1,0:T(8,128)S(1)} %get-tuple-element.18.near_ref, f32[5,24,128]{2,1,0:T(8,128)S(1)} %get-tuple-element.22.far_ref, f32[6,64,128]{2,1,0:T(8,128)S(1)} %get-tuple-element.16.swept_ref.gamma_ref, ...), custom_call_target="tpu_custom_call" | custom-call | tf_op jit(solution)/shard_map/sweep_third/pallas_call | solution.py:466
  10.4 1.2 %collective-permute-done.3.two_ref = f32[6,8,128]{2,1,0:T(8,128)S(1)} collective-permute-done((f32[6,8,128]{2,1,0:T(8,128)S(1)}, f32[6,8,128]{2,1,0:T(8,128)S(1)}, u32[]{:S(2)}, u32[]{:S(2)}) %collective-permute-start.3) | collective-permute-done | bytes 24608 | tf_op jit(solution)/shard_map/ppermute | solution.py:437
  11.6 0.0 collective-permute-done.2.one_ref
  11.6 1.0 %third_edges.1 = f32[5,64,128]{2,1,0:T(8,128)} custom-call(f32[5,64,128]{2,1,0:T(8,128)S(1)} %get-tuple-element.24.inner_ref, f32[6,8,128]{2,1,0:T(8,128)S(1)} %get-tuple-element.25.left_ref, f32[6,8,128]{2,1,0:T(8,128)S(1)} %get-tuple-element.26.right_ref, f32[6,8,128]{2,1,0:T(8,128)S(1)} %collective-permute-done.2.one_ref, ...), custom_call_target="tpu_custom_call" | custom-call | tf_op jit(solution)/shard_map/third_edges/pallas_call | solution.py:473
Async XLA Ops:
  1.2 4.6 %collective-permute-start = (f32[16,8,128]{2,1,0:T(8,128)S(1)}, f32[16,8,128]{2,1,0:T(8,128)S(1)}, u32[]{:S(2)}, u32[]{:S(2)}) collective-permute-start(f32[16,8,128]{2,1,0:T(8,128)S(1)} %get-tuple-element.17), channel_id=1, source_target_pairs={{0,1},{1,0},{2,3},{3,2},{4,8},{5,9},{6,10},{7,11},{8,4},{9,5},{10,... | collective-permute-start | bytes 196616 | tf_op jit(solution)/shard_map/ppermute | solution.py:437
  1.7 6.3 %collective-permute-start.1 = (f32[16,8,128]{2,1,0:T(8,128)S(1)}, f32[16,8,128]{2,1,0:T(8,128)S(1)}, u32[]{:S(2)}, u32[]{:S(2)}) collective-permute-start(f32[16,8,128]{2,1,0:T(8,128)S(1)} %get-tuple-element.19), channel_id=1, source_target_pairs={{0,4},{1,5},{2,6},{3,7},{4,0},{5,1},{6,2},{7,3},{8,12},{9,13},{10,... | collective-permute-start | bytes 196616 | tf_op jit(solution)/shard_map/ppermute | solution.py:437
  8.1 3.5 %collective-permute-start.3 = (f32[6,8,128]{2,1,0:T(8,128)S(1)}, f32[6,8,128]{2,1,0:T(8,128)S(1)}, u32[]{:S(2)}, u32[]{:S(2)}) collective-permute-start(f32[6,8,128]{2,1,0:T(8,128)S(1)} %get-tuple-element.23.window_ref), channel_id=1, source_target_pairs={{0,3},{1,2},{2,1},{3,0},{4,7},{5,6},{6,5},{7,4},{8,11},{9,10},{10,... | collective-permute-start | bytes 73736 | tf_op jit(solution)/shard_map/ppermute | solution.py:437
  8.6 3.1 %collective-permute-start.2 = (f32[6,8,128]{2,1,0:T(8,128)S(1)}, f32[6,8,128]{2,1,0:T(8,128)S(1)}, u32[]{:S(2)}, u32[]{:S(2)}) collective-permute-start(f32[6,8,128]{2,1,0:T(8,128)S(1)} %get-tuple-element.23.window_ref), channel_id=1, source_target_pairs={{0,1},{1,0},{2,3},{3,2},{4,5},{5,4},{6,7},{7,6},{8,9},{9,8},{10,11... | collective-permute-start | bytes 73736 | tf_op jit(solution)/shard_map/ppermute | solution.py:437

commit v6 on v5

--- a/solution.py
+++ b/solution.py
@@ -209,6 +209,24 @@
     return jnp.where(group == y, rolled, window)
 
 
+class EdgePack:
+    def __init__(self, lower=None, upper=None):
+        self.pack = [lower, upper]
+
+    def add(self, y, cons, gamma):
+        prim = primitives(cons, gamma - 1.0, 2)
+        lane = lax.broadcasted_iota(jnp.int32, (SUB, LANES), 1)
+        rolls = [turned(p, -(GROUP * y + 3 * k + 3)) for k, p in enumerate(prim)]
+        for side in range(2):
+            place = (lane + LANES - 3 * (1 - side)) % LANES
+            slot, group = place % GROUP, place // GROUP
+            value = turned(gamma, -(GROUP * y + (16 if side else 18)))
+            for k in reversed(range(5)):
+                value = jnp.where(slot < 3 * (k + 1), rolls[k], value)
+            old = self.pack[side]
+            self.pack[side] = value if old is None else jnp.where(group == y, value, old)
+
+
 SPLIT = 5
 
 
@@ -221,7 +239,7 @@
 KEPT = 36
 
 
-def second_near(rows, swept_ref, two_ref, next_ref, window_ref, kept_ref):
+def second_near(rows, swept_ref, two_ref, next_ref, lower_ref, upper_ref, kept_ref):
     nx = swept_ref.shape[1] // SUB
     row = lax.axis_index("row")
     end = (row == 0) | (row == rows - 1)
@@ -229,7 +247,7 @@
     for base in range(0, nx, SUB):
         at = pl.ds(base, SUB)
         load, load_own_gamma = row_loads(swept_ref, base, nx, sign)
-        windows = [None] * 6
+        pack = EdgePack()
 
         def load_gamma(y):
             if y >= 0:
@@ -245,27 +263,26 @@
             cons[2] = cons[2] * sign
             for f in range(5):
                 next_ref[f, pl.ds(y * nx + base, SUB), :] = cons[f]
-                windows[f] = into_window(windows[f], y, cons[f])
+            pack.add(y, cons, load_own_gamma(y))
 
         sweep = Sweep(SUB, 1, load, load_gamma, halo)
         flux = sweep.run(range(SPLIT), store)
-        for y in range(SUB):
-            windows[5] = into_window(windows[5], y, load_own_gamma(y))
-        for f in range(6):
-            window_ref[f, at, :] = windows[f]
+        lower_ref[at, :], upper_ref[at, :] = pack.pack
         kept = kept_arrays(sweep, flux)
         assert len(kept) == KEPT
         for k in range(KEPT):
             kept_ref[k, at, :] = kept[k]
 
 
-def second_far(swept_ref, one_ref, part_ref, kept_ref, next_ref, window_ref):
+def second_far(
+    swept_ref, one_ref, lower_ref, upper_ref, kept_ref, next_ref, to_one_ref, to_two_ref
+):
     nx = swept_ref.shape[1] // SUB
     sign = own_sign()
     for base in range(0, nx, SUB):
         at = pl.ds(base, SUB)
         load, load_own_gamma = row_loads(swept_ref, base, nx, sign)
-        windows = [part_ref[f, at, :] for f in range(6)]
+        pack = EdgePack(lower_ref[at, :], upper_ref[at, :])
 
         def load_gamma(y):
             return load_own_gamma(y) if y < SUB else one_ref[5 * HALO, at, :]
@@ -279,7 +296,7 @@
             cons[2] = cons[2] * sign
             for f in range(5):
                 next_ref[f, pl.ds((y - SPLIT) * nx + base, SUB), :] = cons[f]
-                windows[f] = into_window(windows[f], y, cons[f])
+            pack.add(y, cons, load_own_gamma(y))
 
         kept = [kept_ref[k, at, :] for k in range(KEPT)]
         sweep = Sweep(SUB, 1, load, load_gamma, halo)
@@ -288,20 +305,20 @@
         sweep.rise[SPLIT] = (None, kept[15:20])
         sweep.state[SPLIT, True] = (kept[20:25], kept[25:30], kept[30])
         sweep.run(range(SPLIT, SUB), store, kept[31:36])
-        for f in range(6):
-            window_ref[f, at, :] = windows[f]
-
-
-def sweep_lanes(cons, gamma, normal):
+        lower, upper = pack.pack
+        odd = lax.rem(lax.axis_index("col"), 2) == 1
+        to_one_ref[at, :] = jnp.where(odd, lower, upper)
+        to_two_ref[at, :] = jnp.where(odd, upper, lower)
+
+
+def sweep_lanes(cons, prim, gamma, normal):
     def ahead(x):
         return pltpu.roll(x, LANES - 1, 1)
 
     def behind(x):
         return pltpu.roll(x, 1, 1)
 
-    gam1 = gamma - 1.0
-    inv_gam1 = recip(gam1)
-    prim = primitives(cons, gam1, normal)
+    inv_gam1 = recip(gamma - 1.0)
     upper, lower_next = [], []
     for q in prim:
         here = ahead(q) - q
@@ -317,15 +334,10 @@
     return updated(cons, flux, [behind(x) for x in flux], normal)
 
 
-def sweep_window(cons, gamma, normal):
-    def turned(x, by):
-        return pltpu.roll(x, (LANES - by) % LANES, 1) if by else x
-
-    gam1 = gamma - 1.0
-    gam = {k: (turned(gamma, k), turned(recip(gam1), k)) for k in range(-1, 2)}
+def sweep_lines(cons, lines, gammas, normal):
+    gam = {k: (g, recip(g - 1.0)) for k, g in gammas.items()}
     states = {key: [] for key in ((-1, 0), (0, 1), (0, 0), (1, 1))}
-    for q in primitives(cons, gam1, normal):
-        line = {k: turned(q, k) for k in range(-3, 4)}
+    for line in lines:
         diff = {k: line[k + 1] - line[k] for k in range(-3, 3)}
         rise = {k: face_rise(diff[k - 1], diff[k], diff[k + 1]) for k in range(-2, 2)}
         for k, which in states:
@@ -340,64 +352,91 @@
     return updated(cons, after, before, normal)
 
 
-def third_kernel(
-    col_axis, cols, near_ref, far_ref, gamma_ref, window_ref, out_ref, left_ref, right_ref
-):
+def turned(x, by):
+    by %= LANES
+    return pltpu.roll(x, LANES - by, 1) if by else x
+
+
+REACH = range(-HALO, HALO + 1)
+LINES = 5 * len(REACH)
+EDGE_ARRAYS = LINES + 3 + 5
+
+
+def beyond(slot, k, cols):
+    col = lax.axis_index("col")
+    if k < 0:
+        return (slot >= 6) & (slot < 6 - k), col == 0
+    return (slot >= 6 - k) & (slot < 6), col == cols - 1
+
+
+def third_kernel(cols, near_ref, far_ref, gamma_ref, out_ref, edge_ref):
     ny = SUB
-    nx = window_ref.shape[1]
-    col = lax.axis_index(col_axis)
+    nx = edge_ref.shape[1]
     slot = lax.broadcasted_iota(jnp.int32, (SUB, LANES), 1) % GROUP
-    at_first = (slot >= jnp.where(col == 0, 3, GROUP)) & (slot <= 5)
-    at_last = (slot >= jnp.where(col == cols - 1, 6, GROUP)) & (slot <= 8)
-    for tile in range(nx // SUB):
-        base = tile * SUB
-        rows = pl.ds(base, SUB)
-        for f in range(6):
-            own = window_ref[f, rows, :]
-            turned = [pltpu.roll(own, by % LANES, 1) for by in (-3, -2, -1, 1, 2, 3)]
-            low = jnp.where(slot == 3, turned[0], jnp.where(slot == 4, turned[1], turned[2]))
-            high = jnp.where(slot == 6, turned[3], jnp.where(slot == 7, turned[4], turned[5]))
-            left_ref[f, rows, :] = jnp.where(at_first, low, own)
-            right_ref[f, rows, :] = jnp.where(at_last, high, own)
+    for base in range(0, nx, SUB):
+        windows = [None] * 11
         for y in range(ny):
             rows_ref, start = (near_ref, y) if y < SPLIT else (far_ref, y - SPLIT)
             cons = [rows_ref[f, pl.ds(start * nx + base, SUB), :] for f in range(5)]
-            inner = sweep_lanes(cons, gamma_ref[5, rows_at(y, base, nx), :], 2)
+            gamma = gamma_ref[5, rows_at(y, base, nx), :]
+            prim = primitives(cons, gamma - 1.0, 2)
+            for k, value in enumerate(prim + [gamma] + cons):
+                windows[k] = into_window(windows[k], y, value)
+            inner = sweep_lanes(cons, prim, gamma, 2)
             for f in range(5):
                 out_ref[f, pl.ds(base * ny + own_row(y), SUB, stride=ny), :] = inner[f]
-
-
-def edge_kernel(
-    col_axis, cols, inner_ref, left_ref, right_ref, one_ref, two_ref, out_ref, held, sems
-):
-    nx = left_ref.shape[1]
+        at = pl.ds(base, SUB)
+        for q, own in enumerate(windows[:6]):
+            line = {k: turned(own, k) for k in (REACH if q < 5 else (-1, 0, 1))}
+            for n, k in enumerate(line):
+                value = line[k]
+                if k:
+                    where, end = beyond(slot, k, cols)
+                    if abs(k) == 1:
+                        last = own
+                    elif k < 0:
+                        last = jnp.where(slot == 6, own, jnp.where(slot == 7, line[-1], line[-2]))
+                    else:
+                        last = jnp.where(slot == 5, own, jnp.where(slot == 4, line[1], line[2]))
+                    value = jnp.where(where & end, last, value)
+                edge_ref[len(REACH) * q + n, at, :] = value
+        for f in range(5):
+            edge_ref[LINES + 3 + f, at, :] = windows[6 + f]
+
+
+def edge_kernel(cols, inner_ref, edge_ref, one_ref, two_ref, out_ref, held, sems):
+    nx = edge_ref.shape[1]
     ny = SUB
-    col = lax.axis_index(col_axis)
-    odd = lax.rem(col, 2) == 1
+    odd = lax.rem(lax.axis_index("col"), 2) == 1
     lane = lax.broadcasted_iota(jnp.int32, (SUB, LANES), 1)
     slot = lane % GROUP
     at_edge = (lane < HALO) | (lane >= LANES - HALO)
-    at_left = (slot >= jnp.where(col == 0, GROUP, 3)) & (slot <= 5)
-    at_right = (slot >= jnp.where(col == cols - 1, GROUP, 6)) & (slot <= 8)
     edge_new = []
-    for tile in range(nx // SUB):
-        rows = pl.ds(tile * SUB, SUB)
-        left_window, right_window = [], []
-        for f in range(6):
-            one, two = one_ref[f, rows, :], two_ref[f, rows, :]
-            before = jnp.where(odd, one, two)
-            after = jnp.where(odd, two, one)
-            left_window.append(jnp.where(at_left, before, left_ref[f, rows, :]))
-            right_window.append(jnp.where(at_right, after, right_ref[f, rows, :]))
-        left_new = sweep_window(left_window[:5], left_window[5], 2)
-        right_new = sweep_window(right_window[:5], right_window[5], 2)
-        edge_new.append([jnp.where(slot >= 6, a, b) for a, b in zip(left_new, right_new)])
+    for base in range(0, nx, SUB):
+        at = pl.ds(base, SUB)
+        one, two = one_ref[at, :], two_ref[at, :]
+        lower, upper = jnp.where(odd, one, two), jnp.where(odd, two, one)
+
+        def joined(index, k, lane_by):
+            own = edge_ref[index, at, :]
+            if not k:
+                return own
+            where, end = beyond(slot, k, cols)
+            got = turned(lower if k < 0 else upper, lane_by)
+            return jnp.where(where & jnp.logical_not(end), got, own)
+
+        lines = [
+            {k: joined(len(REACH) * q + n, k, 3 * q + k - 3) for n, k in enumerate(REACH)}
+            for q in range(5)
+        ]
+        gammas = {-1: joined(LINES, -1, 9), 0: joined(LINES + 1, 0, 0), 1: joined(LINES + 2, 1, 13)}
+        cons = [edge_ref[LINES + 3 + f, at, :] for f in range(5)]
+        edge_new.append(sweep_lines(cons, lines, gammas, 2))
     copies = []
     for f in range(5):
-        for tile in range(nx // SUB):
+        for tile, new in enumerate(edge_new):
             for y in range(ny):
-                turn = (LANES - 6 - GROUP * y) % LANES
-                edge = pltpu.roll(edge_new[tile][f], turn, 1)
+                edge = turned(new[f], GROUP * y + 6)
                 at = pl.ds(tile * SUB * ny + own_row(y), SUB, stride=ny)
                 held[f, at, :] = jnp.where(at_edge, edge, inner_ref[f, at, :])
         copy = pltpu.make_async_copy(held.at[f], out_ref.at[f], sems.at[f])
@@ -448,39 +487,39 @@
     )(state, gamma)
     two = swap(two, "row", True)
     one = swap(one, "row", False)
-    near_rows, window, kept = pl.pallas_call(
+    near_rows, lower, upper, kept = pl.pallas_call(
         functools.partial(second_near, rows),
-        out_shape=(here(5, SPLIT * nx, nz), here(6, nx, nz), here(KEPT, nx, nz)),
+        out_shape=(here(5, SPLIT * nx, nz), here(nx, nz), here(nx, nz), here(KEPT, nx, nz)),
         in_specs=[near] * 2,
-        out_specs=(near,) * 3,
+        out_specs=(near,) * 4,
         name="second_near",
     )(keep(swept), keep(two))
-    far_rows, window = pl.pallas_call(
+    far_rows, one, two = pl.pallas_call(
         second_far,
-        out_shape=(here(5, (ny - SPLIT) * nx, nz), here(6, nx, nz)),
+        out_shape=(here(5, (ny - SPLIT) * nx, nz), here(nx, nz), here(nx, nz)),
+        in_specs=[near] * 5,
+        out_specs=(near,) * 3,
+        name="second_far",
+    )(keep(swept), keep(one), keep(lower), keep(upper), keep(kept))
+    one, two = swap(one, "col", False), swap(two, "col", True)
+    inner, edge = pl.pallas_call(
+        functools.partial(third_kernel, cols),
+        out_shape=(here(5, nx * ny, nz), here(EDGE_ARRAYS, nx, nz)),
+        in_specs=[near] * 3,
+        out_specs=(near,) * 2,
+        name="sweep_third",
+    )(keep(near_rows), keep(far_rows), keep(swept))
+    out = pl.pallas_call(
+        functools.partial(edge_kernel, cols),
+        out_shape=jax.ShapeDtypeStruct((5, nx * ny, nz), jnp.float32),
         in_specs=[near] * 4,
-        out_specs=(near,) * 2,
-        name="second_far",
-    )(keep(swept), keep(one), keep(window), keep(kept))
-    one, two = swap(window, "col", False), swap(window, "col", True)
-    inner, left, right = pl.pallas_call(
-        functools.partial(third_kernel, "col", cols),
-        out_shape=(here(5, nx * ny, nz), here(6, nx, nz), here(6, nx, nz)),
-        in_specs=[near] * 4,
-        out_specs=(near,) * 3,
-        name="sweep_third",
-    )(keep(near_rows), keep(far_rows), keep(swept), keep(window))
-    out = pl.pallas_call(
-        functools.partial(edge_kernel, "col", cols),
-        out_shape=jax.ShapeDtypeStruct((5, nx * ny, nz), jnp.float32),
-        in_specs=[near] * 5,
         out_specs=pl.BlockSpec(memory_space=pltpu.HBM),
         scratch_shapes=[
             pltpu.VMEM((5, nx * ny, nz), jnp.float32),
             pltpu.SemaphoreType.DMA((5,)),
         ],
         name="third_edges",
-    )(keep(inner), keep(left), keep(right), keep(one), keep(two))
+    )(keep(inner), keep(edge), keep(one), keep(two))
     return out.reshape(5, nx, ny, nz)
 
 

time: 12.8 us -> 12.4 us (0.969)
  waiting for transfers between devices: 3.21 us -> 2.06 us
  Pallas kernels: 3.19 us -> 3.91 us
    ppermute x4, waiting for transfers between devices: 3.21 us -> 2.06 us  [body(): lax.ppermute(x, ('row', 'col'), swap_pairs(mesh, axis, inner))]
    pallas_call x2, Pallas kernels: 1.58 us -> 2.28 us  [the longest x1 1.35 us: body(): pl.pallas_call(functools.partial(third_kernel, cols), out_shape=(here(5,...]
  transfers between devices with their start and end apart: 4 -> 4, of which waited for: 2 -> 2; matrix products, arithmetic and copies ran while one was open for 0% -> 0% of each run, Pallas kernels for 7% -> 14%
where the time goes in v6:
time: 12.4 us; the launch traced here: 12.2 us
  starting transfers between devices  6.23 us (50%)
  Pallas kernels  3.91 us (32%)
  waiting for transfers between devices  2.06 us (17%)
    ppermute x4, starting transfers between devices, body(): lax.ppermute(x, ('row', 'col'), swap_pairs(mesh, axis, inner))  6.23 us
    ppermute x4, waiting for transfers between devices, body(): lax.ppermute(x, ('row', 'col'), swap_pairs(mesh, axis, inner))  2.06 us
    pallas_call x1, Pallas kernels, body(): pl.pallas_call(functools.partial(third_kernel, cols), out_shape=(here(5,...  1.35 us
    pallas_call x1, Pallas kernels, body(): pl.pallas_call(first_kernel, out_shape=(here(6, ny * nx, nz), here(5 * HA...  1.17 us
    pallas_call x1, Pallas kernels, body(): pl.pallas_call(functools.partial(edge_kernel, cols), out_shape=jax.ShapeD...  0.94 us
    pallas_call x1, Pallas kernels, body(): pl.pallas_call(functools.partial(second_near, rows), out_shape=(here(5, S...  0.3 us
  transfers between devices with their start and end apart: 4, of which 2 were waited for; matrix products, arithmetic and copies ran while one was open for 0% of the time, Pallas kernels for 14%

profile of v6, /device:TPU:0, one launch (start us, length us, event | category | flops | bytes accessed | tf_op | source)
XLA Modules:
  0.0 12.2 jit_solution(13589350430799907283)
XLA Ops:
  0.0 1.2 %sweep_first.1 = (f32[6,64,128]{2,1,0:T(8,128)S(1)}, f32[16,8,128]{2,1,0:T(8,128)S(1)}, f32[16,8,128]{2,1,0:T(8,128)S(1)}) custom-call(f32[5,8,8,128]{3,2,1,0:T(8,128)} %state_ref.1, f32[8,8,128]{2,1,0:T(8,128)} %gamma_ref.1), custom_call_target="tpu_custom_call" | custom-call | tf_op jit(solution)/shard_map/sweep_first/pallas_call | solution.py:478
  1.2 0.5 %collective-permute-start = (f32[16,8,128]{2,1,0:T(8,128)S(1)}, f32[16,8,128]{2,1,0:T(8,128)S(1)}, u32[]{:S(2)}, u32[]{:S(2)}) collective-permute-start(f32[16,8,128]{2,1,0:T(8,128)S(1)} %get-tuple-element.18), channel_id=1, source_target_pairs={{0,1},{1,0},{2,3},{3,2},{4,8},{5,9},{6,10},{7,11},{8,4},{9,5},{10,... | collective-permute-start | bytes 196616 | tf_op jit(solution)/shard_map/ppermute | solution.py:476
  1.7 4.0 %collective-permute-start.1 = (f32[16,8,128]{2,1,0:T(8,128)S(1)}, f32[16,8,128]{2,1,0:T(8,128)S(1)}, u32[]{:S(2)}, u32[]{:S(2)}) collective-permute-start(f32[16,8,128]{2,1,0:T(8,128)S(1)} %get-tuple-element.20), channel_id=1, source_target_pairs={{0,4},{1,5},{2,6},{3,7},{4,0},{5,1},{6,2},{7,3},{8,12},{9,13},{10,... | collective-permute-start | bytes 196616 | tf_op jit(solution)/shard_map/ppermute | solution.py:476
  5.7 0.0 collective-permute-done.two_ref
  5.7 0.3 %second_near.1 = (f32[5,40,128]{2,1,0:T(8,128)S(1)}, f32[8,128]{1,0:T(8,128)S(1)}, f32[8,128]{1,0:T(8,128)S(1)}, f32[36,8,128]{2,1,0:T(8,128)S(1)}) custom-call(f32[6,64,128]{2,1,0:T(8,128)S(1)} %get-tuple-element.17.swept_ref.gamma_ref, f32[16,8,128]{2,1,0:T(8,128)S(1)} %collective-permute-done.two_ref), custom_call_target="tpu_custom_call" | custom-call | tf_op jit(solution)/shard_map/second_near/pallas_call | solution.py:490
  6.0 1.9 %collective-permute-done.1.one_ref = f32[16,8,128]{2,1,0:T(8,128)S(1)} collective-permute-done((f32[16,8,128]{2,1,0:T(8,128)S(1)}, f32[16,8,128]{2,1,0:T(8,128)S(1)}, u32[]{:S(2)}, u32[]{:S(2)}) %collective-permute-start.1) | collective-permute-done | bytes 65568 | tf_op jit(solution)/shard_map/ppermute | solution.py:476
  8.0 0.2 %second_far.1 = (f32[5,24,128]{2,1,0:T(8,128)S(1)}, f32[8,128]{1,0:T(8,128)S(1)}, f32[8,128]{1,0:T(8,128)S(1)}) custom-call(f32[6,64,128]{2,1,0:T(8,128)S(1)} %get-tuple-element.17.swept_ref.gamma_ref, f32[16,8,128]{2,1,0:T(8,128)S(1)} %collective-permute-done.1.one_ref, f32[8,128]{1,0:T(8,128)S(1)} %get-tuple-element.21.lower_ref, ...), custom_call_target="tpu_custom_call" | custom-call | tf_op jit(solution)/shard_map/second_far/pallas_call | solution.py:497
  8.1 0.1 collective-permute-start.2
  8.2 1.6 %collective-permute-start.3 = (f32[8,128]{1,0:T(8,128)S(1)}, f32[8,128]{1,0:T(8,128)S(1)}, u32[]{:S(2)}, u32[]{:S(2)}) collective-permute-start(f32[8,128]{1,0:T(8,128)S(1)} %get-tuple-element.28), channel_id=1, source_target_pairs={{0,3},{1,2},{2,1},{3,0},{4,7},{5,6},{6,5},{7,4},{8,11},{9,10},{10,... | collective-permute-start | bytes 12296 | tf_op jit(solution)/shard_map/ppermute | solution.py:476
  9.8 1.3 %sweep_third.1 = (f32[5,64,128]{2,1,0:T(8,128)S(1)}, f32[43,8,128]{2,1,0:T(8,128)S(1)}) custom-call(f32[5,40,128]{2,1,0:T(8,128)S(1)} %get-tuple-element.19.near_ref, f32[5,24,128]{2,1,0:T(8,128)S(1)} %get-tuple-element.24.far_ref, f32[6,64,128]{2,1,0:T(8,128)S(1)} %get-tuple-element.17.swept_ref.gamma_ref), custom_call_target="tpu_custom_call" | custom-call | tf_op jit(solution)/shard_map/sweep_third/pallas_call | solution.py:505
  11.2 0.0 collective-permute-done.2.one_ref
  11.2 0.1 %collective-permute-done.3.two_ref = f32[8,128]{1,0:T(8,128)S(1)} collective-permute-done((f32[8,128]{1,0:T(8,128)S(1)}, f32[8,128]{1,0:T(8,128)S(1)}, u32[]{:S(2)}, u32[]{:S(2)}) %collective-permute-start.3) | collective-permute-done | bytes 4128 | tf_op jit(solution)/shard_map/ppermute | solution.py:476
  11.3 0.9 %third_edges.1 = f32[5,64,128]{2,1,0:T(8,128)} custom-call(f32[5,64,128]{2,1,0:T(8,128)S(1)} %get-tuple-element.25.inner_ref, f32[43,8,128]{2,1,0:T(8,128)S(1)} %get-tuple-element.26.edge_ref, f32[8,128]{1,0:T(8,128)S(1)} %collective-permute-done.2.one_ref, f32[8,128]{1,0:T(8,128)S(1)} %collective-permute-done.3.two_ref), custom_call_target="tpu_custom_call" | custom-call | tf_op jit(solution)/shard_map/third_edges/pallas_call | solution.py:512
Async XLA Ops:
  1.2 4.6 %collective-permute-start = (f32[16,8,128]{2,1,0:T(8,128)S(1)}, f32[16,8,128]{2,1,0:T(8,128)S(1)}, u32[]{:S(2)}, u32[]{:S(2)}) collective-permute-start(f32[16,8,128]{2,1,0:T(8,128)S(1)} %get-tuple-element.18), channel_id=1, source_target_pairs={{0,1},{1,0},{2,3},{3,2},{4,8},{5,9},{6,10},{7,11},{8,4},{9,5},{10,... | collective-permute-start | bytes 196616 | tf_op jit(solution)/shard_map/ppermute | solution.py:476
  1.7 6.3 %collective-permute-start.1 = (f32[16,8,128]{2,1,0:T(8,128)S(1)}, f32[16,8,128]{2,1,0:T(8,128)S(1)}, u32[]{:S(2)}, u32[]{:S(2)}) collective-permute-start(f32[16,8,128]{2,1,0:T(8,128)S(1)} %get-tuple-element.20), channel_id=1, source_target_pairs={{0,4},{1,5},{2,6},{3,7},{4,0},{5,1},{6,2},{7,3},{8,12},{9,13},{10,... | collective-permute-start | bytes 196616 | tf_op jit(solution)/shard_map/ppermute | solution.py:476
  8.1 3.0 %collective-permute-start.2 = (f32[8,128]{1,0:T(8,128)S(1)}, f32[8,128]{1,0:T(8,128)S(1)}, u32[]{:S(2)}, u32[]{:S(2)}) collective-permute-start(f32[8,128]{1,0:T(8,128)S(1)} %get-tuple-element.27), channel_id=1, source_target_pairs={{0,1},{1,0},{2,3},{3,2},{4,5},{5,4},{6,7},{7,6},{8,9},{9,8},{10,11... | collective-permute-start | bytes 12296 | tf_op jit(solution)/shard_map/ppermute | solution.py:476
  8.2 3.1 %collective-permute-start.3 = (f32[8,128]{1,0:T(8,128)S(1)}, f32[8,128]{1,0:T(8,128)S(1)}, u32[]{:S(2)}, u32[]{:S(2)}) collective-permute-start(f32[8,128]{1,0:T(8,128)S(1)} %get-tuple-element.28), channel_id=1, source_target_pairs={{0,3},{1,2},{2,1},{3,0},{4,7},{5,6},{6,5},{7,4},{8,11},{9,10},{10,... | collective-permute-start | bytes 12296 | tf_op jit(solution)/shard_map/ppermute | solution.py:476

commit v7 on v6

--- a/solution.py
+++ b/solution.py
@@ -404,7 +404,7 @@
             edge_ref[LINES + 3 + f, at, :] = windows[6 + f]
 
 
-def edge_kernel(cols, inner_ref, edge_ref, one_ref, two_ref, out_ref, held, sems):
+def edge_kernel(cols, inner_ref, edge_ref, two_ref, one_ref, out_ref, held, sems):
     nx = edge_ref.shape[1]
     ny = SUB
     odd = lax.rem(lax.axis_index("col"), 2) == 1
@@ -501,7 +501,8 @@
         out_specs=(near,) * 3,
         name="second_far",
     )(keep(swept), keep(one), keep(lower), keep(upper), keep(kept))
-    one, two = swap(one, "col", False), swap(two, "col", True)
+    two = swap(two, "col", True)
+    one = swap(one, "col", False)
     inner, edge = pl.pallas_call(
         functools.partial(third_kernel, cols),
         out_shape=(here(5, nx * ny, nz), here(EDGE_ARRAYS, nx, nz)),
@@ -519,7 +520,7 @@
             pltpu.SemaphoreType.DMA((5,)),
         ],
         name="third_edges",
-    )(keep(inner), keep(edge), keep(one), keep(two))
+    )(keep(inner), keep(edge), keep(two), keep(one))
     return out.reshape(5, nx, ny, nz)
 
 

time: 12.4 us -> 12.3 us (level)
  no operation moved by 1% of the time
where the time goes in v7:
time: 12.3 us; the launch traced here: 12.2 us
  starting transfers between devices  6.22 us (51%)
  Pallas kernels  3.91 us (32%)
  waiting for transfers between devices  2.01 us (16%)
    ppermute x4, starting transfers between devices, body(): lax.ppermute(x, ('row', 'col'), swap_pairs(mesh, axis, inner))  6.22 us
    ppermute x4, waiting for transfers between devices, body(): lax.ppermute(x, ('row', 'col'), swap_pairs(mesh, axis, inner))  2.01 us
    pallas_call x1, Pallas kernels, body(): pl.pallas_call(functools.partial(third_kernel, cols), out_shape=(here(5,...  1.35 us
    pallas_call x1, Pallas kernels, body(): pl.pallas_call(first_kernel, out_shape=(here(6, ny * nx, nz), here(5 * HA...  1.17 us
    pallas_call x1, Pallas kernels, body(): pl.pallas_call(functools.partial(edge_kernel, cols), out_shape=jax.ShapeD...  0.94 us
    pallas_call x1, Pallas kernels, body(): pl.pallas_call(functools.partial(second_near, rows), out_shape=(here(5, S...  0.3 us
  transfers between devices with their start and end apart: 4, of which 2 were waited for; matrix products, arithmetic and copies ran while one was open for 0% of the time, Pallas kernels for 14%

profile of v7, /device:TPU:0, one launch (start us, length us, event | category | flops | bytes accessed | tf_op | source)
XLA Modules:
  0.0 12.2 jit_solution(5295229395040209941)
XLA Ops:
  0.0 1.2 %sweep_first.1 = (f32[6,64,128]{2,1,0:T(8,128)S(1)}, f32[16,8,128]{2,1,0:T(8,128)S(1)}, f32[16,8,128]{2,1,0:T(8,128)S(1)}) custom-call(f32[5,8,8,128]{3,2,1,0:T(8,128)} %state_ref.1, f32[8,8,128]{2,1,0:T(8,128)} %gamma_ref.1), custom_call_target="tpu_custom_call" | custom-call | tf_op jit(solution)/shard_map/sweep_first/pallas_call | solution.py:478
  1.2 0.5 %collective-permute-start = (f32[16,8,128]{2,1,0:T(8,128)S(1)}, f32[16,8,128]{2,1,0:T(8,128)S(1)}, u32[]{:S(2)}, u32[]{:S(2)}) collective-permute-start(f32[16,8,128]{2,1,0:T(8,128)S(1)} %get-tuple-element.18), channel_id=1, source_target_pairs={{0,1},{1,0},{2,3},{3,2},{4,8},{5,9},{6,10},{7,11},{8,4},{9,5},{10,... | collective-permute-start | bytes 196616 | tf_op jit(solution)/shard_map/ppermute | solution.py:476
  1.7 4.0 %collective-permute-start.1 = (f32[16,8,128]{2,1,0:T(8,128)S(1)}, f32[16,8,128]{2,1,0:T(8,128)S(1)}, u32[]{:S(2)}, u32[]{:S(2)}) collective-permute-start(f32[16,8,128]{2,1,0:T(8,128)S(1)} %get-tuple-element.20), channel_id=1, source_target_pairs={{0,4},{1,5},{2,6},{3,7},{4,0},{5,1},{6,2},{7,3},{8,12},{9,13},{10,... | collective-permute-start | bytes 196616 | tf_op jit(solution)/shard_map/ppermute | solution.py:476
  5.7 0.0 collective-permute-done.two_ref
  5.7 0.3 %second_near.1 = (f32[5,40,128]{2,1,0:T(8,128)S(1)}, f32[8,128]{1,0:T(8,128)S(1)}, f32[8,128]{1,0:T(8,128)S(1)}, f32[36,8,128]{2,1,0:T(8,128)S(1)}) custom-call(f32[6,64,128]{2,1,0:T(8,128)S(1)} %get-tuple-element.17.swept_ref.gamma_ref, f32[16,8,128]{2,1,0:T(8,128)S(1)} %collective-permute-done.two_ref), custom_call_target="tpu_custom_call" | custom-call | tf_op jit(solution)/shard_map/second_near/pallas_call | solution.py:490
  6.0 1.9 %collective-permute-done.1.one_ref = f32[16,8,128]{2,1,0:T(8,128)S(1)} collective-permute-done((f32[16,8,128]{2,1,0:T(8,128)S(1)}, f32[16,8,128]{2,1,0:T(8,128)S(1)}, u32[]{:S(2)}, u32[]{:S(2)}) %collective-permute-start.1) | collective-permute-done | bytes 65568 | tf_op jit(solution)/shard_map/ppermute | solution.py:476
  8.0 0.2 %second_far.1 = (f32[5,24,128]{2,1,0:T(8,128)S(1)}, f32[8,128]{1,0:T(8,128)S(1)}, f32[8,128]{1,0:T(8,128)S(1)}) custom-call(f32[6,64,128]{2,1,0:T(8,128)S(1)} %get-tuple-element.17.swept_ref.gamma_ref, f32[16,8,128]{2,1,0:T(8,128)S(1)} %collective-permute-done.1.one_ref, f32[8,128]{1,0:T(8,128)S(1)} %get-tuple-element.21.lower_ref, ...), custom_call_target="tpu_custom_call" | custom-call | tf_op jit(solution)/shard_map/second_far/pallas_call | solution.py:497
  8.1 0.5 %collective-permute-start.2 = (f32[8,128]{1,0:T(8,128)S(1)}, f32[8,128]{1,0:T(8,128)S(1)}, u32[]{:S(2)}, u32[]{:S(2)}) collective-permute-start(f32[8,128]{1,0:T(8,128)S(1)} %get-tuple-element.27), channel_id=1, source_target_pairs={{0,3},{1,2},{2,1},{3,0},{4,7},{5,6},{6,5},{7,4},{8,11},{9,10},{10,... | collective-permute-start | bytes 12296 | tf_op jit(solution)/shard_map/ppermute | solution.py:476
  8.6 1.2 %collective-permute-start.3 = (f32[8,128]{1,0:T(8,128)S(1)}, f32[8,128]{1,0:T(8,128)S(1)}, u32[]{:S(2)}, u32[]{:S(2)}) collective-permute-start(f32[8,128]{1,0:T(8,128)S(1)} %get-tuple-element.28), channel_id=1, source_target_pairs={{0,1},{1,0},{2,3},{3,2},{4,5},{5,4},{6,7},{7,6},{8,9},{9,8},{10,11... | collective-permute-start | bytes 12296 | tf_op jit(solution)/shard_map/ppermute | solution.py:476
  9.8 1.3 %sweep_third.1 = (f32[5,64,128]{2,1,0:T(8,128)S(1)}, f32[43,8,128]{2,1,0:T(8,128)S(1)}) custom-call(f32[5,40,128]{2,1,0:T(8,128)S(1)} %get-tuple-element.19.near_ref, f32[5,24,128]{2,1,0:T(8,128)S(1)} %get-tuple-element.24.far_ref, f32[6,64,128]{2,1,0:T(8,128)S(1)} %get-tuple-element.17.swept_ref.gamma_ref), custom_call_target="tpu_custom_call" | custom-call | tf_op jit(solution)/shard_map/sweep_third/pallas_call | solution.py:506
  11.2 0.1 collective-permute-done.2.two_ref
  11.2 0.0 collective-permute-done.3.one_ref
  11.2 0.9 %third_edges.1 = f32[5,64,128]{2,1,0:T(8,128)} custom-call(f32[5,64,128]{2,1,0:T(8,128)S(1)} %get-tuple-element.25.inner_ref, f32[43,8,128]{2,1,0:T(8,128)S(1)} %get-tuple-element.26.edge_ref, f32[8,128]{1,0:T(8,128)S(1)} %collective-permute-done.2.two_ref, f32[8,128]{1,0:T(8,128)S(1)} %collective-permute-done.3.one_ref), custom_call_target="tpu_custom_call" | custom-call | tf_op jit(solution)/shard_map/third_edges/pallas_call | solution.py:513
Async XLA Ops:
  1.2 4.6 %collective-permute-start = (f32[16,8,128]{2,1,0:T(8,128)S(1)}, f32[16,8,128]{2,1,0:T(8,128)S(1)}, u32[]{:S(2)}, u32[]{:S(2)}) collective-permute-start(f32[16,8,128]{2,1,0:T(8,128)S(1)} %get-tuple-element.18), channel_id=1, source_target_pairs={{0,1},{1,0},{2,3},{3,2},{4,8},{5,9},{6,10},{7,11},{8,4},{9,5},{10,... | collective-permute-start | bytes 196616 | tf_op jit(solution)/shard_map/ppermute | solution.py:476
  1.7 6.3 %collective-permute-start.1 = (f32[16,8,128]{2,1,0:T(8,128)S(1)}, f32[16,8,128]{2,1,0:T(8,128)S(1)}, u32[]{:S(2)}, u32[]{:S(2)}) collective-permute-start(f32[16,8,128]{2,1,0:T(8,128)S(1)} %get-tuple-element.20), channel_id=1, source_target_pairs={{0,4},{1,5},{2,6},{3,7},{4,0},{5,1},{6,2},{7,3},{8,12},{9,13},{10,... | collective-permute-start | bytes 196616 | tf_op jit(solution)/shard_map/ppermute | solution.py:476
  8.1 3.1 %collective-permute-start.2 = (f32[8,128]{1,0:T(8,128)S(1)}, f32[8,128]{1,0:T(8,128)S(1)}, u32[]{:S(2)}, u32[]{:S(2)}) collective-permute-start(f32[8,128]{1,0:T(8,128)S(1)} %get-tuple-element.27), channel_id=1, source_target_pairs={{0,3},{1,2},{2,1},{3,0},{4,7},{5,6},{6,5},{7,4},{8,11},{9,10},{10,... | collective-permute-start | bytes 12296 | tf_op jit(solution)/shard_map/ppermute | solution.py:476
  8.6 2.6 %collective-permute-start.3 = (f32[8,128]{1,0:T(8,128)S(1)}, f32[8,128]{1,0:T(8,128)S(1)}, u32[]{:S(2)}, u32[]{:S(2)}) collective-permute-start(f32[8,128]{1,0:T(8,128)S(1)} %get-tuple-element.28), channel_id=1, source_target_pairs={{0,1},{1,0},{2,3},{3,2},{4,5},{5,4},{6,7},{7,6},{8,9},{9,8},{10,11... | collective-permute-start | bytes 12296 | tf_op jit(solution)/shard_map/ppermute | solution.py:476

commit v8 on v7

--- a/solution.py
+++ b/solution.py
@@ -10,7 +10,8 @@
 STEP = 0.08
 HALO = 3
 SUB, LANES = 8, 128
-GROUP = LANES // SUB
+GROUP_BITS = 4
+GROUP = 1 << GROUP_BITS
 
 
 def recip(x):
@@ -166,8 +167,16 @@
     return pl.ds(pl.multiple_of(own_row(y) * nx + base, SUB), SUB)
 
 
-def first_kernel(state_ref, gamma_ref, swept_ref, one_ref, two_ref):
+def first_kernel(state_hbm, gamma_hbm, swept_ref, one_ref, two_ref, state_ref, gamma_ref, sems):
     nx, ny = gamma_ref.shape[0], gamma_ref.shape[1]
+    copies = [
+        pltpu.make_async_copy(state_hbm.at[f], state_ref.at[f], sems.at[f]) for f in range(5)
+    ]
+    copies.append(pltpu.make_async_copy(gamma_hbm, gamma_ref, sems.at[5]))
+    for f, copy in enumerate(copies):
+        copy.start(priority=f % 2)
+    for copy in copies:
+        copy.wait()
 
     def store(x, cons):
         for f in range(5):
@@ -200,13 +209,24 @@
     return load, lambda y: swept_ref[5, rows_at(y, base, nx), :]
 
 
+def lanes():
+    return lax.broadcasted_iota(jnp.int32, (SUB, LANES), 1)
+
+
+def groups(by=0):
+    return ((lanes() - by) & (LANES - 1)) >> GROUP_BITS
+
+
+def slots(by=0):
+    return (lanes() - by) & (GROUP - 1)
+
+
 def into_window(window, y, value):
     turn = (GROUP * y + 6) % LANES
     rolled = pltpu.roll(value, turn, 1) if turn else value
     if window is None:
         return rolled
-    group = lax.broadcasted_iota(jnp.int32, (SUB, LANES), 1) // GROUP
-    return jnp.where(group == y, rolled, window)
+    return jnp.where(groups() == y, rolled, window)
 
 
 class EdgePack:
@@ -215,11 +235,9 @@
 
     def add(self, y, cons, gamma):
         prim = primitives(cons, gamma - 1.0, 2)
-        lane = lax.broadcasted_iota(jnp.int32, (SUB, LANES), 1)
         rolls = [turned(p, -(GROUP * y + 3 * k + 3)) for k, p in enumerate(prim)]
         for side in range(2):
-            place = (lane + LANES - 3 * (1 - side)) % LANES
-            slot, group = place % GROUP, place // GROUP
+            slot, group = slots(3 * (1 - side)), groups(3 * (1 - side))
             value = turned(gamma, -(GROUP * y + (16 if side else 18)))
             for k in reversed(range(5)):
                 value = jnp.where(slot < 3 * (k + 1), rolls[k], value)
@@ -309,6 +327,7 @@
         odd = lax.rem(lax.axis_index("col"), 2) == 1
         to_one_ref[at, :] = jnp.where(odd, lower, upper)
         to_two_ref[at, :] = jnp.where(odd, upper, lower)
+        to_two_ref[pl.ds(nx + base, SUB), :] = lower
 
 
 def sweep_lanes(cons, prim, gamma, normal):
@@ -369,22 +388,37 @@
     return (slot >= 6 - k) & (slot < 6), col == cols - 1
 
 
-def third_kernel(cols, near_ref, far_ref, gamma_ref, out_ref, edge_ref):
+def zone_loads(near_ref, far_ref, gamma_ref, base, nx):
+    def load(y):
+        rows_ref, start = (near_ref, y) if y < SPLIT else (far_ref, y - SPLIT)
+        cons = [rows_ref[f, pl.ds(start * nx + base, SUB), :] for f in range(5)]
+        gamma = gamma_ref[5, rows_at(y, base, nx), :]
+        return cons, primitives(cons, gamma - 1.0, 2), gamma
+
+    return load
+
+
+def third_kernel(near_ref, far_ref, gamma_ref, out_ref):
     ny = SUB
+    nx = out_ref.shape[1] // ny
+    for base in range(0, nx, SUB):
+        load = zone_loads(near_ref, far_ref, gamma_ref, base, nx)
+        for y in range(ny):
+            inner = sweep_lanes(*load(y), 2)
+            for f in range(5):
+                out_ref[f, pl.ds(base * ny + own_row(y), SUB, stride=ny), :] = inner[f]
+
+
+def window_kernel(cols, near_ref, far_ref, gamma_ref, edge_ref):
     nx = edge_ref.shape[1]
-    slot = lax.broadcasted_iota(jnp.int32, (SUB, LANES), 1) % GROUP
+    slot = slots()
     for base in range(0, nx, SUB):
+        load = zone_loads(near_ref, far_ref, gamma_ref, base, nx)
         windows = [None] * 11
-        for y in range(ny):
-            rows_ref, start = (near_ref, y) if y < SPLIT else (far_ref, y - SPLIT)
-            cons = [rows_ref[f, pl.ds(start * nx + base, SUB), :] for f in range(5)]
-            gamma = gamma_ref[5, rows_at(y, base, nx), :]
-            prim = primitives(cons, gamma - 1.0, 2)
+        for y in range(SUB):
+            cons, prim, gamma = load(y)
             for k, value in enumerate(prim + [gamma] + cons):
                 windows[k] = into_window(windows[k], y, value)
-            inner = sweep_lanes(cons, prim, gamma, 2)
-            for f in range(5):
-                out_ref[f, pl.ds(base * ny + own_row(y), SUB, stride=ny), :] = inner[f]
         at = pl.ds(base, SUB)
         for q, own in enumerate(windows[:6]):
             line = {k: turned(own, k) for k in (REACH if q < 5 else (-1, 0, 1))}
@@ -404,12 +438,12 @@
             edge_ref[LINES + 3 + f, at, :] = windows[6 + f]
 
 
-def edge_kernel(cols, inner_ref, edge_ref, two_ref, one_ref, out_ref, held, sems):
+def mend_edges(cols, inner_ref, edge_ref, one_ref, two_ref, out_ref, held, sems):
     nx = edge_ref.shape[1]
     ny = SUB
     odd = lax.rem(lax.axis_index("col"), 2) == 1
-    lane = lax.broadcasted_iota(jnp.int32, (SUB, LANES), 1)
-    slot = lane % GROUP
+    lane = lanes()
+    slot = slots()
     at_edge = (lane < HALO) | (lane >= LANES - HALO)
     edge_new = []
     for base in range(0, nx, SUB):
@@ -440,10 +474,27 @@
                 at = pl.ds(tile * SUB * ny + own_row(y), SUB, stride=ny)
                 held[f, at, :] = jnp.where(at_edge, edge, inner_ref[f, at, :])
         copy = pltpu.make_async_copy(held.at[f], out_ref.at[f], sems.at[f])
-        copy.start()
+        copy.start(priority=f % 2)
         copies.append(copy)
     for copy in copies:
         copy.wait()
+
+
+def at_end(cols):
+    col = lax.axis_index("col")
+    return (col == 0) | (col == cols - 1)
+
+
+def end_kernel(cols, inner_ref, edge_ref, one_ref, out_ref, held, sems):
+    @pl.when(at_end(cols))
+    def _():
+        mend_edges(cols, inner_ref, edge_ref, one_ref, one_ref, out_ref, held, sems)
+
+
+def middle_kernel(cols, ends_ref, inner_ref, edge_ref, one_ref, two_ref, out_ref, held, sems):
+    @pl.when(jnp.logical_not(at_end(cols)))
+    def _():
+        mend_edges(cols, inner_ref, edge_ref, one_ref, two_ref, out_ref, held, sems)
 
 
 def swap_pairs(mesh, axis, inner):
@@ -482,7 +533,13 @@
             here(5 * HALO + 1, nx, nz),
             here(5 * HALO + 1, nx, nz),
         ),
+        in_specs=[pl.BlockSpec(memory_space=pltpu.HBM)] * 2,
         out_specs=(near,) * 3,
+        scratch_shapes=[
+            pltpu.VMEM(state.shape, jnp.float32),
+            pltpu.VMEM(gamma.shape, jnp.float32),
+            pltpu.SemaphoreType.DMA((6,)),
+        ],
         name="sweep_first",
     )(state, gamma)
     two = swap(two, "row", True)
@@ -496,31 +553,48 @@
     )(keep(swept), keep(two))
     far_rows, one, two = pl.pallas_call(
         second_far,
-        out_shape=(here(5, (ny - SPLIT) * nx, nz), here(nx, nz), here(nx, nz)),
+        out_shape=(here(5, (ny - SPLIT) * nx, nz), here(nx, nz), here(2 * nx, nz)),
         in_specs=[near] * 5,
         out_specs=(near,) * 3,
         name="second_far",
     )(keep(swept), keep(one), keep(lower), keep(upper), keep(kept))
     two = swap(two, "col", True)
     one = swap(one, "col", False)
-    inner, edge = pl.pallas_call(
-        functools.partial(third_kernel, cols),
-        out_shape=(here(5, nx * ny, nz), here(EDGE_ARRAYS, nx, nz)),
+    rows_in = (keep(near_rows), keep(far_rows), keep(swept))
+    inner = pl.pallas_call(
+        third_kernel,
+        out_shape=here(5, nx * ny, nz),
         in_specs=[near] * 3,
-        out_specs=(near,) * 2,
+        out_specs=near,
         name="sweep_third",
-    )(keep(near_rows), keep(far_rows), keep(swept))
+    )(*rows_in)
+    edge = pl.pallas_call(
+        functools.partial(window_kernel, cols),
+        out_shape=here(EDGE_ARRAYS, nx, nz),
+        in_specs=[near] * 3,
+        out_specs=near,
+        name="third_windows",
+    )(*rows_in)
+    far = pl.BlockSpec(memory_space=pltpu.HBM)
+    whole = jax.ShapeDtypeStruct((5, nx * ny, nz), jnp.float32)
+    scratch = [pltpu.VMEM(whole.shape, jnp.float32), pltpu.SemaphoreType.DMA((5,))]
+    ends = pl.pallas_call(
+        functools.partial(end_kernel, cols),
+        out_shape=whole,
+        in_specs=[near] * 3,
+        out_specs=far,
+        scratch_shapes=scratch,
+        name="third_ends",
+    )(keep(inner), keep(edge), keep(one))
     out = pl.pallas_call(
-        functools.partial(edge_kernel, cols),
-        out_shape=jax.ShapeDtypeStruct((5, nx * ny, nz), jnp.float32),
-        in_specs=[near] * 4,
-        out_specs=pl.BlockSpec(memory_space=pltpu.HBM),
-        scratch_shapes=[
-            pltpu.VMEM((5, nx * ny, nz), jnp.float32),
-            pltpu.SemaphoreType.DMA((5,)),
-        ],
-        name="third_edges",
-    )(keep(inner), keep(edge), keep(two), keep(one))
+        functools.partial(middle_kernel, cols),
+        out_shape=whole,
+        in_specs=[far] + [near] * 4,
+        out_specs=far,
+        input_output_aliases={0: 0},
+        scratch_shapes=scratch,
+        name="third_middle",
+    )(ends, keep(inner), keep(edge), keep(one), keep(two))
     return out.reshape(5, nx, ny, nz)
 
 

time: 12.3 us -> 12.1 us (0.984)
  the two profiles are of different devices: /device:TPU:0 before, /device:TPU:9 now
where the time goes in v8:
time: 12.1 us; the launch traced here: 11.9 us
  starting transfers between devices  4.64 us (38%)
  waiting for transfers between devices  3.89 us (32%)
  Pallas kernels  3.32 us (27%)
    ppermute x4, starting transfers between devices, body(): lax.ppermute(x, ('row', 'col'), swap_pairs(mesh, axis, inner))  4.64 us
    ppermute x4, waiting for transfers between devices, body(): lax.ppermute(x, ('row', 'col'), swap_pairs(mesh, axis, inner))  3.89 us
    pallas_call x1, Pallas kernels, body(): pl.pallas_call(first_kernel, out_shape=(here(6, ny * nx, nz), here(5 * HA...  1.14 us
    pallas_call x1, Pallas kernels, body(): pl.pallas_call(functools.partial(middle_kernel, cols), out_shape=whole, i...  0.93 us
    pallas_call x1, Pallas kernels, body(): pl.pallas_call(third_kernel, out_shape=here(5, nx * ny, nz), in_specs=[ne...  0.52 us
    pallas_call x1, Pallas kernels, body(): pl.pallas_call(functools.partial(second_near, rows), out_shape=(here(5, S...  0.3 us
  transfers between devices with their start and end apart: 4, of which 4 were waited for; matrix products, arithmetic and copies ran while one was open for 0% of the time, Pallas kernels for 9%

profile of v8, /device:TPU:9, one launch (start us, length us, event | category | flops | bytes accessed | tf_op | source)
XLA Modules:
  0.0 11.9 jit_solution(17634981674408247181)
XLA Ops:
  0.0 1.1 %sweep_first.1 = (f32[6,64,128]{2,1,0:T(8,128)S(1)}, f32[16,8,128]{2,1,0:T(8,128)S(1)}, f32[16,8,128]{2,1,0:T(8,128)S(1)}) custom-call(f32[5,8,8,128]{3,2,1,0:T(8,128)} %state_hbm.1, f32[8,8,128]{2,1,0:T(8,128)} %gamma_hbm.1), custom_call_target="tpu_custom_call" | custom-call | tf_op jit(solution)/shard_map/sweep_first/pallas_call | solution.py:529
  1.1 1.2 %collective-permute-start = (f32[16,8,128]{2,1,0:T(8,128)S(1)}, f32[16,8,128]{2,1,0:T(8,128)S(1)}, u32[]{:S(2)}, u32[]{:S(2)}) collective-permute-start(f32[16,8,128]{2,1,0:T(8,128)S(1)} %get-tuple-element.16), channel_id=1, source_target_pairs={{0,1},{1,0},{2,3},{3,2},{4,8},{5,9},{6,10},{7,11},{8,4},{9,5},{10,... | collective-permute-start | bytes 196616 | tf_op jit(solution)/shard_map/ppermute | solution.py:527
  2.3 1.4 %collective-permute-start.1 = (f32[16,8,128]{2,1,0:T(8,128)S(1)}, f32[16,8,128]{2,1,0:T(8,128)S(1)}, u32[]{:S(2)}, u32[]{:S(2)}) collective-permute-start(f32[16,8,128]{2,1,0:T(8,128)S(1)} %get-tuple-element.18), channel_id=1, source_target_pairs={{0,4},{1,5},{2,6},{3,7},{4,0},{5,1},{6,2},{7,3},{8,12},{9,13},{10,... | collective-permute-start | bytes 196616 | tf_op jit(solution)/shard_map/ppermute | solution.py:527
  3.7 1.6 %collective-permute-done.two_ref = f32[16,8,128]{2,1,0:T(8,128)S(1)} collective-permute-done((f32[16,8,128]{2,1,0:T(8,128)S(1)}, f32[16,8,128]{2,1,0:T(8,128)S(1)}, u32[]{:S(2)}, u32[]{:S(2)}) %collective-permute-start) | collective-permute-done | bytes 65568 | tf_op jit(solution)/shard_map/ppermute | solution.py:527
  5.3 0.3 %second_near.1 = (f32[5,40,128]{2,1,0:T(8,128)S(1)}, f32[8,128]{1,0:T(8,128)S(1)}, f32[8,128]{1,0:T(8,128)S(1)}, f32[36,8,128]{2,1,0:T(8,128)S(1)}) custom-call(f32[6,64,128]{2,1,0:T(8,128)S(1)} %get-tuple-element.15.swept_ref.gamma_ref, f32[16,8,128]{2,1,0:T(8,128)S(1)} %collective-permute-done.two_ref), custom_call_target="tpu_custom_call" | custom-call | tf_op jit(solution)/shard_map/second_near/pallas_call | solution.py:547
  5.6 1.5 %collective-permute-done.1.one_ref = f32[16,8,128]{2,1,0:T(8,128)S(1)} collective-permute-done((f32[16,8,128]{2,1,0:T(8,128)S(1)}, f32[16,8,128]{2,1,0:T(8,128)S(1)}, u32[]{:S(2)}, u32[]{:S(2)}) %collective-permute-start.1) | collective-permute-done | bytes 65568 | tf_op jit(solution)/shard_map/ppermute | solution.py:527
  7.1 0.2 %second_far.1 = (f32[5,24,128]{2,1,0:T(8,128)S(1)}, f32[8,128]{1,0:T(8,128)S(1)}, f32[16,128]{1,0:T(8,128)S(1)}) custom-call(f32[6,64,128]{2,1,0:T(8,128)S(1)} %get-tuple-element.15.swept_ref.gamma_ref, f32[16,8,128]{2,1,0:T(8,128)S(1)} %collective-permute-done.1.one_ref, f32[8,128]{1,0:T(8,128)S(1)} %get-tuple-element.19.lower_ref, ...), custom_call_target="tpu_custom_call" | custom-call | tf_op jit(solution)/shard_map/second_far/pallas_call | solution.py:554
  7.3 2.1 %collective-permute-start.3 = (f32[16,128]{1,0:T(8,128)S(1)}, f32[16,128]{1,0:T(8,128)S(1)}, u32[]{:S(2)}, u32[]{:S(2)}) collective-permute-start(f32[16,128]{1,0:T(8,128)S(1)} %get-tuple-element.24), channel_id=1, source_target_pairs={{0,3},{1,2},{2,1},{3,0},{4,7},{5,6},{6,5},{7,4},{8,11},{9,10},{10,... | collective-permute-start | bytes 24584 | tf_op jit(solution)/shard_map/ppermute | solution.py:527
  9.3 0.0 collective-permute-start.2
  9.4 0.5 %sweep_third.1.inner_ref = f32[5,64,128]{2,1,0:T(8,128)S(1)} custom-call(f32[5,40,128]{2,1,0:T(8,128)S(1)} %get-tuple-element.17.near_ref, f32[5,24,128]{2,1,0:T(8,128)S(1)} %get-tuple-element.22.far_ref, f32[6,64,128]{2,1,0:T(8,128)S(1)} %get-tuple-element.15.swept_ref.gamma_ref), custom_call_target="tpu_custom_call" | custom-call | tf_op jit(solution)/shard_map/sweep_third/pallas_call | solution.py:564
  9.9 0.2 %third_windows.1.edge_ref = f32[43,8,128]{2,1,0:T(8,128)S(1)} custom-call(f32[5,40,128]{2,1,0:T(8,128)S(1)} %get-tuple-element.17.near_ref, f32[5,24,128]{2,1,0:T(8,128)S(1)} %get-tuple-element.22.far_ref, f32[6,64,128]{2,1,0:T(8,128)S(1)} %get-tuple-element.15.swept_ref.gamma_ref), custom_call_target="tpu_custom_call" | custom-call | tf_op jit(solution)/shard_map/third_windows/pallas_call | solution.py:571
  10.1 0.4 %collective-permute-done.2.one_ref = f32[8,128]{1,0:T(8,128)S(1)} collective-permute-done((f32[8,128]{1,0:T(8,128)S(1)}, f32[8,128]{1,0:T(8,128)S(1)}, u32[]{:S(2)}, u32[]{:S(2)}) %collective-permute-start.2) | collective-permute-done | bytes 4128 | tf_op jit(solution)/shard_map/ppermute | solution.py:527
  10.6 0.4 %collective-permute-done.3.two_ref = f32[16,128]{1,0:T(8,128)S(1)} collective-permute-done((f32[16,128]{1,0:T(8,128)S(1)}, f32[16,128]{1,0:T(8,128)S(1)}, u32[]{:S(2)}, u32[]{:S(2)}) %collective-permute-start.3) | collective-permute-done | bytes 8224 | tf_op jit(solution)/shard_map/ppermute | solution.py:527
  11.0 0.9 %third_middle.1 = f32[5,64,128]{2,1,0:T(8,128)} custom-call(f32[5,64,128]{2,1,0:T(8,128)} %third_ends.1.ends_ref, f32[5,64,128]{2,1,0:T(8,128)S(1)} %sweep_third.1.inner_ref, f32[43,8,128]{2,1,0:T(8,128)S(1)} %third_windows.1.edge_ref, f32[8,128]{1,0:T(8,128)S(1)} %collective-permute-done.2.one_ref, ...), custom_call_target="tpu_custom_call", output_to_operand_aliasing={{}: (0, {})} | custom-call | tf_op jit(solution)/shard_map/third_middle/pallas_call | solution.py:589
  (1 shorter events, 0.0 us)
Async XLA Ops:
  1.1 4.1 %collective-permute-start = (f32[16,8,128]{2,1,0:T(8,128)S(1)}, f32[16,8,128]{2,1,0:T(8,128)S(1)}, u32[]{:S(2)}, u32[]{:S(2)}) collective-permute-start(f32[16,8,128]{2,1,0:T(8,128)S(1)} %get-tuple-element.16), channel_id=1, source_target_pairs={{0,1},{1,0},{2,3},{3,2},{4,8},{5,9},{6,10},{7,11},{8,4},{9,5},{10,... | collective-permute-start | bytes 196616 | tf_op jit(solution)/shard_map/ppermute | solution.py:527
  2.3 4.8 %collective-permute-start.1 = (f32[16,8,128]{2,1,0:T(8,128)S(1)}, f32[16,8,128]{2,1,0:T(8,128)S(1)}, u32[]{:S(2)}, u32[]{:S(2)}) collective-permute-start(f32[16,8,128]{2,1,0:T(8,128)S(1)} %get-tuple-element.18), channel_id=1, source_target_pairs={{0,4},{1,5},{2,6},{3,7},{4,0},{5,1},{6,2},{7,3},{8,12},{9,13},{10,... | collective-permute-start | bytes 196616 | tf_op jit(solution)/shard_map/ppermute | solution.py:527
  7.3 3.7 %collective-permute-start.3 = (f32[16,128]{1,0:T(8,128)S(1)}, f32[16,128]{1,0:T(8,128)S(1)}, u32[]{:S(2)}, u32[]{:S(2)}) collective-permute-start(f32[16,128]{1,0:T(8,128)S(1)} %get-tuple-element.24), channel_id=1, source_target_pairs={{0,3},{1,2},{2,1},{3,0},{4,7},{5,6},{6,5},{7,4},{8,11},{9,10},{10,... | collective-permute-start | bytes 24584 | tf_op jit(solution)/shard_map/ppermute | solution.py:527
  9.3 1.2 %collective-permute-start.2 = (f32[8,128]{1,0:T(8,128)S(1)}, f32[8,128]{1,0:T(8,128)S(1)}, u32[]{:S(2)}, u32[]{:S(2)}) collective-permute-start(f32[8,128]{1,0:T(8,128)S(1)} %get-tuple-element.23), channel_id=1, source_target_pairs={{0,1},{1,0},{2,3},{3,2},{4,5},{5,4},{6,7},{7,6},{8,9},{9,8},{10,11... | collective-permute-start | bytes 12296 | tf_op jit(solution)/shard_map/ppermute | solution.py:527

commit v9 on v8

--- a/solution.py
+++ b/solution.py
@@ -167,36 +167,89 @@
     return pl.ds(pl.multiple_of(own_row(y) * nx + base, SUB), SUB)
 
 
-def first_kernel(state_hbm, gamma_hbm, swept_ref, one_ref, two_ref, state_ref, gamma_ref, sems):
-    nx, ny = gamma_ref.shape[0], gamma_ref.shape[1]
-    copies = [
-        pltpu.make_async_copy(state_hbm.at[f], state_ref.at[f], sems.at[f]) for f in range(5)
+def shifted(tiles, by, edge):
+    sub = lax.broadcasted_iota(jnp.int32, (SUB, LANES), 0)
+    turned_tiles = [pltpu.roll(tile, SUB - 1 if by == 1 else 1, 0) for tile in tiles]
+    if by == 1:
+        beyond_tiles = turned_tiles[1:] + [edge]
+        return [jnp.where(sub == SUB - 1, b, a) for a, b in zip(turned_tiles, beyond_tiles)]
+    beyond_tiles = [edge] + turned_tiles[:-1]
+    return [jnp.where(sub == 0, b, a) for a, b in zip(turned_tiles, beyond_tiles)]
+
+
+def sweep_sublanes(cons, gamma):
+    gam1 = [g - 1.0 for g in gamma]
+    inv_gam1 = [recip(g) for g in gam1]
+    prim = [primitives(c, g, 0) for c, g in zip(cons, gam1)]
+    upper, lower_next = [], []
+    for q in zip(*prim):
+        here = [b - a for a, b in zip(q, shifted(q, 1, q[-1]))]
+        right = [face_rise(*d) for d in zip(shifted(here, -1, 0.0), here, shifted(here, 1, 0.0))]
+        left = shifted([h - r for h, r in zip(here, right)], -1, 0.0)
+        pairs = [edges(*t) for t in zip(q, right, left)]
+        upper.append([p[0] for p in pairs])
+        lower_next.append(shifted([p[1] for p in pairs], 1, q[-1]))
+    gamma_next, inv_next = shifted(gamma, 1, gamma[-1]), shifted(inv_gam1, 1, inv_gam1[-1])
+    flux = [
+        double_flux(state_flux(u, g, i), state_flux(l, gn, i_n))
+        for u, l, g, i, gn, i_n in zip(
+            zip(*upper), zip(*lower_next), gamma, inv_gam1, gamma_next, inv_next
+        )
     ]
-    copies.append(pltpu.make_async_copy(gamma_hbm, gamma_ref, sems.at[5]))
-    for f, copy in enumerate(copies):
-        copy.start(priority=f % 2)
+    start = state_flux(prim[0], gamma[0], inv_gam1[0])
+    start = double_flux(start, start)
+    before = [shifted(list(f), -1, e) for f, e in zip(zip(*flux), start)]
+    return [updated(c, f, b, 0) for c, f, b in zip(cons, flux, zip(*before))]
+
+
+def raw_kernel(state_hbm, gamma_hbm, two_ref, sems):
+    copies = []
+    for j in range(HALO):
+        row = own_row(j)
+        copies.append(
+            pltpu.make_async_copy(
+                state_hbm.at[:, :, row, :], two_ref.at[pl.ds(0, 5), j], sems.at[j, 0]
+            )
+        )
+        copies.append(pltpu.make_async_copy(gamma_hbm.at[:, row, :], two_ref.at[5, j], sems.at[j, 1]))
+    for k, copy in enumerate(copies):
+        copy.start(priority=k % 2)
     for copy in copies:
         copy.wait()
+
+
+def edge_rows_kernel(state_ref, gamma_ref, one_ref):
+    nx, ny = one_ref.shape[1], SUB
+    tiles = [pl.ds(base, SUB) for base in range(0, nx, SUB)]
+    for j in range(HALO):
+        row = own_row(ny - 1 - j)
+        at = [pl.ds(base * ny + row, SUB, stride=ny) for base in range(0, nx, SUB)]
+        gamma = [gamma_ref[rows, :] for rows in at]
+        swept = sweep_sublanes([[state_ref[f, rows, :] for f in range(5)] for rows in at], gamma)
+        for tile, cons, g in zip(tiles, swept, gamma):
+            for k, value in enumerate(primitives(cons, g - 1.0, 1)):
+                one_ref[HALO * k + j, tile, :] = value
+            if j == 0:
+                one_ref[5 * HALO, tile, :] = g
+
+
+def first_kernel(state_ref, gamma_ref, swept_ref):
+    ny = SUB
+    nx = gamma_ref.shape[0] // ny
+
+    def load_gamma(x):
+        return gamma_ref[pl.ds(x * ny, ny), :]
 
     def store(x, cons):
         for f in range(5):
             swept_ref[f, pl.ds(x, ny, stride=nx), :] = cons[f]
 
-    sweep = Sweep(nx, 0, lambda x: [state_ref[f, x] for f in range(5)], lambda x: gamma_ref[x])
+    sweep = Sweep(
+        nx, 0, lambda x: [state_ref[f, pl.ds(x * ny, ny), :] for f in range(5)], load_gamma
+    )
     sweep.run(range(nx), store)
     for x in range(nx):
-        swept_ref[5, pl.ds(x, ny, stride=nx), :] = gamma_ref[x]
-    for base in range(0, nx, SUB):
-        at = pl.ds(base, SUB)
-        for out_ref, nearest in ((one_ref, range(ny - 1, ny - 1 - HALO, -1)), (two_ref, range(HALO))):
-            for j, y in enumerate(nearest):
-                row = rows_at(y, base, nx)
-                gamma = swept_ref[5, row, :]
-                prim = primitives([swept_ref[f, row, :] for f in range(5)], gamma - 1.0, 1)
-                for k in range(5):
-                    out_ref[HALO * k + j, at, :] = prim[k]
-                if j == 0:
-                    out_ref[5 * HALO, at, :] = gamma
+        swept_ref[5, pl.ds(x, ny, stride=nx), :] = load_gamma(x)
 
 
 def row_loads(swept_ref, base, nx, sign):
@@ -262,6 +315,13 @@
     row = lax.axis_index("row")
     end = (row == 0) | (row == rows - 1)
     sign = own_sign()
+    tiles = [pl.ds(base, SUB) for base in range(0, nx, SUB)]
+    halos = []
+    for j in range(HALO):
+        gamma = [two_ref[5 * HALO + j, tile, :] for tile in tiles]
+        cons = [[two_ref[HALO * f + j, tile, :] for f in range(5)] for tile in tiles]
+        swept = sweep_sublanes(cons, gamma)
+        halos.append([primitives(c, g - 1.0, 1) for c, g in zip(swept, gamma)])
     for base in range(0, nx, SUB):
         at = pl.ds(base, SUB)
         load, load_own_gamma = row_loads(swept_ref, base, nx, sign)
@@ -273,7 +333,7 @@
             return jnp.where(end, load_own_gamma(0), two_ref[5 * HALO, at, :])
 
         def halo(y):
-            got = [two_ref[HALO * k - 1 - y, at, :] for k in range(5)]
+            got = list(halos[-1 - y][base // SUB])
             got[1] = got[1] * sign
             return [jnp.where(end, p, q) for p, q in zip(sweep.get(0), got)]
 
@@ -526,23 +586,30 @@
     near = pl.BlockSpec(memory_space=pltpu.VMEM)
     swap = lambda x, axis, inner: lax.ppermute(x, ("row", "col"), swap_pairs(mesh, axis, inner))
 
-    swept, one, two = pl.pallas_call(
+    two = pl.pallas_call(
+        raw_kernel,
+        out_shape=here(6, HALO, nx, nz),
+        in_specs=[pl.BlockSpec(memory_space=pltpu.HBM)] * 2,
+        out_specs=near,
+        scratch_shapes=[pltpu.SemaphoreType.DMA((HALO, 2))],
+        name="raw_edges",
+    )(state, gamma)
+    two = swap(two, "row", True).reshape(6 * HALO, nx, nz)
+    held = (keep(state.reshape(5, nx * ny, nz)), keep(gamma.reshape(nx * ny, nz)))
+    one = pl.pallas_call(
+        edge_rows_kernel,
+        out_shape=here(5 * HALO + 1, nx, nz),
+        in_specs=[near] * 2,
+        out_specs=near,
+        name="edge_rows",
+    )(*held)
+    swept = pl.pallas_call(
         first_kernel,
-        out_shape=(
-            here(6, ny * nx, nz),
-            here(5 * HALO + 1, nx, nz),
-            here(5 * HALO + 1, nx, nz),
-        ),
-        in_specs=[pl.BlockSpec(memory_space=pltpu.HBM)] * 2,
-        out_specs=(near,) * 3,
-        scratch_shapes=[
-            pltpu.VMEM(state.shape, jnp.float32),
-            pltpu.VMEM(gamma.shape, jnp.float32),
-            pltpu.SemaphoreType.DMA((6,)),
-        ],
+        out_shape=here(6, ny * nx, nz),
+        in_specs=[near] * 2,
+        out_specs=near,
         name="sweep_first",
-    )(state, gamma)
-    two = swap(two, "row", True)
+    )(*held)
     one = swap(one, "row", False)
     near_rows, lower, upper, kept = pl.pallas_call(
         functools.partial(second_near, rows),

time: 12.1 us -> 12 us (level)
  the two profiles are of different devices: /device:TPU:9 before, /device:TPU:1 now
where the time goes in v9:
time: 12 us; the launch traced here: 11.9 us
  starting transfers between devices  5.75 us (48%)
  Pallas kernels  3.58 us (30%)
  waiting for transfers between devices  2.47 us (21%)
    ppermute x4, starting transfers between devices, body(): lax.ppermute(x, ('row', 'col'), swap_pairs(mesh, axis, inner))  5.75 us
    ppermute x4, waiting for transfers between devices, body(): lax.ppermute(x, ('row', 'col'), swap_pairs(mesh, axis, inner))  2.47 us
    pallas_call x1, Pallas kernels, body(): pl.pallas_call(functools.partial(middle_kernel, cols), out_shape=whole, i...  0.93 us
    pallas_call x1, Pallas kernels, body(): pl.pallas_call(raw_kernel, out_shape=here(6, HALO, nx, nz), in_specs=[pl....  0.9 us
    pallas_call x1, Pallas kernels, body(): pl.pallas_call(third_kernel, out_shape=here(5, nx * ny, nz), in_specs=[ne...  0.52 us
    pallas_call x1, Pallas kernels, body(): pl.pallas_call(functools.partial(second_near, rows), out_shape=(here(5, S...  0.43 us
  transfers between devices with their start and end apart: 4, of which 3 were waited for; matrix products, arithmetic and copies ran while one was open for 0% of the time, Pallas kernels for 13%

profile of v9, /device:TPU:1, one launch (start us, length us, event | category | flops | bytes accessed | tf_op | source)
XLA Modules:
  0.0 11.9 jit_solution(3987683085338980205)
XLA Ops:
  0.0 0.0 copy-start.1
  0.0 0.0 copy-start
  0.0 0.9 %raw_edges.1 = f32[6,3,8,128]{3,2,1,0:T(8,128)S(1)} custom-call(f32[5,8,8,128]{3,2,1,0:T(8,128)} %state_hbm.1, f32[8,8,128]{2,1,0:T(8,128)} %gamma_hbm.1), custom_call_target="tpu_custom_call" | custom-call | tf_op jit(solution)/shard_map/raw_edges/pallas_call | solution.py:589
  0.9 0.1 %collective-permute-start = (f32[6,3,8,128]{3,2,1,0:T(8,128)S(1)}, f32[6,3,8,128]{3,2,1,0:T(8,128)S(1)}, u32[]{:S(2)}, u32[]{:S(2)}) collective-permute-start(f32[6,3,8,128]{3,2,1,0:T(8,128)S(1)} %raw_edges.1), channel_id=1, source_target_pairs={{0,1},{1,0},{2,3},{3,2},{4,8},{5,9},{6,10},{7,11},{8,4},{9,5},{10,... | collective-permute-start | bytes 221192 | tf_op jit(solution)/shard_map/ppermute | solution.py:587
  1.0 0.0 copy-done.1
  1.0 0.0 copy-done
  1.0 0.2 %edge_rows.1 = f32[16,8,128]{2,1,0:T(8,128)S(1)} custom-call(f32[5,64,128]{2,1,0:T(8,128)S(1)} %bitcast.4, f32[64,128]{1,0:T(8,128)S(1)} %bitcast.6), custom_call_target="tpu_custom_call" | custom-call | tf_op jit(solution)/shard_map/edge_rows/pallas_call | solution.py:599
  1.2 3.3 %collective-permute-start.1 = (f32[16,8,128]{2,1,0:T(8,128)S(1)}, f32[16,8,128]{2,1,0:T(8,128)S(1)}, u32[]{:S(2)}, u32[]{:S(2)}) collective-permute-start(f32[16,8,128]{2,1,0:T(8,128)S(1)} %edge_rows.1), channel_id=1, source_target_pairs={{0,4},{1,5},{2,6},{3,7},{4,0},{5,1},{6,2},{7,3},{8,12},{9,13},{10,... | collective-permute-start | bytes 196616 | tf_op jit(solution)/shard_map/ppermute | solution.py:587
  4.5 0.2 %sweep_first.1.swept_ref.gamma_ref = f32[6,64,128]{2,1,0:T(8,128)S(1)} custom-call(f32[5,64,128]{2,1,0:T(8,128)S(1)} %bitcast.5, f32[64,128]{1,0:T(8,128)S(1)} %bitcast.7), custom_call_target="tpu_custom_call" | custom-call | tf_op jit(solution)/shard_map/sweep_first/pallas_call | solution.py:606
  4.7 0.0 collective-permute-done
  4.7 0.4 %second_near.1 = (f32[5,40,128]{2,1,0:T(8,128)S(1)}, f32[8,128]{1,0:T(8,128)S(1)}, f32[8,128]{1,0:T(8,128)S(1)}, f32[36,8,128]{2,1,0:T(8,128)S(1)}) custom-call(f32[6,64,128]{2,1,0:T(8,128)S(1)} %sweep_first.1.swept_ref.gamma_ref, f32[18,8,128]{2,1,0:T(8,128)S(1)} %bitcast.8), custom_call_target="tpu_custom_call" | custom-call | tf_op jit(solution)/shard_map/second_near/pallas_call | solution.py:614
  5.2 1.7 %collective-permute-done.1.one_ref = f32[16,8,128]{2,1,0:T(8,128)S(1)} collective-permute-done((f32[16,8,128]{2,1,0:T(8,128)S(1)}, f32[16,8,128]{2,1,0:T(8,128)S(1)}, u32[]{:S(2)}, u32[]{:S(2)}) %collective-permute-start.1) | collective-permute-done | bytes 65568 | tf_op jit(solution)/shard_map/ppermute | solution.py:587
  6.8 0.2 %second_far.1 = (f32[5,24,128]{2,1,0:T(8,128)S(1)}, f32[8,128]{1,0:T(8,128)S(1)}, f32[16,128]{1,0:T(8,128)S(1)}) custom-call(f32[6,64,128]{2,1,0:T(8,128)S(1)} %sweep_first.1.swept_ref.gamma_ref, f32[16,8,128]{2,1,0:T(8,128)S(1)} %collective-permute-done.1.one_ref, f32[8,128]{1,0:T(8,128)S(1)} %get-tuple-element.13.lower_ref, ...), custom_call_target="tpu_custom_call" | custom-call | tf_op jit(solution)/shard_map/second_far/pallas_call | solution.py:621
  7.0 2.3 %collective-permute-start.3 = (f32[16,128]{1,0:T(8,128)S(1)}, f32[16,128]{1,0:T(8,128)S(1)}, u32[]{:S(2)}, u32[]{:S(2)}) collective-permute-start(f32[16,128]{1,0:T(8,128)S(1)} %get-tuple-element.18), channel_id=1, source_target_pairs={{0,3},{1,2},{2,1},{3,0},{4,7},{5,6},{6,5},{7,4},{8,11},{9,10},{10,... | collective-permute-start | bytes 24584 | tf_op jit(solution)/shard_map/ppermute | solution.py:587
  9.3 0.0 collective-permute-start.2
  9.3 0.5 %sweep_third.1.inner_ref = f32[5,64,128]{2,1,0:T(8,128)S(1)} custom-call(f32[5,40,128]{2,1,0:T(8,128)S(1)} %get-tuple-element.12.near_ref, f32[5,24,128]{2,1,0:T(8,128)S(1)} %get-tuple-element.16.far_ref, f32[6,64,128]{2,1,0:T(8,128)S(1)} %sweep_first.1.swept_ref.gamma_ref), custom_call_target="tpu_custom_call" | custom-call | tf_op jit(solution)/shard_map/sweep_third/pallas_call | solution.py:631
  9.8 0.2 %third_windows.1.edge_ref = f32[43,8,128]{2,1,0:T(8,128)S(1)} custom-call(f32[5,40,128]{2,1,0:T(8,128)S(1)} %get-tuple-element.12.near_ref, f32[5,24,128]{2,1,0:T(8,128)S(1)} %get-tuple-element.16.far_ref, f32[6,64,128]{2,1,0:T(8,128)S(1)} %sweep_first.1.swept_ref.gamma_ref), custom_call_target="tpu_custom_call" | custom-call | tf_op jit(solution)/shard_map/third_windows/pallas_call | solution.py:638
  10.1 0.4 %collective-permute-done.2.one_ref = f32[8,128]{1,0:T(8,128)S(1)} collective-permute-done((f32[8,128]{1,0:T(8,128)S(1)}, f32[8,128]{1,0:T(8,128)S(1)}, u32[]{:S(2)}, u32[]{:S(2)}) %collective-permute-start.2) | collective-permute-done | bytes 4128 | tf_op jit(solution)/shard_map/ppermute | solution.py:587
  10.5 0.4 %collective-permute-done.3.two_ref = f32[16,128]{1,0:T(8,128)S(1)} collective-permute-done((f32[16,128]{1,0:T(8,128)S(1)}, f32[16,128]{1,0:T(8,128)S(1)}, u32[]{:S(2)}, u32[]{:S(2)}) %collective-permute-start.3) | collective-permute-done | bytes 8224 | tf_op jit(solution)/shard_map/ppermute | solution.py:587
  10.9 0.9 %third_middle.1 = f32[5,64,128]{2,1,0:T(8,128)} custom-call(f32[5,64,128]{2,1,0:T(8,128)} %third_ends.1.ends_ref, f32[5,64,128]{2,1,0:T(8,128)S(1)} %sweep_third.1.inner_ref, f32[43,8,128]{2,1,0:T(8,128)S(1)} %third_windows.1.edge_ref, f32[8,128]{1,0:T(8,128)S(1)} %collective-permute-done.2.one_ref, ...), custom_call_target="tpu_custom_call", output_to_operand_aliasing={{}: (0, {})} | custom-call | tf_op jit(solution)/shard_map/third_middle/pallas_call | solution.py:656
  (1 shorter events, 0.0 us)
Async XLA Ops:
  0.0 1.0 %copy-start.1 = (f32[8,8,128]{2,1,0:T(8,128)S(1)}, f32[8,8,128]{2,1,0:T(8,128)}, u32[]{:S(2)}) copy-start(f32[8,8,128]{2,1,0:T(8,128)} %gamma_hbm.1) | copy-start | bytes 98308
  0.0 1.0 %copy-start = (f32[5,8,8,128]{3,2,1,0:T(8,128)S(1)}, f32[5,8,8,128]{3,2,1,0:T(8,128)}, u32[]{:S(2)}) copy-start(f32[5,8,8,128]{3,2,1,0:T(8,128)} %state_hbm.1) | copy-start | bytes 491524
  0.9 3.8 %collective-permute-start = (f32[6,3,8,128]{3,2,1,0:T(8,128)S(1)}, f32[6,3,8,128]{3,2,1,0:T(8,128)S(1)}, u32[]{:S(2)}, u32[]{:S(2)}) collective-permute-start(f32[6,3,8,128]{3,2,1,0:T(8,128)S(1)} %raw_edges.1), channel_id=1, source_target_pairs={{0,1},{1,0},{2,3},{3,2},{4,8},{5,9},{6,10},{7,11},{8,4},{9,5},{10,... | collective-permute-start | bytes 221192 | tf_op jit(solution)/shard_map/ppermute | solution.py:587
  1.2 5.6 %collective-permute-start.1 = (f32[16,8,128]{2,1,0:T(8,128)S(1)}, f32[16,8,128]{2,1,0:T(8,128)S(1)}, u32[]{:S(2)}, u32[]{:S(2)}) collective-permute-start(f32[16,8,128]{2,1,0:T(8,128)S(1)} %edge_rows.1), channel_id=1, source_target_pairs={{0,4},{1,5},{2,6},{3,7},{4,0},{5,1},{6,2},{7,3},{8,12},{9,13},{10,... | collective-permute-start | bytes 196616 | tf_op jit(solution)/shard_map/ppermute | solution.py:587
  7.0 3.9 %collective-permute-start.3 = (f32[16,128]{1,0:T(8,128)S(1)}, f32[16,128]{1,0:T(8,128)S(1)}, u32[]{:S(2)}, u32[]{:S(2)}) collective-permute-start(f32[16,128]{1,0:T(8,128)S(1)} %get-tuple-element.18), channel_id=1, source_target_pairs={{0,3},{1,2},{2,1},{3,0},{4,7},{5,6},{6,5},{7,4},{8,11},{9,10},{10,... | collective-permute-start | bytes 24584 | tf_op jit(solution)/shard_map/ppermute | solution.py:587
  9.3 1.2 %collective-permute-start.2 = (f32[8,128]{1,0:T(8,128)S(1)}, f32[8,128]{1,0:T(8,128)S(1)}, u32[]{:S(2)}, u32[]{:S(2)}) collective-permute-start(f32[8,128]{1,0:T(8,128)S(1)} %get-tuple-element.17), channel_id=1, source_target_pairs={{0,1},{1,0},{2,3},{3,2},{4,5},{5,4},{6,7},{7,6},{8,9},{9,8},{10,11... | collective-permute-start | bytes 12296 | tf_op jit(solution)/shard_map/ppermute | solution.py:587

commit v10 on v9

--- a/solution.py
+++ b/solution.py
@@ -218,19 +218,28 @@
         copy.wait()
 
 
-def edge_rows_kernel(state_ref, gamma_ref, one_ref):
+def edge_rows_kernel(state_ref, gamma_ref, one_ref, rim_ref):
     nx, ny = one_ref.shape[1], SUB
-    tiles = [pl.ds(base, SUB) for base in range(0, nx, SUB)]
+    tiles = range(0, nx, SUB)
+    ends = [[None, None] for _ in tiles]
+
+    def put(n, tile, value):
+        one_ref[n, pl.ds(tile * SUB, SUB), :] = value
+        ends[tile][n // SUB] = into_window(ends[tile][n // SUB], n % SUB, value)
+
     for j in range(HALO):
         row = own_row(ny - 1 - j)
-        at = [pl.ds(base * ny + row, SUB, stride=ny) for base in range(0, nx, SUB)]
+        at = [pl.ds(base * ny + row, SUB, stride=ny) for base in tiles]
         gamma = [gamma_ref[rows, :] for rows in at]
         swept = sweep_sublanes([[state_ref[f, rows, :] for f in range(5)] for rows in at], gamma)
-        for tile, cons, g in zip(tiles, swept, gamma):
+        for tile, (cons, g) in enumerate(zip(swept, gamma)):
             for k, value in enumerate(primitives(cons, g - 1.0, 1)):
-                one_ref[HALO * k + j, tile, :] = value
+                put(HALO * k + j, tile, value)
             if j == 0:
-                one_ref[5 * HALO, tile, :] = g
+                put(5 * HALO, tile, g)
+    for tile, base in enumerate(tiles):
+        for n in range(2):
+            rim_ref[pl.ds(n * nx + base, SUB), :] = ends[tile][n]
 
 
 def first_kernel(state_ref, gamma_ref, swept_ref):
@@ -352,42 +361,67 @@
             kept_ref[k, at, :] = kept[k]
 
 
-def second_far(
-    swept_ref, one_ref, lower_ref, upper_ref, kept_ref, next_ref, to_one_ref, to_two_ref
+def sweep_far(swept_ref, kept_ref, base, received, store):
+    nx = swept_ref.shape[1] // SUB
+    at = pl.ds(base, SUB)
+    sign = own_sign()
+    load, load_own_gamma = row_loads(swept_ref, base, nx, sign)
+
+    def load_gamma(y):
+        return load_own_gamma(y) if y < SUB else received(5 * HALO)
+
+    def halo(y):
+        got = [received(HALO * k + y - SUB) for k in range(5)]
+        got[1] = got[1] * sign
+        return got
+
+    def signed_store(y, cons):
+        cons[2] = cons[2] * sign
+        store(y, cons, load_own_gamma(y))
+
+    kept = [kept_ref[k, at, :] for k in range(KEPT)]
+    sweep = Sweep(SUB, 1, load, load_gamma, halo)
+    sweep.prim[SPLIT + 1], sweep.prim[SPLIT + 2] = kept[0:5], kept[5:10]
+    sweep.diff[SPLIT] = kept[10:15]
+    sweep.rise[SPLIT] = (None, kept[15:20])
+    sweep.state[SPLIT, True] = (kept[20:25], kept[25:30], kept[30])
+    sweep.run(range(SPLIT, SUB), signed_store, kept[31:36])
+
+
+def rim_kernel(
+    swept_ref, rim_ref, lower_ref, upper_ref, kept_ref, next_ref, to_one_ref, to_two_ref
 ):
     nx = swept_ref.shape[1] // SUB
-    sign = own_sign()
     for base in range(0, nx, SUB):
         at = pl.ds(base, SUB)
-        load, load_own_gamma = row_loads(swept_ref, base, nx, sign)
         pack = EdgePack(lower_ref[at, :], upper_ref[at, :])
 
-        def load_gamma(y):
-            return load_own_gamma(y) if y < SUB else one_ref[5 * HALO, at, :]
-
-        def halo(y):
-            got = [one_ref[HALO * k + y - SUB, at, :] for k in range(5)]
-            got[1] = got[1] * sign
-            return got
-
-        def store(y, cons):
-            cons[2] = cons[2] * sign
+        def received(n):
+            return turned(rim_ref[pl.ds(n // SUB * nx + base, SUB), :], GROUP * (n % SUB) + 6)
+
+        def store(y, cons, gamma):
             for f in range(5):
                 next_ref[f, pl.ds((y - SPLIT) * nx + base, SUB), :] = cons[f]
-            pack.add(y, cons, load_own_gamma(y))
-
-        kept = [kept_ref[k, at, :] for k in range(KEPT)]
-        sweep = Sweep(SUB, 1, load, load_gamma, halo)
-        sweep.prim[SPLIT + 1], sweep.prim[SPLIT + 2] = kept[0:5], kept[5:10]
-        sweep.diff[SPLIT] = kept[10:15]
-        sweep.rise[SPLIT] = (None, kept[15:20])
-        sweep.state[SPLIT, True] = (kept[20:25], kept[25:30], kept[30])
-        sweep.run(range(SPLIT, SUB), store, kept[31:36])
+            pack.add(y, cons, gamma)
+
+        sweep_far(swept_ref, kept_ref, base, received, store)
         lower, upper = pack.pack
         odd = lax.rem(lax.axis_index("col"), 2) == 1
         to_one_ref[at, :] = jnp.where(odd, lower, upper)
         to_two_ref[at, :] = jnp.where(odd, upper, lower)
         to_two_ref[pl.ds(nx + base, SUB), :] = lower
+
+
+def second_far(swept_ref, one_ref, kept_ref, *others):
+    next_ref = others[-1]
+    nx = swept_ref.shape[1] // SUB
+    for base in range(0, nx, SUB):
+
+        def store(y, cons, gamma):
+            for f in range(5):
+                next_ref[f, pl.ds((y - SPLIT) * nx + base, SUB), :] = cons[f]
+
+        sweep_far(swept_ref, kept_ref, base, lambda n: one_ref[n, pl.ds(base, SUB), :], store)
 
 
 def sweep_lanes(cons, prim, gamma, normal):
@@ -458,15 +492,16 @@
     return load
 
 
-def third_kernel(near_ref, far_ref, gamma_ref, out_ref):
-    ny = SUB
-    nx = out_ref.shape[1] // ny
+def third_kernel(first, rows_ref, gamma_ref, out_ref):
+    nx = gamma_ref.shape[1] // SUB
     for base in range(0, nx, SUB):
-        load = zone_loads(near_ref, far_ref, gamma_ref, base, nx)
-        for y in range(ny):
-            inner = sweep_lanes(*load(y), 2)
+        for y in range(rows_ref.shape[1] // nx):
+            at = pl.ds(y * nx + base, SUB)
+            cons = [rows_ref[f, at, :] for f in range(5)]
+            gamma = gamma_ref[5, rows_at(first + y, base, nx), :]
+            inner = sweep_lanes(cons, primitives(cons, gamma - 1.0, 2), gamma, 2)
             for f in range(5):
-                out_ref[f, pl.ds(base * ny + own_row(y), SUB, stride=ny), :] = inner[f]
+                out_ref[f, at, :] = inner[f]
 
 
 def window_kernel(cols, near_ref, far_ref, gamma_ref, edge_ref):
@@ -498,7 +533,7 @@
             edge_ref[LINES + 3 + f, at, :] = windows[6 + f]
 
 
-def mend_edges(cols, inner_ref, edge_ref, one_ref, two_ref, out_ref, held, sems):
+def mend_edges(cols, near_ref, far_ref, edge_ref, one_ref, two_ref, out_ref, held, sems):
     nx = edge_ref.shape[1]
     ny = SUB
     odd = lax.rem(lax.axis_index("col"), 2) == 1
@@ -532,7 +567,9 @@
             for y in range(ny):
                 edge = turned(new[f], GROUP * y + 6)
                 at = pl.ds(tile * SUB * ny + own_row(y), SUB, stride=ny)
-                held[f, at, :] = jnp.where(at_edge, edge, inner_ref[f, at, :])
+                rows_ref, start = (near_ref, y) if y < SPLIT else (far_ref, y - SPLIT)
+                inner = rows_ref[f, pl.ds(start * nx + tile * SUB, SUB), :]
+                held[f, at, :] = jnp.where(at_edge, edge, inner)
         copy = pltpu.make_async_copy(held.at[f], out_ref.at[f], sems.at[f])
         copy.start(priority=f % 2)
         copies.append(copy)
@@ -545,16 +582,18 @@
     return (col == 0) | (col == cols - 1)
 
 
-def end_kernel(cols, inner_ref, edge_ref, one_ref, out_ref, held, sems):
+def end_kernel(cols, near_ref, far_ref, edge_ref, one_ref, out_ref, held, sems):
     @pl.when(at_end(cols))
     def _():
-        mend_edges(cols, inner_ref, edge_ref, one_ref, one_ref, out_ref, held, sems)
-
-
-def middle_kernel(cols, ends_ref, inner_ref, edge_ref, one_ref, two_ref, out_ref, held, sems):
+        mend_edges(cols, near_ref, far_ref, edge_ref, one_ref, one_ref, out_ref, held, sems)
+
+
+def middle_kernel(
+    cols, ends_ref, near_ref, far_ref, edge_ref, one_ref, two_ref, out_ref, held, sems
+):
     @pl.when(jnp.logical_not(at_end(cols)))
     def _():
-        mend_edges(cols, inner_ref, edge_ref, one_ref, two_ref, out_ref, held, sems)
+        mend_edges(cols, near_ref, far_ref, edge_ref, one_ref, two_ref, out_ref, held, sems)
 
 
 def swap_pairs(mesh, axis, inner):
@@ -596,11 +635,11 @@
     )(state, gamma)
     two = swap(two, "row", True).reshape(6 * HALO, nx, nz)
     held = (keep(state.reshape(5, nx * ny, nz)), keep(gamma.reshape(nx * ny, nz)))
-    one = pl.pallas_call(
+    one, rim = pl.pallas_call(
         edge_rows_kernel,
-        out_shape=here(5 * HALO + 1, nx, nz),
+        out_shape=(here(5 * HALO + 1, nx, nz), here(2 * nx, nz)),
         in_specs=[near] * 2,
-        out_specs=near,
+        out_specs=(near,) * 2,
         name="edge_rows",
     )(*held)
     swept = pl.pallas_call(
@@ -610,6 +649,7 @@
         out_specs=near,
         name="sweep_first",
     )(*held)
+    rim = swap(rim, "row", False)
     one = swap(one, "row", False)
     near_rows, lower, upper, kept = pl.pallas_call(
         functools.partial(second_near, rows),
@@ -618,50 +658,62 @@
         out_specs=(near,) * 4,
         name="second_near",
     )(keep(swept), keep(two))
-    far_rows, one, two = pl.pallas_call(
-        second_far,
-        out_shape=(here(5, (ny - SPLIT) * nx, nz), here(nx, nz), here(2 * nx, nz)),
+    far_shape = here(5, (ny - SPLIT) * nx, nz)
+    rim_rows, to_one, to_two = pl.pallas_call(
+        rim_kernel,
+        out_shape=(far_shape, here(nx, nz), here(2 * nx, nz)),
         in_specs=[near] * 5,
         out_specs=(near,) * 3,
-        name="second_far",
-    )(keep(swept), keep(one), keep(lower), keep(upper), keep(kept))
-    two = swap(two, "col", True)
-    one = swap(one, "col", False)
-    rows_in = (keep(near_rows), keep(far_rows), keep(swept))
-    inner = pl.pallas_call(
-        third_kernel,
-        out_shape=here(5, nx * ny, nz),
-        in_specs=[near] * 3,
-        out_specs=near,
-        name="sweep_third",
-    )(*rows_in)
+        cost_estimate=pl.CostEstimate(flops=10**9, bytes_accessed=0, transcendentals=0),
+        name="second_rim",
+    )(keep(swept), keep(rim), keep(lower), keep(upper), keep(kept))
+    two = swap(to_two, "col", True)
+    col_one = swap(to_one, "col", False)
+    def third(first, rows_in):
+        return pl.pallas_call(
+            functools.partial(third_kernel, first),
+            out_shape=here(*rows_in.shape),
+            in_specs=[near] * 2,
+            out_specs=near,
+            name="third_far" if first else "third_near",
+        )(keep(rows_in), keep(swept))
+
+    inner_near = third(0, near_rows)
     edge = pl.pallas_call(
         functools.partial(window_kernel, cols),
         out_shape=here(EDGE_ARRAYS, nx, nz),
         in_specs=[near] * 3,
         out_specs=near,
         name="third_windows",
-    )(*rows_in)
+    )(keep(near_rows), keep(rim_rows), keep(swept))
+    far_rows = pl.pallas_call(
+        second_far,
+        out_shape=far_shape,
+        in_specs=[near] * 5,
+        out_specs=near,
+        name="second_far",
+    )(keep(swept), keep(one), keep(kept), keep(inner_near), keep(edge))
+    inner = (keep(inner_near), keep(third(SPLIT, far_rows)))
     far = pl.BlockSpec(memory_space=pltpu.HBM)
     whole = jax.ShapeDtypeStruct((5, nx * ny, nz), jnp.float32)
     scratch = [pltpu.VMEM(whole.shape, jnp.float32), pltpu.SemaphoreType.DMA((5,))]
     ends = pl.pallas_call(
         functools.partial(end_kernel, cols),
         out_shape=whole,
-        in_specs=[near] * 3,
+        in_specs=[near] * 4,
         out_specs=far,
         scratch_shapes=scratch,
         name="third_ends",
-    )(keep(inner), keep(edge), keep(one))
+    )(*inner, keep(edge), keep(col_one))
     out = pl.pallas_call(
         functools.partial(middle_kernel, cols),
         out_shape=whole,
-        in_specs=[far] + [near] * 4,
+        in_specs=[far] + [near] * 5,
         out_specs=far,
         input_output_aliases={0: 0},
         scratch_shapes=scratch,
         name="third_middle",
-    )(ends, keep(inner), keep(edge), keep(one), keep(two))
+    )(ends, *inner, keep(edge), keep(col_one), keep(two))
     return out.reshape(5, nx, ny, nz)
 
 

time: 12 us -> 11.7 us (0.975)
  the two profiles are of different devices: /device:TPU:1 before, /device:TPU:0 now
where the time goes in v10:
time: 11.7 us; the launch traced here: 11.5 us
  starting transfers between devices  6.36 us (54%)
  Pallas kernels  4.12 us (35%)
  waiting for transfers between devices  0.94 us (8%)
    ppermute x5, starting transfers between devices, body(): lax.ppermute(x, ('row', 'col'), swap_pairs(mesh, axis, inner))  6.36 us
    ppermute x5, waiting for transfers between devices, body(): lax.ppermute(x, ('row', 'col'), swap_pairs(mesh, axis, inner))  0.94 us
    pallas_call x1, Pallas kernels, body(): pl.pallas_call(functools.partial(end_kernel, cols), out_shape=whole, in_s...  0.93 us
    pallas_call x1, Pallas kernels, body(): pl.pallas_call(raw_kernel, out_shape=here(6, HALO, nx, nz), in_specs=[pl....  0.9 us
    pallas_call x2, Pallas kernels, third(): pl.pallas_call(functools.partial(third_kernel, first), out_shape=here(*ro...  0.85 us
    pallas_call x1, Pallas kernels, body(): pl.pallas_call(functools.partial(second_near, rows), out_shape=(here(5, S...  0.43 us
  transfers between devices with their start and end apart: 5, of which 2 were waited for; matrix products, arithmetic and copies ran while one was open for 0% of the time, Pallas kernels for 28%

profile of v10, /device:TPU:0, one launch (start us, length us, event | category | flops | bytes accessed | tf_op | source)
XLA Modules:
  0.0 11.5 jit_solution(2792998444505083802)
XLA Ops:
  0.0 0.0 copy-start
  0.0 0.0 copy-start.1
  0.0 0.9 %raw_edges.1 = f32[6,3,8,128]{3,2,1,0:T(8,128)S(1)} custom-call(f32[5,8,8,128]{3,2,1,0:T(8,128)} %state_hbm.1, f32[8,8,128]{2,1,0:T(8,128)} %gamma_hbm.1), custom_call_target="tpu_custom_call" | custom-call | tf_op jit(solution)/shard_map/raw_edges/pallas_call | solution.py:628
  0.9 0.5 %collective-permute-start = (f32[6,3,8,128]{3,2,1,0:T(8,128)S(1)}, f32[6,3,8,128]{3,2,1,0:T(8,128)S(1)}, u32[]{:S(2)}, u32[]{:S(2)}) collective-permute-start(f32[6,3,8,128]{3,2,1,0:T(8,128)S(1)} %raw_edges.1), channel_id=1, source_target_pairs={{0,1},{1,0},{2,3},{3,2},{4,8},{5,9},{6,10},{7,11},{8,4},{9,5},{10,... | collective-permute-start | bytes 221192 | tf_op jit(solution)/shard_map/ppermute | solution.py:626
  1.4 0.0 copy-done
  1.4 0.0 copy-done.1
  1.4 0.2 %edge_rows.1 = (f32[16,8,128]{2,1,0:T(8,128)S(1)}, f32[16,128]{1,0:T(8,128)S(1)}) custom-call(f32[5,64,128]{2,1,0:T(8,128)S(1)} %bitcast.4, f32[64,128]{1,0:T(8,128)S(1)} %bitcast.6), custom_call_target="tpu_custom_call" | custom-call | tf_op jit(solution)/shard_map/edge_rows/pallas_call | solution.py:638
  1.6 4.1 %collective-permute-start.2 = (f32[16,128]{1,0:T(8,128)S(1)}, f32[16,128]{1,0:T(8,128)S(1)}, u32[]{:S(2)}, u32[]{:S(2)}) collective-permute-start(f32[16,128]{1,0:T(8,128)S(1)} %get-tuple-element.17), channel_id=1, source_target_pairs={{0,4},{1,5},{2,6},{3,7},{4,0},{5,1},{6,2},{7,3},{8,12},{9,13},{10,... | collective-permute-start | bytes 24584 | tf_op jit(solution)/shard_map/ppermute | solution.py:626
  5.7 0.1 collective-permute-start.1
  5.8 0.2 %sweep_first.1.swept_ref.gamma_ref = f32[6,64,128]{2,1,0:T(8,128)S(1)} custom-call(f32[5,64,128]{2,1,0:T(8,128)S(1)} %bitcast.5, f32[64,128]{1,0:T(8,128)S(1)} %bitcast.7), custom_call_target="tpu_custom_call" | custom-call | tf_op jit(solution)/shard_map/sweep_first/pallas_call | solution.py:645
  6.0 0.0 collective-permute-done
  6.1 0.4 %second_near.1 = (f32[5,40,128]{2,1,0:T(8,128)S(1)}, f32[8,128]{1,0:T(8,128)S(1)}, f32[8,128]{1,0:T(8,128)S(1)}, f32[36,8,128]{2,1,0:T(8,128)S(1)}) custom-call(f32[6,64,128]{2,1,0:T(8,128)S(1)} %sweep_first.1.swept_ref.gamma_ref, f32[18,8,128]{2,1,0:T(8,128)S(1)} %bitcast.8), custom_call_target="tpu_custom_call" | custom-call | tf_op jit(solution)/shard_map/second_near/pallas_call | solution.py:654
  6.5 0.9 %collective-permute-done.2.rim_ref = f32[16,128]{1,0:T(8,128)S(1)} collective-permute-done((f32[16,128]{1,0:T(8,128)S(1)}, f32[16,128]{1,0:T(8,128)S(1)}, u32[]{:S(2)}, u32[]{:S(2)}) %collective-permute-start.2) | collective-permute-done | bytes 8224 | tf_op jit(solution)/shard_map/ppermute | solution.py:626
  7.4 0.2 %second_rim.1 = (f32[5,24,128]{2,1,0:T(8,128)S(1)}, f32[8,128]{1,0:T(8,128)S(1)}, f32[16,128]{1,0:T(8,128)S(1)}) custom-call(f32[6,64,128]{2,1,0:T(8,128)S(1)} %sweep_first.1.swept_ref.gamma_ref, f32[16,128]{1,0:T(8,128)S(1)} %collective-permute-done.2.rim_ref, f32[8,128]{1,0:T(8,128)S(1)} %get-tuple-element.18.lower_ref, ...), custom_call_target="tpu_custom_call" | custom-call | flops 1000000000 | tf_op jit(solution)/shard_map/second_rim/pallas_call | solution.py:662
  7.6 0.1 collective-permute-start.4
  7.7 1.6 %collective-permute-start.3 = (f32[8,128]{1,0:T(8,128)S(1)}, f32[8,128]{1,0:T(8,128)S(1)}, u32[]{:S(2)}, u32[]{:S(2)}) collective-permute-start(f32[8,128]{1,0:T(8,128)S(1)} %get-tuple-element.21), channel_id=1, source_target_pairs={{0,1},{1,0},{2,3},{3,2},{4,5},{5,4},{6,7},{7,6},{8,9},{9,8},{10,11... | collective-permute-start | bytes 12296 | tf_op jit(solution)/shard_map/ppermute | solution.py:626
  9.3 0.4 %third_near.1.others_0_.near_ref = f32[5,40,128]{2,1,0:T(8,128)S(1)} custom-call(f32[5,40,128]{2,1,0:T(8,128)S(1)} %get-tuple-element.14.rows_ref.near_ref, f32[6,64,128]{2,1,0:T(8,128)S(1)} %sweep_first.1.swept_ref.gamma_ref), custom_call_target="tpu_custom_call" | custom-call | tf_op jit(solution)/shard_map/third_near/pallas_call | solution.py:673
  9.7 0.2 %third_windows.1.others_1_.edge_ref = f32[43,8,128]{2,1,0:T(8,128)S(1)} custom-call(f32[5,40,128]{2,1,0:T(8,128)S(1)} %get-tuple-element.14.rows_ref.near_ref, f32[5,24,128]{2,1,0:T(8,128)S(1)} %get-tuple-element.20.far_ref, f32[6,64,128]{2,1,0:T(8,128)S(1)} %sweep_first.1.swept_ref.gamma_ref), custom_call_target="tpu_custom_call" | custom-call | tf_op jit(solution)/shard_map/third_windows/pallas_call | solution.py:682
  9.9 0.1 collective-permute-done.1.one_ref
  10.0 0.1 second_far.1.rows_ref
  10.1 0.4 %third_far.1.far_ref = f32[5,24,128]{2,1,0:T(8,128)S(1)} custom-call(f32[5,24,128]{2,1,0:T(8,128)S(1)} %second_far.1.rows_ref, f32[6,64,128]{2,1,0:T(8,128)S(1)} %sweep_first.1.swept_ref.gamma_ref), custom_call_target="tpu_custom_call" | custom-call | tf_op jit(solution)/shard_map/third_far/pallas_call | solution.py:673
  10.5 0.0 collective-permute-done.3.one_ref
  10.5 0.9 %third_ends.1.ends_ref = f32[5,64,128]{2,1,0:T(8,128)} custom-call(f32[5,40,128]{2,1,0:T(8,128)S(1)} %third_near.1.others_0_.near_ref, f32[5,24,128]{2,1,0:T(8,128)S(1)} %third_far.1.far_ref, f32[43,8,128]{2,1,0:T(8,128)S(1)} %third_windows.1.others_1_.edge_ref, f32[8,128]{1,0:T(8,128)S(1)} %collective-permute-done.3.one_ref), custom_call_target="tpu_custom_call" | custom-call | tf_op jit(solution)/shard_map/third_ends/pallas_call | solution.py:700
  11.5 0.0 collective-permute-done.4.two_ref
  11.5 0.1 third_middle.1
Async XLA Ops:
  0.0 1.4 %copy-start = (f32[5,8,8,128]{3,2,1,0:T(8,128)S(1)}, f32[5,8,8,128]{3,2,1,0:T(8,128)}, u32[]{:S(2)}) copy-start(f32[5,8,8,128]{3,2,1,0:T(8,128)} %state_hbm.1) | copy-start | bytes 491524
  0.0 1.4 %copy-start.1 = (f32[8,8,128]{2,1,0:T(8,128)S(1)}, f32[8,8,128]{2,1,0:T(8,128)}, u32[]{:S(2)}) copy-start(f32[8,8,128]{2,1,0:T(8,128)} %gamma_hbm.1) | copy-start | bytes 98308
  0.9 5.1 %collective-permute-start = (f32[6,3,8,128]{3,2,1,0:T(8,128)S(1)}, f32[6,3,8,128]{3,2,1,0:T(8,128)S(1)}, u32[]{:S(2)}, u32[]{:S(2)}) collective-permute-start(f32[6,3,8,128]{3,2,1,0:T(8,128)S(1)} %raw_edges.1), channel_id=1, source_target_pairs={{0,1},{1,0},{2,3},{3,2},{4,8},{5,9},{6,10},{7,11},{8,4},{9,5},{10,... | collective-permute-start | bytes 221192 | tf_op jit(solution)/shard_map/ppermute | solution.py:626
  1.6 5.7 %collective-permute-start.2 = (f32[16,128]{1,0:T(8,128)S(1)}, f32[16,128]{1,0:T(8,128)S(1)}, u32[]{:S(2)}, u32[]{:S(2)}) collective-permute-start(f32[16,128]{1,0:T(8,128)S(1)} %get-tuple-element.17), channel_id=1, source_target_pairs={{0,4},{1,5},{2,6},{3,7},{4,0},{5,1},{6,2},{7,3},{8,12},{9,13},{10,... | collective-permute-start | bytes 24584 | tf_op jit(solution)/shard_map/ppermute | solution.py:626
  5.7 4.3 %collective-permute-start.1 = (f32[16,8,128]{2,1,0:T(8,128)S(1)}, f32[16,8,128]{2,1,0:T(8,128)S(1)}, u32[]{:S(2)}, u32[]{:S(2)}) collective-permute-start(f32[16,8,128]{2,1,0:T(8,128)S(1)} %get-tuple-element.15), channel_id=1, source_target_pairs={{0,4},{1,5},{2,6},{3,7},{4,0},{5,1},{6,2},{7,3},{8,12},{9,13},{10,... | collective-permute-start | bytes 196616 | tf_op jit(solution)/shard_map/ppermute | solution.py:626
  7.6 3.9 %collective-permute-start.4 = (f32[16,128]{1,0:T(8,128)S(1)}, f32[16,128]{1,0:T(8,128)S(1)}, u32[]{:S(2)}, u32[]{:S(2)}) collective-permute-start(f32[16,128]{1,0:T(8,128)S(1)} %get-tuple-element.22), channel_id=1, source_target_pairs={{0,3},{1,2},{2,1},{3,0},{4,7},{5,6},{6,5},{7,4},{8,11},{9,10},{10,... | collective-permute-start | bytes 24584 | tf_op jit(solution)/shard_map/ppermute | solution.py:626
  7.7 2.8 %collective-permute-start.3 = (f32[8,128]{1,0:T(8,128)S(1)}, f32[8,128]{1,0:T(8,128)S(1)}, u32[]{:S(2)}, u32[]{:S(2)}) collective-permute-start(f32[8,128]{1,0:T(8,128)S(1)} %get-tuple-element.21), channel_id=1, source_target_pairs={{0,1},{1,0},{2,3},{3,2},{4,5},{5,4},{6,7},{7,6},{8,9},{9,8},{10,11... | collective-permute-start | bytes 12296 | tf_op jit(solution)/shard_map/ppermute | solution.py:626

commit v11 on v10

--- a/solution.py
+++ b/solution.py
@@ -424,27 +424,25 @@
         sweep_far(swept_ref, kept_ref, base, lambda n: one_ref[n, pl.ds(base, SUB), :], store)
 
 
+def turned(x, by):
+    by %= LANES
+    return pltpu.roll(x, LANES - by, 1) if by else x
+
+
 def sweep_lanes(cons, prim, gamma, normal):
-    def ahead(x):
-        return pltpu.roll(x, LANES - 1, 1)
-
-    def behind(x):
-        return pltpu.roll(x, 1, 1)
-
     inv_gam1 = recip(gamma - 1.0)
     upper, lower_next = [], []
     for q in prim:
-        here = ahead(q) - q
-        right = face_rise(behind(here), here, ahead(here))
-        left = behind(here - right)
-        up, low = edges(q, right, left)
-        upper.append(up)
-        lower_next.append(ahead(low))
+        line = [turned(q, k) for k in range(-2, 4)]
+        diff = [b - a for a, b in zip(line, line[1:])]
+        rise = [face_rise(*diff[k : k + 3]) for k in range(3)]
+        upper.append(q + clamp_zero(rise[1], 2.0 * (diff[1] - rise[0])))
+        lower_next.append(line[3] - clamp_zero(diff[2] - rise[1], 2.0 * rise[2]))
     flux = double_flux(
         state_flux(upper, gamma, inv_gam1),
-        state_flux(lower_next, ahead(gamma), ahead(inv_gam1)),
+        state_flux(lower_next, turned(gamma, 1), turned(inv_gam1, 1)),
     )
-    return updated(cons, flux, [behind(x) for x in flux], normal)
+    return updated(cons, flux, [turned(x, -1) for x in flux], normal)
 
 
 def sweep_lines(cons, lines, gammas, normal):
@@ -463,11 +461,6 @@
     before = double_flux(side[-1, 0], side[0, 0])
     after = double_flux(side[0, 1], side[1, 1])
     return updated(cons, after, before, normal)
-
-
-def turned(x, by):
-    by %= LANES
-    return pltpu.roll(x, LANES - by, 1) if by else x
 
 
 REACH = range(-HALO, HALO + 1)

time: 11.7 us -> 11.5 us (0.983)
  Pallas kernels: 4.12 us -> 3.93 us
    pallas_call x2, Pallas kernels: 0.85 us -> 0.65 us  [third(): pl.pallas_call(functools.partial(third_kernel, first), out_shape=here(*ro...]
  transfers between devices with their start and end apart: 5 -> 5, of which waited for: 2 -> 2; matrix products, arithmetic and copies ran while one was open for 0% -> 0% of each run, Pallas kernels for 28% -> 26%
where the time goes in v11:
time: 11.5 us; the launch traced here: 11.4 us
  starting transfers between devices  6.36 us (55%)
  Pallas kernels  3.93 us (34%)
  waiting for transfers between devices  1 us (9%)
    ppermute x5, starting transfers between devices, body(): lax.ppermute(x, ('row', 'col'), swap_pairs(mesh, axis, inner))  6.36 us
    ppermute x5, waiting for transfers between devices, body(): lax.ppermute(x, ('row', 'col'), swap_pairs(mesh, axis, inner))  1 us
    pallas_call x1, Pallas kernels, body(): pl.pallas_call(functools.partial(end_kernel, cols), out_shape=whole, in_s...  0.93 us
    pallas_call x1, Pallas kernels, body(): pl.pallas_call(raw_kernel, out_shape=here(6, HALO, nx, nz), in_specs=[pl....  0.9 us
    pallas_call x2, Pallas kernels, third(): pl.pallas_call(functools.partial(third_kernel, first), out_shape=here(*ro...  0.65 us
    pallas_call x1, Pallas kernels, body(): pl.pallas_call(functools.partial(second_near, rows), out_shape=(here(5, S...  0.43 us
    pallas_call x1, Pallas kernels, body(): pl.pallas_call(functools.partial(window_kernel, cols), out_shape=here(EDG...  0.23 us
  transfers between devices with their start and end apart: 5, of which 2 were waited for; matrix products, arithmetic and copies ran while one was open for 0% of the time, Pallas kernels for 26%

profile of v11, /device:TPU:0, one launch (start us, length us, event | category | flops | bytes accessed | tf_op | source)
XLA Modules:
  0.0 11.4 jit_solution(10873680656131071436)
XLA Ops:
  0.0 0.0 copy-start
  0.0 0.0 copy-start.1
  0.0 0.9 %raw_edges.1 = f32[6,3,8,128]{3,2,1,0:T(8,128)S(1)} custom-call(f32[5,8,8,128]{3,2,1,0:T(8,128)} %state_hbm.1, f32[8,8,128]{2,1,0:T(8,128)} %gamma_hbm.1), custom_call_target="tpu_custom_call" | custom-call | tf_op jit(solution)/shard_map/raw_edges/pallas_call | solution.py:621
  0.9 0.5 %collective-permute-start = (f32[6,3,8,128]{3,2,1,0:T(8,128)S(1)}, f32[6,3,8,128]{3,2,1,0:T(8,128)S(1)}, u32[]{:S(2)}, u32[]{:S(2)}) collective-permute-start(f32[6,3,8,128]{3,2,1,0:T(8,128)S(1)} %raw_edges.1), channel_id=1, source_target_pairs={{0,1},{1,0},{2,3},{3,2},{4,8},{5,9},{6,10},{7,11},{8,4},{9,5},{10,... | collective-permute-start | bytes 221192 | tf_op jit(solution)/shard_map/ppermute | solution.py:619
  1.4 0.0 copy-done
  1.4 0.0 copy-done.1
  1.4 0.2 %edge_rows.1 = (f32[16,8,128]{2,1,0:T(8,128)S(1)}, f32[16,128]{1,0:T(8,128)S(1)}) custom-call(f32[5,64,128]{2,1,0:T(8,128)S(1)} %bitcast.4, f32[64,128]{1,0:T(8,128)S(1)} %bitcast.6), custom_call_target="tpu_custom_call" | custom-call | tf_op jit(solution)/shard_map/edge_rows/pallas_call | solution.py:631
  1.6 4.1 %collective-permute-start.2 = (f32[16,128]{1,0:T(8,128)S(1)}, f32[16,128]{1,0:T(8,128)S(1)}, u32[]{:S(2)}, u32[]{:S(2)}) collective-permute-start(f32[16,128]{1,0:T(8,128)S(1)} %get-tuple-element.17), channel_id=1, source_target_pairs={{0,4},{1,5},{2,6},{3,7},{4,0},{5,1},{6,2},{7,3},{8,12},{9,13},{10,... | collective-permute-start | bytes 24584 | tf_op jit(solution)/shard_map/ppermute | solution.py:619
  5.7 0.1 collective-permute-start.1
  5.8 0.2 %sweep_first.1.swept_ref.gamma_ref = f32[6,64,128]{2,1,0:T(8,128)S(1)} custom-call(f32[5,64,128]{2,1,0:T(8,128)S(1)} %bitcast.5, f32[64,128]{1,0:T(8,128)S(1)} %bitcast.7), custom_call_target="tpu_custom_call" | custom-call | tf_op jit(solution)/shard_map/sweep_first/pallas_call | solution.py:638
  6.0 0.0 collective-permute-done
  6.1 0.4 %second_near.1 = (f32[5,40,128]{2,1,0:T(8,128)S(1)}, f32[8,128]{1,0:T(8,128)S(1)}, f32[8,128]{1,0:T(8,128)S(1)}, f32[36,8,128]{2,1,0:T(8,128)S(1)}) custom-call(f32[6,64,128]{2,1,0:T(8,128)S(1)} %sweep_first.1.swept_ref.gamma_ref, f32[18,8,128]{2,1,0:T(8,128)S(1)} %bitcast.8), custom_call_target="tpu_custom_call" | custom-call | tf_op jit(solution)/shard_map/second_near/pallas_call | solution.py:647
  6.5 0.9 %collective-permute-done.2.rim_ref = f32[16,128]{1,0:T(8,128)S(1)} collective-permute-done((f32[16,128]{1,0:T(8,128)S(1)}, f32[16,128]{1,0:T(8,128)S(1)}, u32[]{:S(2)}, u32[]{:S(2)}) %collective-permute-start.2) | collective-permute-done | bytes 8224 | tf_op jit(solution)/shard_map/ppermute | solution.py:619
  7.4 0.2 %second_rim.1 = (f32[5,24,128]{2,1,0:T(8,128)S(1)}, f32[8,128]{1,0:T(8,128)S(1)}, f32[16,128]{1,0:T(8,128)S(1)}) custom-call(f32[6,64,128]{2,1,0:T(8,128)S(1)} %sweep_first.1.swept_ref.gamma_ref, f32[16,128]{1,0:T(8,128)S(1)} %collective-permute-done.2.rim_ref, f32[8,128]{1,0:T(8,128)S(1)} %get-tuple-element.18.lower_ref, ...), custom_call_target="tpu_custom_call" | custom-call | flops 1000000000 | tf_op jit(solution)/shard_map/second_rim/pallas_call | solution.py:655
  7.6 0.1 collective-permute-start.4
  7.7 1.6 %collective-permute-start.3 = (f32[8,128]{1,0:T(8,128)S(1)}, f32[8,128]{1,0:T(8,128)S(1)}, u32[]{:S(2)}, u32[]{:S(2)}) collective-permute-start(f32[8,128]{1,0:T(8,128)S(1)} %get-tuple-element.21), channel_id=1, source_target_pairs={{0,1},{1,0},{2,3},{3,2},{4,5},{5,4},{6,7},{7,6},{8,9},{9,8},{10,11... | collective-permute-start | bytes 12296 | tf_op jit(solution)/shard_map/ppermute | solution.py:619
  9.3 0.4 %third_near.1.others_0_.near_ref = f32[5,40,128]{2,1,0:T(8,128)S(1)} custom-call(f32[5,40,128]{2,1,0:T(8,128)S(1)} %get-tuple-element.14.rows_ref.near_ref, f32[6,64,128]{2,1,0:T(8,128)S(1)} %sweep_first.1.swept_ref.gamma_ref), custom_call_target="tpu_custom_call" | custom-call | tf_op jit(solution)/shard_map/third_near/pallas_call | solution.py:666
  9.6 0.2 %third_windows.1.others_1_.edge_ref = f32[43,8,128]{2,1,0:T(8,128)S(1)} custom-call(f32[5,40,128]{2,1,0:T(8,128)S(1)} %get-tuple-element.14.rows_ref.near_ref, f32[5,24,128]{2,1,0:T(8,128)S(1)} %get-tuple-element.20.far_ref, f32[6,64,128]{2,1,0:T(8,128)S(1)} %sweep_first.1.swept_ref.gamma_ref), custom_call_target="tpu_custom_call" | custom-call | tf_op jit(solution)/shard_map/third_windows/pallas_call | solution.py:675
  9.9 0.1 %collective-permute-done.1.one_ref = f32[16,8,128]{2,1,0:T(8,128)S(1)} collective-permute-done((f32[16,8,128]{2,1,0:T(8,128)S(1)}, f32[16,8,128]{2,1,0:T(8,128)S(1)}, u32[]{:S(2)}, u32[]{:S(2)}) %collective-permute-start.1) | collective-permute-done | bytes 65568 | tf_op jit(solution)/shard_map/ppermute | solution.py:619
  10.0 0.1 second_far.1.rows_ref
  10.1 0.3 %third_far.1.far_ref = f32[5,24,128]{2,1,0:T(8,128)S(1)} custom-call(f32[5,24,128]{2,1,0:T(8,128)S(1)} %second_far.1.rows_ref, f32[6,64,128]{2,1,0:T(8,128)S(1)} %sweep_first.1.swept_ref.gamma_ref), custom_call_target="tpu_custom_call" | custom-call | tf_op jit(solution)/shard_map/third_far/pallas_call | solution.py:666
  10.4 0.0 collective-permute-done.3.one_ref
  10.4 0.9 %third_ends.1.ends_ref = f32[5,64,128]{2,1,0:T(8,128)} custom-call(f32[5,40,128]{2,1,0:T(8,128)S(1)} %third_near.1.others_0_.near_ref, f32[5,24,128]{2,1,0:T(8,128)S(1)} %third_far.1.far_ref, f32[43,8,128]{2,1,0:T(8,128)S(1)} %third_windows.1.others_1_.edge_ref, f32[8,128]{1,0:T(8,128)S(1)} %collective-permute-done.3.one_ref), custom_call_target="tpu_custom_call" | custom-call | tf_op jit(solution)/shard_map/third_ends/pallas_call | solution.py:693
  11.3 0.0 collective-permute-done.4.two_ref
  11.3 0.1 third_middle.1
Async XLA Ops:
  0.0 1.4 %copy-start = (f32[5,8,8,128]{3,2,1,0:T(8,128)S(1)}, f32[5,8,8,128]{3,2,1,0:T(8,128)}, u32[]{:S(2)}) copy-start(f32[5,8,8,128]{3,2,1,0:T(8,128)} %state_hbm.1) | copy-start | bytes 491524
  0.0 1.4 %copy-start.1 = (f32[8,8,128]{2,1,0:T(8,128)S(1)}, f32[8,8,128]{2,1,0:T(8,128)}, u32[]{:S(2)}) copy-start(f32[8,8,128]{2,1,0:T(8,128)} %gamma_hbm.1) | copy-start | bytes 98308
  0.9 5.1 %collective-permute-start = (f32[6,3,8,128]{3,2,1,0:T(8,128)S(1)}, f32[6,3,8,128]{3,2,1,0:T(8,128)S(1)}, u32[]{:S(2)}, u32[]{:S(2)}) collective-permute-start(f32[6,3,8,128]{3,2,1,0:T(8,128)S(1)} %raw_edges.1), channel_id=1, source_target_pairs={{0,1},{1,0},{2,3},{3,2},{4,8},{5,9},{6,10},{7,11},{8,4},{9,5},{10,... | collective-permute-start | bytes 221192 | tf_op jit(solution)/shard_map/ppermute | solution.py:619
  1.6 5.7 %collective-permute-start.2 = (f32[16,128]{1,0:T(8,128)S(1)}, f32[16,128]{1,0:T(8,128)S(1)}, u32[]{:S(2)}, u32[]{:S(2)}) collective-permute-start(f32[16,128]{1,0:T(8,128)S(1)} %get-tuple-element.17), channel_id=1, source_target_pairs={{0,4},{1,5},{2,6},{3,7},{4,0},{5,1},{6,2},{7,3},{8,12},{9,13},{10,... | collective-permute-start | bytes 24584 | tf_op jit(solution)/shard_map/ppermute | solution.py:619
  5.7 4.3 %collective-permute-start.1 = (f32[16,8,128]{2,1,0:T(8,128)S(1)}, f32[16,8,128]{2,1,0:T(8,128)S(1)}, u32[]{:S(2)}, u32[]{:S(2)}) collective-permute-start(f32[16,8,128]{2,1,0:T(8,128)S(1)} %get-tuple-element.15), channel_id=1, source_target_pairs={{0,4},{1,5},{2,6},{3,7},{4,0},{5,1},{6,2},{7,3},{8,12},{9,13},{10,... | collective-permute-start | bytes 196616 | tf_op jit(solution)/shard_map/ppermute | solution.py:619
  7.6 3.7 %collective-permute-start.4 = (f32[16,128]{1,0:T(8,128)S(1)}, f32[16,128]{1,0:T(8,128)S(1)}, u32[]{:S(2)}, u32[]{:S(2)}) collective-permute-start(f32[16,128]{1,0:T(8,128)S(1)} %get-tuple-element.22), channel_id=1, source_target_pairs={{0,3},{1,2},{2,1},{3,0},{4,7},{5,6},{6,5},{7,4},{8,11},{9,10},{10,... | collective-permute-start | bytes 24584 | tf_op jit(solution)/shard_map/ppermute | solution.py:619
  7.7 2.7 %collective-permute-start.3 = (f32[8,128]{1,0:T(8,128)S(1)}, f32[8,128]{1,0:T(8,128)S(1)}, u32[]{:S(2)}, u32[]{:S(2)}) collective-permute-start(f32[8,128]{1,0:T(8,128)S(1)} %get-tuple-element.21), channel_id=1, source_target_pairs={{0,1},{1,0},{2,3},{3,2},{4,5},{5,4},{6,7},{7,6},{8,9},{9,8},{10,11... | collective-permute-start | bytes 12296 | tf_op jit(solution)/shard_map/ppermute | solution.py:619

commit v12 on v11

--- a/solution.py
+++ b/solution.py
@@ -89,6 +89,7 @@
         self.n, self.normal = n, normal
         self.load, self.load_gamma, self.halo = load, load_gamma, halo
         self.cons, self.gam, self.prim, self.diff, self.rise, self.state = {}, {}, {}, {}, {}, {}
+        self.flux = {}
 
     def zone(self, i):
         return i if self.halo else min(max(i, 0), self.n - 1)
@@ -140,6 +141,8 @@
         return self.state[i, upper]
 
     def face(self, i):
+        if i in self.flux:
+            return self.flux[i]
         if not self.halo and i < 0:
             return double_flux(self.get_state(0, True), self.get_state(0, True))
         if not self.halo and i == self.n - 1:
@@ -308,18 +311,64 @@
 
 
 SPLIT = 5
-
-
-def kept_arrays(sweep, flux):
+INNER = 3
+
+
+def far_arrays(sweep):
     cons, fluxes, speed = sweep.get_state(SPLIT, True)
     kept = [sweep.get(SPLIT + 1), sweep.get(SPLIT + 2), sweep.get_diff(SPLIT)]
-    return sum(kept + [sweep.get_rise(SPLIT)[1], cons, fluxes, [speed], flux], [])
-
-
-KEPT = 36
-
-
-def second_near(rows, swept_ref, two_ref, next_ref, lower_ref, upper_ref, kept_ref):
+    return sum(kept + [sweep.get_rise(SPLIT)[1], cons, fluxes, [speed], sweep.face(SPLIT - 1)], [])
+
+
+def near_arrays(sweep):
+    last = INNER - 1
+    cons, fluxes, speed = sweep.get_state(last, False)
+    kept = [sweep.get(last - 2), sweep.get(last - 1), sweep.get_diff(last - 2)]
+    kept += [sweep.get_diff(last - 1), sweep.get_rise(last - 1)[0]]
+    return sum(kept + [cons, fluxes, [speed], sweep.face(last)], [])
+
+
+KEPT_FAR, KEPT_NEAR = 36, 41
+
+
+def inner_kernel(swept_ref, next_ref, lower_ref, upper_ref, near_ref, far_ref):
+    nx = swept_ref.shape[1] // SUB
+    sign = own_sign()
+    for base in range(0, nx, SUB):
+        at = pl.ds(base, SUB)
+        load, load_gamma = row_loads(swept_ref, base, nx, sign)
+        pack = EdgePack()
+
+        def store(y, cons):
+            cons[2] = cons[2] * sign
+            for f in range(5):
+                next_ref[f, pl.ds((y - INNER) * nx + base, SUB), :] = cons[f]
+            pack.add(y, cons, load_gamma(y))
+
+        sweep = Sweep(SUB, 1, load, load_gamma, lambda y: None)
+        for i in range(INNER - 1, SPLIT):
+            sweep.flux[i] = sweep.face(i)
+        sweep.run(range(INNER, SPLIT), store)
+        lower_ref[at, :], upper_ref[at, :] = pack.pack
+        for ref, kept in ((near_ref, near_arrays(sweep)), (far_ref, far_arrays(sweep))):
+            assert len(kept) == ref.shape[0]
+            for k, value in enumerate(kept):
+                ref[k, at, :] = value
+
+
+def second_near(
+    rows,
+    swept_ref,
+    two_ref,
+    inner_ref,
+    lower_in,
+    upper_in,
+    kept_ref,
+    ahead_ref,
+    next_ref,
+    lower_ref,
+    upper_ref,
+):
     nx = swept_ref.shape[1] // SUB
     row = lax.axis_index("row")
     end = (row == 0) | (row == rows - 1)
@@ -334,7 +383,8 @@
     for base in range(0, nx, SUB):
         at = pl.ds(base, SUB)
         load, load_own_gamma = row_loads(swept_ref, base, nx, sign)
-        pack = EdgePack()
+        pack = EdgePack(lower_in[at, :], upper_in[at, :])
+        kept = [kept_ref[k, at, :] for k in range(KEPT_NEAR)]
 
         def load_gamma(y):
             if y >= 0:
@@ -344,7 +394,7 @@
         def halo(y):
             got = list(halos[-1 - y][base // SUB])
             got[1] = got[1] * sign
-            return [jnp.where(end, p, q) for p, q in zip(sweep.get(0), got)]
+            return [jnp.where(end, p, q) for p, q in zip(kept[0:5], got)]
 
         def store(y, cons):
             cons[2] = cons[2] * sign
@@ -352,13 +402,19 @@
                 next_ref[f, pl.ds(y * nx + base, SUB), :] = cons[f]
             pack.add(y, cons, load_own_gamma(y))
 
+        last = INNER - 1
         sweep = Sweep(SUB, 1, load, load_gamma, halo)
-        flux = sweep.run(range(SPLIT), store)
+        sweep.prim[last - 2], sweep.prim[last - 1] = kept[0:5], kept[5:10]
+        sweep.diff[last - 2], sweep.diff[last - 1] = kept[10:15], kept[15:20]
+        sweep.rise[last - 1] = (kept[20:25], None)
+        sweep.state[last, False] = (kept[25:30], kept[30:35], kept[35])
+        sweep.flux[last] = kept[36:41]
+        sweep.run(range(INNER), store)
         lower_ref[at, :], upper_ref[at, :] = pack.pack
-        kept = kept_arrays(sweep, flux)
-        assert len(kept) == KEPT
-        for k in range(KEPT):
-            kept_ref[k, at, :] = kept[k]
+        for f in range(5):
+            for y in range(SPLIT - INNER):
+                at_row = pl.ds(y * nx + base, SUB)
+                next_ref[f, pl.ds((y + INNER) * nx + base, SUB), :] = inner_ref[f, at_row, :]
 
 
 def sweep_far(swept_ref, kept_ref, base, received, store):
@@ -379,7 +435,7 @@
         cons[2] = cons[2] * sign
         store(y, cons, load_own_gamma(y))
 
-    kept = [kept_ref[k, at, :] for k in range(KEPT)]
+    kept = [kept_ref[k, at, :] for k in range(KEPT_FAR)]
     sweep = Sweep(SUB, 1, load, load_gamma, halo)
     sweep.prim[SPLIT + 1], sweep.prim[SPLIT + 2] = kept[0:5], kept[5:10]
     sweep.diff[SPLIT] = kept[10:15]
@@ -485,10 +541,10 @@
     return load
 
 
-def third_kernel(first, rows_ref, gamma_ref, out_ref):
+def third_kernel(first, count, rows_ref, gamma_ref, out_ref):
     nx = gamma_ref.shape[1] // SUB
     for base in range(0, nx, SUB):
-        for y in range(rows_ref.shape[1] // nx):
+        for y in range(count):
             at = pl.ds(y * nx + base, SUB)
             cons = [rows_ref[f, at, :] for f in range(5)]
             gamma = gamma_ref[5, rows_at(first + y, base, nx), :]
@@ -526,7 +582,7 @@
             edge_ref[LINES + 3 + f, at, :] = windows[6 + f]
 
 
-def mend_edges(cols, near_ref, far_ref, edge_ref, one_ref, two_ref, out_ref, held, sems):
+def mend_edges(cols, near_ref, inner_ref, far_ref, edge_ref, one_ref, two_ref, out_ref, held, sems):
     nx = edge_ref.shape[1]
     ny = SUB
     odd = lax.rem(lax.axis_index("col"), 2) == 1
@@ -560,7 +616,12 @@
             for y in range(ny):
                 edge = turned(new[f], GROUP * y + 6)
                 at = pl.ds(tile * SUB * ny + own_row(y), SUB, stride=ny)
-                rows_ref, start = (near_ref, y) if y < SPLIT else (far_ref, y - SPLIT)
+                if y < INNER:
+                    rows_ref, start = near_ref, y
+                elif y < SPLIT:
+                    rows_ref, start = inner_ref, y - INNER
+                else:
+                    rows_ref, start = far_ref, y - SPLIT
                 inner = rows_ref[f, pl.ds(start * nx + tile * SUB, SUB), :]
                 held[f, at, :] = jnp.where(at_edge, edge, inner)
         copy = pltpu.make_async_copy(held.at[f], out_ref.at[f], sems.at[f])
@@ -575,18 +636,22 @@
     return (col == 0) | (col == cols - 1)
 
 
-def end_kernel(cols, near_ref, far_ref, edge_ref, one_ref, out_ref, held, sems):
+def end_kernel(cols, near_ref, inner_ref, far_ref, edge_ref, one_ref, out_ref, held, sems):
     @pl.when(at_end(cols))
     def _():
-        mend_edges(cols, near_ref, far_ref, edge_ref, one_ref, one_ref, out_ref, held, sems)
+        mend_edges(
+            cols, near_ref, inner_ref, far_ref, edge_ref, one_ref, one_ref, out_ref, held, sems
+        )
 
 
 def middle_kernel(
-    cols, ends_ref, near_ref, far_ref, edge_ref, one_ref, two_ref, out_ref, held, sems
+    cols, ends_ref, near_ref, inner_ref, far_ref, edge_ref, one_ref, two_ref, out_ref, held, sems
 ):
     @pl.when(jnp.logical_not(at_end(cols)))
     def _():
-        mend_edges(cols, near_ref, far_ref, edge_ref, one_ref, two_ref, out_ref, held, sems)
+        mend_edges(
+            cols, near_ref, inner_ref, far_ref, edge_ref, one_ref, two_ref, out_ref, held, sems
+        )
 
 
 def swap_pairs(mesh, axis, inner):
@@ -644,13 +709,45 @@
     )(*held)
     rim = swap(rim, "row", False)
     one = swap(one, "row", False)
-    near_rows, lower, upper, kept = pl.pallas_call(
+    inner_rows, lower, upper, kept_near, kept = pl.pallas_call(
+        inner_kernel,
+        out_shape=(
+            here(5, (SPLIT - INNER) * nx, nz),
+            here(nx, nz),
+            here(nx, nz),
+            here(KEPT_NEAR, nx, nz),
+            here(KEPT_FAR, nx, nz),
+        ),
+        in_specs=[near],
+        out_specs=(near,) * 5,
+        name="second_inner",
+    )(keep(swept))
+
+    def third(first, count, rows_in, name):
+        return pl.pallas_call(
+            functools.partial(third_kernel, first, count),
+            out_shape=here(5, count * nx, nz),
+            in_specs=[near] * 2,
+            out_specs=near,
+            name=name,
+        )(keep(rows_in), keep(swept))
+
+    inner_z = third(INNER, SPLIT - INNER, inner_rows, "third_inner")
+    near_rows, lower, upper = pl.pallas_call(
         functools.partial(second_near, rows),
-        out_shape=(here(5, SPLIT * nx, nz), here(nx, nz), here(nx, nz), here(KEPT, nx, nz)),
-        in_specs=[near] * 2,
-        out_specs=(near,) * 4,
+        out_shape=(here(5, SPLIT * nx, nz), here(nx, nz), here(nx, nz)),
+        in_specs=[near] * 7,
+        out_specs=(near,) * 3,
         name="second_near",
-    )(keep(swept), keep(two))
+    )(
+        keep(swept),
+        keep(two),
+        keep(inner_rows),
+        keep(lower),
+        keep(upper),
+        keep(kept_near),
+        keep(inner_z),
+    )
     far_shape = here(5, (ny - SPLIT) * nx, nz)
     rim_rows, to_one, to_two = pl.pallas_call(
         rim_kernel,
@@ -662,16 +759,7 @@
     )(keep(swept), keep(rim), keep(lower), keep(upper), keep(kept))
     two = swap(to_two, "col", True)
     col_one = swap(to_one, "col", False)
-    def third(first, rows_in):
-        return pl.pallas_call(
-            functools.partial(third_kernel, first),
-            out_shape=here(*rows_in.shape),
-            in_specs=[near] * 2,
-            out_specs=near,
-            name="third_far" if first else "third_near",
-        )(keep(rows_in), keep(swept))
-
-    inner_near = third(0, near_rows)
+    inner_near = third(0, INNER, near_rows, "third_near")
     edge = pl.pallas_call(
         functools.partial(window_kernel, cols),
         out_shape=here(EDGE_ARRAYS, nx, nz),
@@ -686,14 +774,14 @@
         out_specs=near,
         name="second_far",
     )(keep(swept), keep(one), keep(kept), keep(inner_near), keep(edge))
-    inner = (keep(inner_near), keep(third(SPLIT, far_rows)))
+    inner = (keep(inner_near), keep(inner_z), keep(third(SPLIT, ny - SPLIT, far_rows, "third_far")))
     far = pl.BlockSpec(memory_space=pltpu.HBM)
     whole = jax.ShapeDtypeStruct((5, nx * ny, nz), jnp.float32)
     scratch = [pltpu.VMEM(whole.shape, jnp.float32), pltpu.SemaphoreType.DMA((5,))]
     ends = pl.pallas_call(
         functools.partial(end_kernel, cols),
         out_shape=whole,
-        in_specs=[near] * 4,
+        in_specs=[near] * 5,
         out_specs=far,
         scratch_shapes=scratch,
         name="third_ends",
@@ -701,7 +789,7 @@
     out = pl.pallas_call(
         functools.partial(middle_kernel, cols),
         out_shape=whole,
-        in_specs=[far] + [near] * 5,
+        in_specs=[far] + [near] * 6,
         out_specs=far,
         input_output_aliases={0: 0},
         scratch_shapes=scratch,

time: 11.5 us -> 11.5 us (level)
  waiting for transfers between devices: 1 us -> 0.77 us
  Pallas kernels: 3.93 us -> 4.15 us
    pallas_call x2 -> x4, Pallas kernels: 0.65 us -> 1.01 us  [the longest x3 0.82 us: third(): pl.pallas_call(functools.partial(third_kernel, first, count), out_shape=h...]
    ppermute x5, waiting for transfers between devices: 1 us -> 0.77 us  [body(): lax.ppermute(x, ('row', 'col'), swap_pairs(mesh, axis, inner))]
    pallas_call x1, Pallas kernels: 0.43 us -> 0.29 us  [body(): pl.pallas_call(functools.partial(second_near, rows), out_shape=(here(5, S...]
  transfers between devices with their start and end apart: 5 -> 5, of which waited for: 2 -> 2; matrix products, arithmetic and copies ran while one was open for 0% -> 0% of each run, Pallas kernels for 26% -> 28%
where the time goes in v12:
time: 11.5 us; the launch traced here: 11.4 us
  starting transfers between devices  6.36 us (55%)
  Pallas kernels  4.15 us (36%)
  waiting for transfers between devices  0.77 us (7%)
    ppermute x5, starting transfers between devices, body(): lax.ppermute(x, ('row', 'col'), swap_pairs(mesh, axis, inner))  6.36 us
    pallas_call x1, Pallas kernels, body(): pl.pallas_call(functools.partial(end_kernel, cols), out_shape=whole, in_s...  0.93 us
    pallas_call x1, Pallas kernels, body(): pl.pallas_call(raw_kernel, out_shape=here(6, HALO, nx, nz), in_specs=[pl....  0.9 us
    pallas_call x3, Pallas kernels, third(): pl.pallas_call(functools.partial(third_kernel, first, count), out_shape=h...  0.82 us
    ppermute x5, waiting for transfers between devices, body(): lax.ppermute(x, ('row', 'col'), swap_pairs(mesh, axis, inner))  0.77 us
    pallas_call x1, Pallas kernels, body(): pl.pallas_call(functools.partial(second_near, rows), out_shape=(here(5, S...  0.29 us
    pallas_call x1, Pallas kernels, body(): pl.pallas_call(functools.partial(window_kernel, cols), out_shape=here(EDG...  0.23 us
  transfers between devices with their start and end apart: 5, of which 2 were waited for; matrix products, arithmetic and copies ran while one was open for 0% of the time, Pallas kernels for 28%

profile of v12, /device:TPU:0, one launch (start us, length us, event | category | flops | bytes accessed | tf_op | source)
XLA Modules:
  0.0 11.4 jit_solution(14219727970478532867)
XLA Ops:
  0.0 0.0 copy-start
  0.0 0.0 copy-start.1
  0.0 0.9 %raw_edges.1 = f32[6,3,8,128]{3,2,1,0:T(8,128)S(1)} custom-call(f32[5,8,8,128]{3,2,1,0:T(8,128)} %state_hbm.1, f32[8,8,128]{2,1,0:T(8,128)} %gamma_hbm.1), custom_call_target="tpu_custom_call" | custom-call | tf_op jit(solution)/shard_map/raw_edges/pallas_call | solution.py:686
  0.9 0.5 %collective-permute-start = (f32[6,3,8,128]{3,2,1,0:T(8,128)S(1)}, f32[6,3,8,128]{3,2,1,0:T(8,128)S(1)}, u32[]{:S(2)}, u32[]{:S(2)}) collective-permute-start(f32[6,3,8,128]{3,2,1,0:T(8,128)S(1)} %raw_edges.1), channel_id=1, source_target_pairs={{0,1},{1,0},{2,3},{3,2},{4,8},{5,9},{6,10},{7,11},{8,4},{9,5},{10,... | collective-permute-start | bytes 221192 | tf_op jit(solution)/shard_map/ppermute | solution.py:684
  1.4 0.0 copy-done
  1.4 0.0 copy-done.1
  1.4 0.2 %edge_rows.1 = (f32[16,8,128]{2,1,0:T(8,128)S(1)}, f32[16,128]{1,0:T(8,128)S(1)}) custom-call(f32[5,64,128]{2,1,0:T(8,128)S(1)} %bitcast.4, f32[64,128]{1,0:T(8,128)S(1)} %bitcast.6), custom_call_target="tpu_custom_call" | custom-call | tf_op jit(solution)/shard_map/edge_rows/pallas_call | solution.py:696
  1.6 4.1 %collective-permute-start.2 = (f32[16,128]{1,0:T(8,128)S(1)}, f32[16,128]{1,0:T(8,128)S(1)}, u32[]{:S(2)}, u32[]{:S(2)}) collective-permute-start(f32[16,128]{1,0:T(8,128)S(1)} %get-tuple-element.25), channel_id=1, source_target_pairs={{0,4},{1,5},{2,6},{3,7},{4,0},{5,1},{6,2},{7,3},{8,12},{9,13},{10,... | collective-permute-start | bytes 24584 | tf_op jit(solution)/shard_map/ppermute | solution.py:684
  5.7 0.1 collective-permute-start.1
  5.8 0.2 %sweep_first.1.swept_ref.gamma_ref = f32[6,64,128]{2,1,0:T(8,128)S(1)} custom-call(f32[5,64,128]{2,1,0:T(8,128)S(1)} %bitcast.5, f32[64,128]{1,0:T(8,128)S(1)} %bitcast.7), custom_call_target="tpu_custom_call" | custom-call | tf_op jit(solution)/shard_map/sweep_first/pallas_call | solution.py:703
  6.0 0.2 %second_inner.1 = (f32[5,16,128]{2,1,0:T(8,128)S(1)}, f32[8,128]{1,0:T(8,128)S(1)}, f32[8,128]{1,0:T(8,128)S(1)}, f32[41,8,128]{2,1,0:T(8,128)S(1)}, f32[36,8,128]{2,1,0:T(8,128)S(1)}) custom-call(f32[6,64,128]{2,1,0:T(8,128)S(1)} %sweep_first.1.swept_ref.gamma_ref), custom_call_target="tpu_custom_call" | custom-call | tf_op jit(solution)/shard_map/second_inner/pallas_call | solution.py:712
  6.2 0.3 %third_inner.1.ahead_ref.inner_ref = f32[5,16,128]{2,1,0:T(8,128)S(1)} custom-call(f32[5,16,128]{2,1,0:T(8,128)S(1)} %get-tuple-element.18.rows_ref.inner_ref, f32[6,64,128]{2,1,0:T(8,128)S(1)} %sweep_first.1.swept_ref.gamma_ref), custom_call_target="tpu_custom_call" | custom-call | tf_op jit(solution)/shard_map/third_inner/pallas_call | solution.py:727
  6.5 0.0 collective-permute-done
  6.5 0.3 %second_near.1 = (f32[5,40,128]{2,1,0:T(8,128)S(1)}, f32[8,128]{1,0:T(8,128)S(1)}, f32[8,128]{1,0:T(8,128)S(1)}) custom-call(f32[6,64,128]{2,1,0:T(8,128)S(1)} %sweep_first.1.swept_ref.gamma_ref, f32[18,8,128]{2,1,0:T(8,128)S(1)} %bitcast.8, f32[5,16,128]{2,1,0:T(8,128)S(1)} %get-tuple-element.18.rows_ref.inner_ref, ...), custom_call_target="tpu_custom_call" | custom-call | tf_op jit(solution)/shard_map/second_near/pallas_call | solution.py:736
  6.8 0.6 %collective-permute-done.2.rim_ref = f32[16,128]{1,0:T(8,128)S(1)} collective-permute-done((f32[16,128]{1,0:T(8,128)S(1)}, f32[16,128]{1,0:T(8,128)S(1)}, u32[]{:S(2)}, u32[]{:S(2)}) %collective-permute-start.2) | collective-permute-done | bytes 8224 | tf_op jit(solution)/shard_map/ppermute | solution.py:684
  7.4 0.2 %second_rim.1 = (f32[5,24,128]{2,1,0:T(8,128)S(1)}, f32[8,128]{1,0:T(8,128)S(1)}, f32[16,128]{1,0:T(8,128)S(1)}) custom-call(f32[6,64,128]{2,1,0:T(8,128)S(1)} %sweep_first.1.swept_ref.gamma_ref, f32[16,128]{1,0:T(8,128)S(1)} %collective-permute-done.2.rim_ref, f32[8,128]{1,0:T(8,128)S(1)} %get-tuple-element.26.lower_ref, ...), custom_call_target="tpu_custom_call" | custom-call | flops 1000000000 | tf_op jit(solution)/shard_map/second_rim/pallas_call | solution.py:752
  7.6 0.1 collective-permute-start.4
  7.7 1.6 %collective-permute-start.3 = (f32[8,128]{1,0:T(8,128)S(1)}, f32[8,128]{1,0:T(8,128)S(1)}, u32[]{:S(2)}, u32[]{:S(2)}) collective-permute-start(f32[8,128]{1,0:T(8,128)S(1)} %get-tuple-element.29), channel_id=1, source_target_pairs={{0,1},{1,0},{2,3},{3,2},{4,5},{5,4},{6,7},{7,6},{8,9},{9,8},{10,11... | collective-permute-start | bytes 12296 | tf_op jit(solution)/shard_map/ppermute | solution.py:684
  9.3 0.3 %third_near.1.others_0_.near_ref = f32[5,24,128]{2,1,0:T(8,128)S(1)} custom-call(f32[5,40,128]{2,1,0:T(8,128)S(1)} %get-tuple-element.22.rows_ref.near_ref, f32[6,64,128]{2,1,0:T(8,128)S(1)} %sweep_first.1.swept_ref.gamma_ref), custom_call_target="tpu_custom_call" | custom-call | tf_op jit(solution)/shard_map/third_near/pallas_call | solution.py:727
  9.5 0.2 %third_windows.1.others_1_.edge_ref = f32[43,8,128]{2,1,0:T(8,128)S(1)} custom-call(f32[5,40,128]{2,1,0:T(8,128)S(1)} %get-tuple-element.22.rows_ref.near_ref, f32[5,24,128]{2,1,0:T(8,128)S(1)} %get-tuple-element.28.far_ref, f32[6,64,128]{2,1,0:T(8,128)S(1)} %sweep_first.1.swept_ref.gamma_ref), custom_call_target="tpu_custom_call" | custom-call | tf_op jit(solution)/shard_map/third_windows/pallas_call | solution.py:763
  9.8 0.2 %collective-permute-done.1.one_ref = f32[16,8,128]{2,1,0:T(8,128)S(1)} collective-permute-done((f32[16,8,128]{2,1,0:T(8,128)S(1)}, f32[16,8,128]{2,1,0:T(8,128)S(1)}, u32[]{:S(2)}, u32[]{:S(2)}) %collective-permute-start.1) | collective-permute-done | bytes 65568 | tf_op jit(solution)/shard_map/ppermute | solution.py:684
  10.0 0.1 second_far.1.rows_ref
  10.1 0.3 %third_far.1.far_ref = f32[5,24,128]{2,1,0:T(8,128)S(1)} custom-call(f32[5,24,128]{2,1,0:T(8,128)S(1)} %second_far.1.rows_ref, f32[6,64,128]{2,1,0:T(8,128)S(1)} %sweep_first.1.swept_ref.gamma_ref), custom_call_target="tpu_custom_call" | custom-call | tf_op jit(solution)/shard_map/third_far/pallas_call | solution.py:727
  10.4 0.0 collective-permute-done.3.one_ref
  10.4 0.9 %third_ends.1.ends_ref = f32[5,64,128]{2,1,0:T(8,128)} custom-call(f32[5,24,128]{2,1,0:T(8,128)S(1)} %third_near.1.others_0_.near_ref, f32[5,16,128]{2,1,0:T(8,128)S(1)} %third_inner.1.ahead_ref.inner_ref, f32[5,24,128]{2,1,0:T(8,128)S(1)} %third_far.1.far_ref, f32[43,8,128]{2,1,0:T(8,128)S(1)} %third_windows.1.others_1_.edge_ref, ...), custom_call_target="tpu_custom_call" | custom-call | tf_op jit(solution)/shard_map/third_ends/pallas_call | solution.py:781
  11.3 0.0 collective-permute-done.4.two_ref
  11.3 0.1 third_middle.1
Async XLA Ops:
  0.0 1.4 %copy-start = (f32[5,8,8,128]{3,2,1,0:T(8,128)S(1)}, f32[5,8,8,128]{3,2,1,0:T(8,128)}, u32[]{:S(2)}) copy-start(f32[5,8,8,128]{3,2,1,0:T(8,128)} %state_hbm.1) | copy-start | bytes 491524
  0.0 1.4 %copy-start.1 = (f32[8,8,128]{2,1,0:T(8,128)S(1)}, f32[8,8,128]{2,1,0:T(8,128)}, u32[]{:S(2)}) copy-start(f32[8,8,128]{2,1,0:T(8,128)} %gamma_hbm.1) | copy-start | bytes 98308
  0.9 5.6 %collective-permute-start = (f32[6,3,8,128]{3,2,1,0:T(8,128)S(1)}, f32[6,3,8,128]{3,2,1,0:T(8,128)S(1)}, u32[]{:S(2)}, u32[]{:S(2)}) collective-permute-start(f32[6,3,8,128]{3,2,1,0:T(8,128)S(1)} %raw_edges.1), channel_id=1, source_target_pairs={{0,1},{1,0},{2,3},{3,2},{4,8},{5,9},{6,10},{7,11},{8,4},{9,5},{10,... | collective-permute-start | bytes 221192 | tf_op jit(solution)/shard_map/ppermute | solution.py:684
  1.6 5.7 %collective-permute-start.2 = (f32[16,128]{1,0:T(8,128)S(1)}, f32[16,128]{1,0:T(8,128)S(1)}, u32[]{:S(2)}, u32[]{:S(2)}) collective-permute-start(f32[16,128]{1,0:T(8,128)S(1)} %get-tuple-element.25), channel_id=1, source_target_pairs={{0,4},{1,5},{2,6},{3,7},{4,0},{5,1},{6,2},{7,3},{8,12},{9,13},{10,... | collective-permute-start | bytes 24584 | tf_op jit(solution)/shard_map/ppermute | solution.py:684
  5.7 4.3 %collective-permute-start.1 = (f32[16,8,128]{2,1,0:T(8,128)S(1)}, f32[16,8,128]{2,1,0:T(8,128)S(1)}, u32[]{:S(2)}, u32[]{:S(2)}) collective-permute-start(f32[16,8,128]{2,1,0:T(8,128)S(1)} %get-tuple-element.23), channel_id=1, source_target_pairs={{0,4},{1,5},{2,6},{3,7},{4,0},{5,1},{6,2},{7,3},{8,12},{9,13},{10,... | collective-permute-start | bytes 196616 | tf_op jit(solution)/shard_map/ppermute | solution.py:684
  7.6 3.7 %collective-permute-start.4 = (f32[16,128]{1,0:T(8,128)S(1)}, f32[16,128]{1,0:T(8,128)S(1)}, u32[]{:S(2)}, u32[]{:S(2)}) collective-permute-start(f32[16,128]{1,0:T(8,128)S(1)} %get-tuple-element.30), channel_id=1, source_target_pairs={{0,3},{1,2},{2,1},{3,0},{4,7},{5,6},{6,5},{7,4},{8,11},{9,10},{10,... | collective-permute-start | bytes 24584 | tf_op jit(solution)/shard_map/ppermute | solution.py:684
  7.7 2.7 %collective-permute-start.3 = (f32[8,128]{1,0:T(8,128)S(1)}, f32[8,128]{1,0:T(8,128)S(1)}, u32[]{:S(2)}, u32[]{:S(2)}) collective-permute-start(f32[8,128]{1,0:T(8,128)S(1)} %get-tuple-element.29), channel_id=1, source_target_pairs={{0,1},{1,0},{2,3},{3,2},{4,5},{5,4},{6,7},{7,6},{8,9},{9,8},{10,11... | collective-permute-start | bytes 12296 | tf_op jit(solution)/shard_map/ppermute | solution.py:684

commit v13 on v12

--- a/solution.py
+++ b/solution.py
@@ -474,8 +474,9 @@
     for base in range(0, nx, SUB):
 
         def store(y, cons, gamma):
+            inner = sweep_lanes(cons, primitives(cons, gamma - 1.0, 2), gamma, 2)
             for f in range(5):
-                next_ref[f, pl.ds((y - SPLIT) * nx + base, SUB), :] = cons[f]
+                next_ref[f, pl.ds((y - SPLIT) * nx + base, SUB), :] = inner[f]
 
         sweep_far(swept_ref, kept_ref, base, lambda n: one_ref[n, pl.ds(base, SUB), :], store)
 
@@ -774,7 +775,7 @@
         out_specs=near,
         name="second_far",
     )(keep(swept), keep(one), keep(kept), keep(inner_near), keep(edge))
-    inner = (keep(inner_near), keep(inner_z), keep(third(SPLIT, ny - SPLIT, far_rows, "third_far")))
+    inner = (keep(inner_near), keep(inner_z), keep(far_rows))
     far = pl.BlockSpec(memory_space=pltpu.HBM)
     whole = jax.ShapeDtypeStruct((5, nx * ny, nz), jnp.float32)
     scratch = [pltpu.VMEM(whole.shape, jnp.float32), pltpu.SemaphoreType.DMA((5,))]

time: 11.5 us -> 11.5 us (level)
    pallas_call x3 -> x2, Pallas kernels: 0.82 us -> 0.54 us  [third(): pl.pallas_call(functools.partial(third_kernel, first, count), out_shape=h...]
    pallas_call x1, Pallas kernels: 0.09 us -> 0.3 us  [body(): pl.pallas_call(second_far, out_shape=far_shape, in_specs=[near] * 5, out_...]
where the time goes in v13:
time: 11.5 us; the launch traced here: 11.3 us
  starting transfers between devices  6.36 us (55%)
  Pallas kernels  4.09 us (36%)
  waiting for transfers between devices  0.77 us (7%)
    ppermute x5, starting transfers between devices, body(): lax.ppermute(x, ('row', 'col'), swap_pairs(mesh, axis, inner))  6.36 us
    pallas_call x1, Pallas kernels, body(): pl.pallas_call(functools.partial(end_kernel, cols), out_shape=whole, in_s...  0.93 us
    pallas_call x1, Pallas kernels, body(): pl.pallas_call(raw_kernel, out_shape=here(6, HALO, nx, nz), in_specs=[pl....  0.9 us
    ppermute x5, waiting for transfers between devices, body(): lax.ppermute(x, ('row', 'col'), swap_pairs(mesh, axis, inner))  0.77 us
    pallas_call x2, Pallas kernels, third(): pl.pallas_call(functools.partial(third_kernel, first, count), out_shape=h...  0.54 us
    pallas_call x1, Pallas kernels, body(): pl.pallas_call(second_far, out_shape=far_shape, in_specs=[near] * 5, out_...  0.3 us
    pallas_call x1, Pallas kernels, body(): pl.pallas_call(functools.partial(second_near, rows), out_shape=(here(5, S...  0.29 us
    pallas_call x1, Pallas kernels, body(): pl.pallas_call(functools.partial(window_kernel, cols), out_shape=here(EDG...  0.23 us
  transfers between devices with their start and end apart: 5, of which 2 were waited for; matrix products, arithmetic and copies ran while one was open for 0% of the time, Pallas kernels for 28%

profile of v13, /device:TPU:0, one launch (start us, length us, event | category | flops | bytes accessed | tf_op | source)
XLA Modules:
  0.0 11.3 jit_solution(3576182685662303972)
XLA Ops:
  0.0 0.0 copy-start
  0.0 0.0 copy-start.1
  0.0 0.9 %raw_edges.1 = f32[6,3,8,128]{3,2,1,0:T(8,128)S(1)} custom-call(f32[5,8,8,128]{3,2,1,0:T(8,128)} %state_hbm.1, f32[8,8,128]{2,1,0:T(8,128)} %gamma_hbm.1), custom_call_target="tpu_custom_call" | custom-call | tf_op jit(solution)/shard_map/raw_edges/pallas_call | solution.py:687
  0.9 0.5 %collective-permute-start = (f32[6,3,8,128]{3,2,1,0:T(8,128)S(1)}, f32[6,3,8,128]{3,2,1,0:T(8,128)S(1)}, u32[]{:S(2)}, u32[]{:S(2)}) collective-permute-start(f32[6,3,8,128]{3,2,1,0:T(8,128)S(1)} %raw_edges.1), channel_id=1, source_target_pairs={{0,1},{1,0},{2,3},{3,2},{4,8},{5,9},{6,10},{7,11},{8,4},{9,5},{10,... | collective-permute-start | bytes 221192 | tf_op jit(solution)/shard_map/ppermute | solution.py:685
  1.4 0.0 copy-done
  1.4 0.0 copy-done.1
  1.4 0.2 %edge_rows.1 = (f32[16,8,128]{2,1,0:T(8,128)S(1)}, f32[16,128]{1,0:T(8,128)S(1)}) custom-call(f32[5,64,128]{2,1,0:T(8,128)S(1)} %bitcast.4, f32[64,128]{1,0:T(8,128)S(1)} %bitcast.6), custom_call_target="tpu_custom_call" | custom-call | tf_op jit(solution)/shard_map/edge_rows/pallas_call | solution.py:697
  1.6 4.1 %collective-permute-start.2 = (f32[16,128]{1,0:T(8,128)S(1)}, f32[16,128]{1,0:T(8,128)S(1)}, u32[]{:S(2)}, u32[]{:S(2)}) collective-permute-start(f32[16,128]{1,0:T(8,128)S(1)} %get-tuple-element.25), channel_id=1, source_target_pairs={{0,4},{1,5},{2,6},{3,7},{4,0},{5,1},{6,2},{7,3},{8,12},{9,13},{10,... | collective-permute-start | bytes 24584 | tf_op jit(solution)/shard_map/ppermute | solution.py:685
  5.7 0.1 collective-permute-start.1
  5.8 0.2 %sweep_first.1.swept_ref.gamma_ref = f32[6,64,128]{2,1,0:T(8,128)S(1)} custom-call(f32[5,64,128]{2,1,0:T(8,128)S(1)} %bitcast.5, f32[64,128]{1,0:T(8,128)S(1)} %bitcast.7), custom_call_target="tpu_custom_call" | custom-call | tf_op jit(solution)/shard_map/sweep_first/pallas_call | solution.py:704
  6.0 0.2 %second_inner.1 = (f32[5,16,128]{2,1,0:T(8,128)S(1)}, f32[8,128]{1,0:T(8,128)S(1)}, f32[8,128]{1,0:T(8,128)S(1)}, f32[41,8,128]{2,1,0:T(8,128)S(1)}, f32[36,8,128]{2,1,0:T(8,128)S(1)}) custom-call(f32[6,64,128]{2,1,0:T(8,128)S(1)} %sweep_first.1.swept_ref.gamma_ref), custom_call_target="tpu_custom_call" | custom-call | tf_op jit(solution)/shard_map/second_inner/pallas_call | solution.py:713
  6.2 0.3 %third_inner.1.ahead_ref.inner_ref = f32[5,16,128]{2,1,0:T(8,128)S(1)} custom-call(f32[5,16,128]{2,1,0:T(8,128)S(1)} %get-tuple-element.18.rows_ref.inner_ref, f32[6,64,128]{2,1,0:T(8,128)S(1)} %sweep_first.1.swept_ref.gamma_ref), custom_call_target="tpu_custom_call" | custom-call | tf_op jit(solution)/shard_map/third_inner/pallas_call | solution.py:728
  6.5 0.0 collective-permute-done
  6.5 0.3 %second_near.1 = (f32[5,40,128]{2,1,0:T(8,128)S(1)}, f32[8,128]{1,0:T(8,128)S(1)}, f32[8,128]{1,0:T(8,128)S(1)}) custom-call(f32[6,64,128]{2,1,0:T(8,128)S(1)} %sweep_first.1.swept_ref.gamma_ref, f32[18,8,128]{2,1,0:T(8,128)S(1)} %bitcast.8, f32[5,16,128]{2,1,0:T(8,128)S(1)} %get-tuple-element.18.rows_ref.inner_ref, ...), custom_call_target="tpu_custom_call" | custom-call | tf_op jit(solution)/shard_map/second_near/pallas_call | solution.py:737
  6.8 0.6 %collective-permute-done.2.rim_ref = f32[16,128]{1,0:T(8,128)S(1)} collective-permute-done((f32[16,128]{1,0:T(8,128)S(1)}, f32[16,128]{1,0:T(8,128)S(1)}, u32[]{:S(2)}, u32[]{:S(2)}) %collective-permute-start.2) | collective-permute-done | bytes 8224 | tf_op jit(solution)/shard_map/ppermute | solution.py:685
  7.4 0.2 %second_rim.1 = (f32[5,24,128]{2,1,0:T(8,128)S(1)}, f32[8,128]{1,0:T(8,128)S(1)}, f32[16,128]{1,0:T(8,128)S(1)}) custom-call(f32[6,64,128]{2,1,0:T(8,128)S(1)} %sweep_first.1.swept_ref.gamma_ref, f32[16,128]{1,0:T(8,128)S(1)} %collective-permute-done.2.rim_ref, f32[8,128]{1,0:T(8,128)S(1)} %get-tuple-element.26.lower_ref, ...), custom_call_target="tpu_custom_call" | custom-call | flops 1000000000 | tf_op jit(solution)/shard_map/second_rim/pallas_call | solution.py:753
  7.6 0.1 collective-permute-start.4
  7.7 1.6 %collective-permute-start.3 = (f32[8,128]{1,0:T(8,128)S(1)}, f32[8,128]{1,0:T(8,128)S(1)}, u32[]{:S(2)}, u32[]{:S(2)}) collective-permute-start(f32[8,128]{1,0:T(8,128)S(1)} %get-tuple-element.29), channel_id=1, source_target_pairs={{0,1},{1,0},{2,3},{3,2},{4,5},{5,4},{6,7},{7,6},{8,9},{9,8},{10,11... | collective-permute-start | bytes 12296 | tf_op jit(solution)/shard_map/ppermute | solution.py:685
  9.3 0.3 %third_near.1.others_0_.near_ref = f32[5,24,128]{2,1,0:T(8,128)S(1)} custom-call(f32[5,40,128]{2,1,0:T(8,128)S(1)} %get-tuple-element.22.rows_ref.near_ref, f32[6,64,128]{2,1,0:T(8,128)S(1)} %sweep_first.1.swept_ref.gamma_ref), custom_call_target="tpu_custom_call" | custom-call | tf_op jit(solution)/shard_map/third_near/pallas_call | solution.py:728
  9.5 0.2 %third_windows.1.others_1_.edge_ref = f32[43,8,128]{2,1,0:T(8,128)S(1)} custom-call(f32[5,40,128]{2,1,0:T(8,128)S(1)} %get-tuple-element.22.rows_ref.near_ref, f32[5,24,128]{2,1,0:T(8,128)S(1)} %get-tuple-element.28.far_ref, f32[6,64,128]{2,1,0:T(8,128)S(1)} %sweep_first.1.swept_ref.gamma_ref), custom_call_target="tpu_custom_call" | custom-call | tf_op jit(solution)/shard_map/third_windows/pallas_call | solution.py:764
  9.8 0.2 %collective-permute-done.1.one_ref = f32[16,8,128]{2,1,0:T(8,128)S(1)} collective-permute-done((f32[16,8,128]{2,1,0:T(8,128)S(1)}, f32[16,8,128]{2,1,0:T(8,128)S(1)}, u32[]{:S(2)}, u32[]{:S(2)}) %collective-permute-start.1) | collective-permute-done | bytes 65568 | tf_op jit(solution)/shard_map/ppermute | solution.py:685
  10.0 0.3 %second_far.1.far_ref = f32[5,24,128]{2,1,0:T(8,128)S(1)} custom-call(f32[6,64,128]{2,1,0:T(8,128)S(1)} %sweep_first.1.swept_ref.gamma_ref, f32[16,8,128]{2,1,0:T(8,128)S(1)} %collective-permute-done.1.one_ref, f32[36,8,128]{2,1,0:T(8,128)S(1)} %get-tuple-element.24.kept_ref, f32[5,24,128]{2,1,0:T(8,128)S(1)} %third_near.1.others_0_.near_ref, ...), custom_call_target="tpu_custom_call" | custom-call | tf_op jit(solution)/shard_map/second_far/pallas_call | solution.py:771
  10.3 0.0 collective-permute-done.3.one_ref
  10.3 0.9 %third_ends.1.ends_ref = f32[5,64,128]{2,1,0:T(8,128)} custom-call(f32[5,24,128]{2,1,0:T(8,128)S(1)} %third_near.1.others_0_.near_ref, f32[5,16,128]{2,1,0:T(8,128)S(1)} %third_inner.1.ahead_ref.inner_ref, f32[5,24,128]{2,1,0:T(8,128)S(1)} %second_far.1.far_ref, f32[43,8,128]{2,1,0:T(8,128)S(1)} %third_windows.1.others_1_.edge_ref, ...), custom_call_target="tpu_custom_call" | custom-call | tf_op jit(solution)/shard_map/third_ends/pallas_call | solution.py:782
  11.3 0.0 collective-permute-done.4.two_ref
  11.3 0.1 third_middle.1
Async XLA Ops:
  0.0 1.4 %copy-start = (f32[5,8,8,128]{3,2,1,0:T(8,128)S(1)}, f32[5,8,8,128]{3,2,1,0:T(8,128)}, u32[]{:S(2)}) copy-start(f32[5,8,8,128]{3,2,1,0:T(8,128)} %state_hbm.1) | copy-start | bytes 491524
  0.0 1.4 %copy-start.1 = (f32[8,8,128]{2,1,0:T(8,128)S(1)}, f32[8,8,128]{2,1,0:T(8,128)}, u32[]{:S(2)}) copy-start(f32[8,8,128]{2,1,0:T(8,128)} %gamma_hbm.1) | copy-start | bytes 98308
  0.9 5.6 %collective-permute-start = (f32[6,3,8,128]{3,2,1,0:T(8,128)S(1)}, f32[6,3,8,128]{3,2,1,0:T(8,128)S(1)}, u32[]{:S(2)}, u32[]{:S(2)}) collective-permute-start(f32[6,3,8,128]{3,2,1,0:T(8,128)S(1)} %raw_edges.1), channel_id=1, source_target_pairs={{0,1},{1,0},{2,3},{3,2},{4,8},{5,9},{6,10},{7,11},{8,4},{9,5},{10,... | collective-permute-start | bytes 221192 | tf_op jit(solution)/shard_map/ppermute | solution.py:685
  1.6 5.7 %collective-permute-start.2 = (f32[16,128]{1,0:T(8,128)S(1)}, f32[16,128]{1,0:T(8,128)S(1)}, u32[]{:S(2)}, u32[]{:S(2)}) collective-permute-start(f32[16,128]{1,0:T(8,128)S(1)} %get-tuple-element.25), channel_id=1, source_target_pairs={{0,4},{1,5},{2,6},{3,7},{4,0},{5,1},{6,2},{7,3},{8,12},{9,13},{10,... | collective-permute-start | bytes 24584 | tf_op jit(solution)/shard_map/ppermute | solution.py:685
  5.7 4.3 %collective-permute-start.1 = (f32[16,8,128]{2,1,0:T(8,128)S(1)}, f32[16,8,128]{2,1,0:T(8,128)S(1)}, u32[]{:S(2)}, u32[]{:S(2)}) collective-permute-start(f32[16,8,128]{2,1,0:T(8,128)S(1)} %get-tuple-element.23), channel_id=1, source_target_pairs={{0,4},{1,5},{2,6},{3,7},{4,0},{5,1},{6,2},{7,3},{8,12},{9,13},{10,... | collective-permute-start | bytes 196616 | tf_op jit(solution)/shard_map/ppermute | solution.py:685
  7.6 3.7 %collective-permute-start.4 = (f32[16,128]{1,0:T(8,128)S(1)}, f32[16,128]{1,0:T(8,128)S(1)}, u32[]{:S(2)}, u32[]{:S(2)}) collective-permute-start(f32[16,128]{1,0:T(8,128)S(1)} %get-tuple-element.30), channel_id=1, source_target_pairs={{0,3},{1,2},{2,1},{3,0},{4,7},{5,6},{6,5},{7,4},{8,11},{9,10},{10,... | collective-permute-start | bytes 24584 | tf_op jit(solution)/shard_map/ppermute | solution.py:685
  7.7 2.6 %collective-permute-start.3 = (f32[8,128]{1,0:T(8,128)S(1)}, f32[8,128]{1,0:T(8,128)S(1)}, u32[]{:S(2)}, u32[]{:S(2)}) collective-permute-start(f32[8,128]{1,0:T(8,128)S(1)} %get-tuple-element.29), channel_id=1, source_target_pairs={{0,1},{1,0},{2,3},{3,2},{4,5},{5,4},{6,7},{7,6},{8,9},{9,8},{10,11... | collective-permute-start | bytes 12296 | tf_op jit(solution)/shard_map/ppermute | solution.py:685
